TPU v7x, 128 devices: a whole 4x4x4 slice. The times are simulated.
128 devices in a mesh: db: 16 (over z, y_lo, core), mp: 8 (over x, y_hi).
Axes of the slice: x: 4, y: 4 (y_hi: 2, y_lo: 2; y = y_hi * 2 + y_lo), z: 4, core: 2. Of those that a mesh axis runs over, the one named last changes fastest.
Arguments:
- queries: bfloat16 [4096, 4096], P('db', 'mp'), may hold values from -80 to 80
- database: bfloat16 [256, 128, 8192], P('db', None, 'mp'), may hold values from -6 to 6
- neighbor_owner: int32 [64, 2], P('db'), may hold values from 0 to 15, all different within a row; in each aligned block of 4 rows (0 to 3, 4 to 7, ...) at most 2 rows name the same one
- neighbor_slot: int32 [64, 2], P('db'), may hold values from 0 to 15
- key_weight: bfloat16 [8192, 4096], P(None, 'mp'), may hold values from -0.0625 to 0.0625
- value_weight: bfloat16 [8192, 4096], P(None, 'mp'), may hold values from -0.0625 to 0.0625
- cotangent: bfloat16 [4096, 4096], P('db', 'mp'), may hold values from -8 to 8
Outputs:
- attended: bfloat16 [4096, 4096], P('db', 'mp')
- query_grad: bfloat16 [4096, 4096], P('db', 'mp')
- value_weight_grad: float32 [8192, 4096], P('db', 'mp')
Inputs may be any that keep to these rules, and one draw needn't show every extreme that they name: `neighbor_owner`: the 2 owners of one query span differ. Among the 4 query spans of one index of db, no owner is named more than 2 times, and in some such block one owner is named exactly 2 times.
All inputs are finite; a program needn't handle non-finite values.
Results may differ from a plain program's by a relative error of at most 0.023.
The roundings to bfloat16 on the way count: a program that leaves them out, or rounds other values in their place, can miss the bound.
Values may be sent and summed in bfloat16 or wider, within the bound.
No kernel may reach another device: no remote copies, remote signals or barrier semaphores. Data moves between devices by JAX's collectives and lax.ppermute only.
A program may use at most 128 MiB of HBM per device.

v0:
```python
import jax
import jax.numpy as jnp
from jax import lax
from jax.sharding import PartitionSpec as P

HEAD_DIM = 128
SPAN_LEN = 64
CAPACITY = 2


def weight_term(encoded_rows, gradient_rows):
    return lax.dot_general(
        encoded_rows, gradient_rows, (((0,), (0,)), ((), ())), preferred_element_type=jnp.float32
    )


def per_device(
    queries, database, neighbor_owner, neighbor_slot, key_weight, value_weight, cotangent
):
    owners = lax.axis_size("db")
    spans = neighbor_owner.shape[0]
    request_count = neighbor_owner.shape[0] * neighbor_owner.shape[1]
    neighbor_len = database.shape[1]
    feature_width = database.shape[2]
    local_width = key_weight.shape[1]
    heads_here = local_width // HEAD_DIM
    score_scale = HEAD_DIM ** (-0.5)
    flat_owner = neighbor_owner.reshape(request_count)
    flat_slot = neighbor_slot.reshape(request_count)
    positions = jnp.arange(request_count)
    earlier = positions[:, None] > positions[None, :]
    slot_rank = jnp.sum((flat_owner[:, None] == flat_owner[None, :]) & earlier, axis=1)
    capacity_rows = jnp.arange(CAPACITY)
    matches = (jnp.arange(owners)[:, None, None] == flat_owner[None, None, :]) & (
        capacity_rows[None, :, None] == slot_rank[None, None, :]
    )
    wanted = jnp.sum(jnp.where(matches, flat_slot[None, None, :] + 1, 0), axis=2)
    asked_slots = lax.all_to_all(wanted, "db", split_axis=0, concat_axis=0, tiled=True)
    chosen = jnp.maximum(asked_slots - 1, 0).reshape(owners * CAPACITY)
    packed = jnp.take(database, chosen, axis=0).reshape(
        owners, CAPACITY, neighbor_len, feature_width
    )
    arrived = lax.all_to_all(packed, "db", split_axis=0, concat_axis=0, tiled=True)
    fetched = jnp.take(
        arrived.reshape(owners * CAPACITY, neighbor_len, feature_width),
        flat_owner * CAPACITY + slot_rank,
        axis=0,
    )
    gathered = lax.all_gather(fetched, "mp", axis=2, tiled=True)
    model_width = gathered.shape[2]
    encoded_rows = gathered.reshape(request_count * neighbor_len, model_width)
    key_rows = jnp.dot(encoded_rows, key_weight, preferred_element_type=jnp.float32).astype(
        jnp.bfloat16
    )
    value_rows = jnp.dot(encoded_rows, value_weight, preferred_element_type=jnp.float32).astype(
        jnp.bfloat16
    )
    query_blocks = queries.reshape(spans, SPAN_LEN, heads_here, HEAD_DIM)
    grad_blocks = cotangent.reshape(spans, SPAN_LEN, heads_here, HEAD_DIM)
    key_blocks = key_rows.reshape(spans, -1, heads_here, HEAD_DIM)
    value_blocks = value_rows.reshape(spans, -1, heads_here, HEAD_DIM)
    scores = (
        jnp.einsum("cqhd,ckhd->chqk", query_blocks, key_blocks, preferred_element_type=jnp.float32)
        * score_scale
    )
    highest = jnp.max(scores, axis=-1, keepdims=True)
    raised = jnp.exp(scores - highest)
    probabilities = raised / jnp.sum(raised, axis=-1, keepdims=True)
    weights = probabilities.astype(jnp.bfloat16)
    attended = jnp.einsum(
        "chqk,ckhd->cqhd", weights, value_blocks, preferred_element_type=jnp.float32
    ).astype(jnp.bfloat16)
    value_grad = jnp.einsum(
        "chqk,cqhd->ckhd", weights, grad_blocks, preferred_element_type=jnp.float32
    ).astype(jnp.bfloat16)
    value_grad = value_grad.reshape(-1, local_width)
    prob_grad = jnp.einsum(
        "cqhd,ckhd->chqk", grad_blocks, value_blocks, preferred_element_type=jnp.float32
    )
    centre = jnp.sum(probabilities * prob_grad, axis=-1, keepdims=True)
    score_grad = (probabilities * (prob_grad - centre)).astype(jnp.bfloat16)
    query_grad = (
        jnp.einsum("chqk,ckhd->cqhd", score_grad, key_blocks, preferred_element_type=jnp.float32)
        * score_scale
    ).astype(jnp.bfloat16)
    value_weight_grad = lax.psum_scatter(
        weight_term(encoded_rows, value_grad).astype(jnp.bfloat16),
        "db",
        scatter_dimension=0,
        tiled=True,
    ).astype(jnp.float32)
    return (
        attended.reshape(-1, local_width),
        query_grad.reshape(-1, local_width),
        value_weight_grad,
    )


def solution(mesh):
    return jax.shard_map(
        per_device,
        mesh=mesh,
        in_specs=(
            P("db", "mp"),
            P("db", None, "mp"),
            P("db", None),
            P("db", None),
            P(None, "mp"),
            P(None, "mp"),
            P("db", "mp"),
        ),
        out_specs=(P("db", "mp"), P("db", "mp"), P("db", "mp")),
        check_vma=False,
    )
```

profile of v0, /device:TPU:6, one launch (start us, length us, event | category | flops | bytes accessed | tf_op | source)
XLA Modules:
  0.0 474.2 jit_solution(2178217840004651248)
XLA Ops:
  7.2 0.8 copy.69
  8.0 0.2 convert_reduce_fusion
  8.3 0.7 broadcast_add_fusion
  9.0 0.1 copy.70
  9.3 12.3 %all_to_all.14 = s32[16,1,2]{2,1,0:T(1,128)S(1)} all-to-all(s32[16,1,2]{2,1,0:T(1,128)S(1)} %copy.71), channel_id=1, replica_groups=mesh['db'=16,'mp'=8] {'db'}, dimensions={0} | all-to-all | bytes 256 | tf_op jit(solution)/shard_map/all_to_all | solution.py:38
  21.7 0.1 copy.73
  22.0 7.0 %gather_fusion = bf16[32,128,1024]{2,1,0:T(8,128)(2,1)} fusion(bf16[16,128,1024]{2,1,0:T(8,128)(2,1)} %param.8, s32[1024]{0:T(1024)S(1)} %pad_clamp_fusion.1), kind=kCustom, calls=%fused_computation | custom fusion | bytes 16777344 | tf_op jit(solution)/shard_map/jit(_take)/gather | solution.py:40
  29.0 7.5 %broadcast_select_fusion = bf16[16,2,128,1024]{3,2,1,0:T(8,128)(2,1)} fusion(bf16[16,2,128,1024]{3,2,1,0:T(8,128)(2,1)} %bitcast.46, pred[16,2]{1,0:T(8,128)(4,1)S(1)} %copy.73), kind=kLoop, calls=%fused_computation.4 | loop fusion | flops 4194304 | bytes 16777248 | tf_op jit(solution)/shard_map/jit(_take)/select_n | solution.py:40
  36.4 4.9 %all-to-all-start.1 = ((bf16[16,2,128,1024]{3,2,1,0:T(8,128)(2,1)}), bf16[16,2,128,1024]{3,2,1,0:T(8,128)(2,1)}, u32[]{:S(2)}, u32[]{:S(2)}) async-start(bf16[16,2,128,1024]{3,2,1,0:T(8,128)(2,1)} %broadcast_select_fusion), calls=%async_computation.1 | async-start | bytes 16777216 | tf_op jit(solution)/shard_map/all_to_all | solution.py:43
  41.5 0.1 copy.75
  41.7 95.0 %all-to-all-done.1 = bf16[16,2,128,1024]{3,2,1,0:T(8,128)(2,1)} async-done(((bf16[16,2,128,1024]{3,2,1,0:T(8,128)(2,1)}), bf16[16,2,128,1024]{3,2,1,0:T(8,128)(2,1)}, u32[]{:S(2)}, u32[]{:S(2)}) %all-to-all-start.1) | async-done | bytes 8388640 | tf_op jit(solution)/shard_map/all_to_all | solution.py:43
  136.7 4.1 gather_fusion.1
  140.8 1.6 broadcast_select_fusion.1
  142.4 0.2 reduce-scatter.2.cloned.1.call-start
  142.8 183.3 %all-gather.2.cloned.1.call-done = bf16[8,128,8192]{2,1,0:T(8,128)(2,1)} async-done(((bf16[8,128,1024]{2,1,0:T(8,128)(2,1)}), bf16[8,128,8192]{2,1,0:T(8,128)(2,1)}) %all-gather.2.cloned.1.call-update) | async-done | bytes 16777232 | tf_op jit(solution)/shard_map/all_gather | solution.py:49
  326.1 14.8 %convolution_convert_fusion.1 = bf16[1024,512]{1,0:T(8,128)(2,1)S(1)} fusion(bf16[1024,8192]{1,0:T(8,128)(2,1)} %bitcast.51, bf16[8192,512]{1,0:T(8,128)(2,1)} %param.11), kind=kOutput, calls=%fused_computation.6 | convolution fusion | flops 8590458880 | bytes 26214400 | tf_op jit(solution)/shard_map/dot_general | solution.py:52
  340.8 0.3 reshape.175
  341.1 0.5 fusion.4
  341.6 2.8 fusion.22
  344.5 3.2 fusion.2
  347.7 2.0 copy.85
  349.7 17.5 %convolution_convert_fusion = bf16[8192,512]{1,0:T(8,128)(2,1)} fusion(bf16[1024,8192]{1,0:T(8,128)(2,1)} %bitcast.52, bf16[128,8,4,128]{3,2,1,0:T(4,128)(2,1)S(1)} %bitcast.47), kind=kOutput, calls=%fused_computation.3 | convolution fusion | flops 8594128896 | bytes 26214400 | tf_op jit(solution)/shard_map/dot_general | solution.py:12
  367.3 15.8 %convolution_convert_fusion.2 = bf16[1024,512]{1,0:T(8,128)(2,1)} fusion(bf16[1024,8192]{1,0:T(8,128)(2,1)} %bitcast.53, bf16[8192,512]{1,0:T(8,128)(2,1)} %param.12), kind=kOutput, calls=%fused_computation.7 | convolution fusion | flops 8590458880 | bytes 26214400 | tf_op jit(solution)/shard_map/dot_general | solution.py:55
  383.0 2.2 reshape.174
  385.2 3.8 fusion.6
  389.0 1.2 copy.79
  390.2 2.8 multiply_reduce_fusion
  392.9 3.3 fusion.7
  396.2 0.2 copy.83
  396.4 0.9 copy_bitcast_fusion
  397.3 67.9 %reduce-scatter.2.cloned.1.call-done = bf16[512,512]{1,0:T(8,128)(2,1)} async-done(((bf16[8192,512]{1,0:T(8,128)(2,1)}), bf16[512,512]{1,0:T(8,128)(2,1)}) %reduce-scatter.2.cloned.1.call-update) | async-done | bytes 524304 | tf_op jit(solution)/shard_map/reduce_scatter | solution.py:86
  465.2 2.1 convert_element_type.51
  (30 shorter events, 1.0 us)
Async XLA Ops:
  36.4 5.0 %copy-start.3 = (s32[4,2]{0,1:T(2,128)S(1)}, s32[4,2]{0,1:T(2,128)}, u32[]{:S(2)}) copy-start(s32[4,2]{0,1:T(2,128)} %param.9) | copy-start | bytes 100
  36.4 100.2 %all-to-all-start.1 = ((bf16[16,2,128,1024]{3,2,1,0:T(8,128)(2,1)}), bf16[16,2,128,1024]{3,2,1,0:T(8,128)(2,1)}, u32[]{:S(2)}, u32[]{:S(2)}) async-start(bf16[16,2,128,1024]{3,2,1,0:T(8,128)(2,1)} %broadcast_select_fusion), calls=%async_computation.1 | async-start | bytes 16777216 | tf_op jit(solution)/shard_map/all_to_all | solution.py:43
  41.4 101.2 %copy-start = (bf16[256,512]{1,0:T(8,128)(2,1)S(1)}, bf16[256,512]{1,0:T(8,128)(2,1)}, u32[]{:S(2)}) copy-start(bf16[256,512]{1,0:T(8,128)(2,1)} %param.13) | copy-start | bytes 786436
  41.4 101.3 %copy-start.1 = (bf16[256,512]{1,0:T(8,128)(2,1)S(1)}, bf16[256,512]{1,0:T(8,128)(2,1)}, u32[]{:S(2)}) copy-start(bf16[256,512]{1,0:T(8,128)(2,1)} %param.7) | copy-start | bytes 786436
  41.4 284.7 %all-gather.2.cloned.1.call-start = ((), (), s32[]{:S(2)}) async-start(), calls=%async_computation.3 | async-start | bytes 18874368 | tf_op jit(solution)/shard_map/all_gather | solution.py:49
  142.4 322.8 %reduce-scatter.2.cloned.1.call-start = ((), (), s32[]{:S(2)}) async-start(), calls=%async_computation.4 | async-start | bytes 8912896 | tf_op jit(solution)/shard_map/reduce_scatter | solution.py:86
  142.7 201.7 %copy-start.2 = (bf16[4,64,4,128]{3,2,1,0:T(4,128)(2,1)}, bf16[4,64,4,128]{3,2,1,0:T(4,128)(2,1)S(1)}, u32[]{:S(2)}) copy-start(bf16[4,64,4,128]{3,2,1,0:T(4,128)(2,1)S(1)} %reshape.178) | copy-start | bytes 786436
Sparse Core Ops, SparseCore 0:
  142.5 183.5 all-gather.1
  367.4 97.7 reduce-scatter.1
where the time goes:
time: 475 us; the launch traced here: 474 us
  waiting for transfers between devices  346 us (73%)
  matrix products  61.6 us (13%)
  local copies, waits for them, and re-layouts  19.6 us (4%)
  other arithmetic  15.1 us (3%)
  between operations  14.2 us (3%)
  blocking collectives  12.3 us (3%)
  starting transfers between devices  5.19 us (1%)
    all_gather x1, waiting for transfers between devices, per_device(): gathered = lax.all_gather(fetched, 'mp', axis=2, tiled=True)  183 us
    all_to_all x1, waiting for transfers between devices, per_device(): lax.all_to_all(packed, 'db', split_axis=0, concat_axis=0, tiled=True)  95 us
    reduce_scatter x1, waiting for transfers between devices, per_device(): lax.psum_scatter(weight_term(encoded_rows, value_grad).astype(jnp.bfloat1...  67.9 us
    dot_general x1, matrix products, weight_term(): lax.dot_general(encoded_rows, gradient_rows, (((0,), (0,)), ((), ())), pr...  17.5 us
    dot_general x1, matrix products, per_device(): jnp.dot(encoded_rows, value_weight, preferred_element_type=jnp.float32)  15.8 us
    dot_general x1, matrix products, per_device(): jnp.dot(encoded_rows, key_weight, preferred_element_type=jnp.float32)  14.8 us
    all_to_all x1, blocking collectives, per_device(): lax.all_to_all(wanted, 'db', split_axis=0, concat_axis=0, tiled=True)  12.3 us
  transfers between devices with their start and end apart: 3, of which 3 were waited for; matrix products, arithmetic and copies ran while one was open for 6% of the time, Pallas kernels for 0%

commit v1 on v0

v1 whole, which is shorter than its diff:
```python
import functools

import jax
import jax.numpy as jnp
from jax import lax
from jax.experimental import pallas as pl
from jax.experimental.pallas import tpu as pltpu
from jax.sharding import Mesh
from jax.sharding import PartitionSpec as P

HEAD_DIM = 128
SPAN_LEN = 64
CHUNKS = (32, 32, 32, 32)
DB = ("z", "ylo", "core")
MP = ("x", "yhi")
VMEM_LIMIT = 40 * 1024 * 1024
TARGETS = ((2, 1), (2, 0), (1, 1), (3, 1), (1, 0), (3, 0), (0, 1), (0, 0))


def ring(values, axis, shift, size):
    return lax.ppermute(values, axis, [(i, (i + shift) % size) for i in range(size)])


def pack_kernel(first, rows, place, wanted, own, beside, across, corner, packet, sems):
    z, ylo, core = place[0], place[1], place[2]
    count = packet.shape[0]
    pools = (own, beside, across, corner)
    cuts = (first, 0, first, 0)

    def each(act):
        for i in range(count):
            owner = wanted[0, i]
            slot = wanted[0, count + i]
            here = owner // 4 == z
            which = (owner // 2 % 2 + ylo) % 2 + 2 * ((owner % 2 + core) % 2)
            for n, (pool, cut) in enumerate(zip(pools, cuts)):
                @pl.when(here & (which == n))
                def _():
                    act(
                        pltpu.make_async_copy(
                            pool.at[slot, pl.ds(cut, rows)], packet.at[i], sems.at[i]
                        )
                    )

    each(lambda copy: copy.start())
    each(lambda copy: copy.wait())


def merge_kernel(first, rows, place, wanted, own, beside, across, corner, one, two, three, merged, sems):
    z, ylo, core = place[0], place[1], place[2]
    count = merged.shape[0]
    pools = (own, beside, across, corner)
    cuts = (first, 0, first, 0)

    def each(act):
        for i in range(count):
            owner = wanted[0, i]
            slot = wanted[0, count + i]
            away = (owner // 4 + 4 - z) % 4
            which = (owner // 2 % 2 + ylo) % 2 + 2 * ((owner % 2 + core) % 2)
            for n, (pool, cut) in enumerate(zip(pools, cuts)):
                @pl.when((away == 0) & (which == n))
                def _():
                    act(
                        pltpu.make_async_copy(
                            pool.at[slot, pl.ds(cut, rows)], merged.at[i], sems.at[i]
                        )
                    )
            for n, packet in enumerate((one, two, three)):
                @pl.when(away == n + 1)
                def _():
                    act(pltpu.make_async_copy(packet.at[i], merged.at[i], sems.at[i]))

    each(lambda copy: copy.start())
    each(lambda copy: copy.wait())


def copies_call(kernel, name, count, rows, width, place, wanted, arrays):
    return pl.pallas_call(
        kernel,
        name=name,
        out_shape=jax.ShapeDtypeStruct((count, rows, width), jnp.bfloat16),
        grid_spec=pltpu.PrefetchScalarGridSpec(
            num_scalar_prefetch=2,
            grid=(1,),
            in_specs=[pl.BlockSpec(memory_space=pl.ANY)] * len(arrays),
            out_specs=pl.BlockSpec(memory_space=pl.ANY),
            scratch_shapes=[pltpu.SemaphoreType.DMA((count,))],
        ),
        cost_estimate=pl.CostEstimate(
            flops=0, bytes_accessed=2 * count * rows * width * 2, transcendentals=0
        ),
    )(place, wanted, *arrays)


def project_kernel(
    place, own, left, right, far0, far1, key_weight, value_weight, keys, values, encoded, key_sum, value_sum
):
    step = pl.program_id(0)

    @pl.when(step == 0)
    def _():
        key_sum[...] = jnp.zeros_like(key_sum)
        value_sum[...] = jnp.zeros_like(value_sum)

    def add(piece):
        rows = piece[0]
        encoded[0] = rows
        key_sum[...] += jnp.dot(rows, key_weight[...], preferred_element_type=jnp.float32)
        value_sum[...] += jnp.dot(rows, value_weight[...], preferred_element_type=jnp.float32)

    for piece, (low, high) in (
        (own, (0, 2)), (left, (2, 4)), (right, (4, 6)), (far0, (6, 7)), (far1, (7, 8))
    ):
        pl.when((step >= low) & (step < high))(functools.partial(add, piece))

    @pl.when(step == 7)
    def _():
        keys[...] = key_sum[...].astype(keys.dtype)
        values[...] = value_sum[...].astype(values.dtype)


def project(place, pieces, key_weight, value_weight):
    own, left, right, far0, far1 = pieces
    rows, depth = own.shape[1], own.shape[2]
    width = key_weight.shape[1]

    def slice_of(step, place):
        hop = step // 2
        shift = jnp.where(hop == 0, 0, jnp.where(hop == 1, 3, jnp.where(hop == 2, 1, 2)))
        return (place[3] + shift) % 4 * 2 + step % 2

    def pair(low):
        return pl.BlockSpec(
            (1, rows, depth), lambda step, place: (jnp.clip(step - low, 0, 1), 0, 0)
        )

    single = pl.BlockSpec((1, rows, depth), lambda step, place: (0, 0, 0))
    weight = pl.BlockSpec((depth, width), lambda step, place: (slice_of(step, place), 0))
    whole = pl.BlockSpec((rows, width), lambda step, place: (0, 0))
    return pl.pallas_call(
        project_kernel,
        name="project",
        out_shape=(
            jax.ShapeDtypeStruct((rows, width), jnp.bfloat16),
            jax.ShapeDtypeStruct((rows, width), jnp.bfloat16),
            jax.ShapeDtypeStruct((8, rows, depth), jnp.bfloat16),
        ),
        grid_spec=pltpu.PrefetchScalarGridSpec(
            num_scalar_prefetch=1,
            grid=(8,),
            in_specs=[pair(0), pair(2), pair(4), single, single, weight, weight],
            out_specs=(
                whole,
                whole,
                pl.BlockSpec((1, rows, depth), lambda step, place: (slice_of(step, place), 0, 0)),
            ),
            scratch_shapes=[pltpu.VMEM((rows, width), jnp.float32)] * 2,
        ),
        compiler_params=pltpu.CompilerParams(vmem_limit_bytes=VMEM_LIMIT),
        cost_estimate=pl.CostEstimate(
            flops=4 * rows * 8 * depth * width,
            bytes_accessed=32 * depth * width + 32 * rows * depth,
            transcendentals=0,
        ),
    )(place, own, left, right, far0, far1, key_weight, value_weight)


def span_rows(parts, span, low, high):
    pieces = []
    for part in parts:
        size = part.shape[0] // 4
        pieces.append(part[span * size:(span + 1) * size, low:high])
    return jnp.concatenate(pieces, axis=0)


def weigh_kernel(chunks, *refs):
    queries, cotangent = refs[0], refs[1]
    key_parts = refs[2:2 + chunks]
    chances, gradient, stacked = refs[2 + chunks:]
    width = queries.shape[1]
    scale = HEAD_DIM ** (-0.5)
    for span in range(4):
        tokens = slice(span * SPAN_LEN, (span + 1) * SPAN_LEN)
        for head in range(width // HEAD_DIM):
            low, high = head * HEAD_DIM, (head + 1) * HEAD_DIM
            keys = span_rows(key_parts, span, low, high)
            scores = lax.dot_general(
                queries[tokens, low:high], keys, (((1,), (1,)), ((), ())),
                preferred_element_type=jnp.float32,
            ) * scale
            raised = jnp.exp(scores - jnp.max(scores, axis=-1, keepdims=True))
            found = raised / jnp.sum(raised, axis=-1, keepdims=True)
            chances[span * (width // HEAD_DIM) + head] = found
            part = lax.dot_general(
                found.astype(jnp.bfloat16), cotangent[tokens, low:high], (((0,), (0,)), ((), ())),
                preferred_element_type=jnp.float32,
            ).astype(jnp.bfloat16)
            base, start = 0, 0
            for key_part in key_parts:
                size = key_part.shape[0] // 4
                at = base + span * size
                stacked[at:at + size, low:high] = part[start:start + size]
                start += size
                base += key_part.shape[0]
    gradient[...] = stacked[...].T


def weigh(queries, cotangent, key_parts):
    tokens, width = queries.shape
    rows = sum(part.shape[0] for part in key_parts)
    heads = width // HEAD_DIM
    vmem = pl.BlockSpec(memory_space=pltpu.VMEM)
    return pl.pallas_call(
        functools.partial(weigh_kernel, len(key_parts)),
        name="weigh",
        out_shape=(
            jax.ShapeDtypeStruct((4 * heads, SPAN_LEN, rows // 4), jnp.float32),
            jax.ShapeDtypeStruct((width, rows), jnp.bfloat16),
        ),
        in_specs=[vmem] * (2 + len(key_parts)),
        out_specs=(vmem, vmem),
        scratch_shapes=[pltpu.VMEM((rows, width), jnp.bfloat16)],
        compiler_params=pltpu.CompilerParams(vmem_limit_bytes=VMEM_LIMIT),
        cost_estimate=pl.CostEstimate(
            flops=4 * tokens * (rows // 4) * width,
            bytes_accessed=8 * rows * width,
            transcendentals=tokens * rows,
        ),
    )(queries, cotangent, *key_parts)


def attend_kernel(chunks, *refs):
    cotangent, chances = refs[0], refs[1]
    key_parts = refs[2:2 + chunks]
    value_parts = refs[2 + chunks:2 + 2 * chunks]
    attended, query_grad = refs[2 + 2 * chunks:]
    width = cotangent.shape[1]
    scale = HEAD_DIM ** (-0.5)
    for span in range(4):
        tokens = slice(span * SPAN_LEN, (span + 1) * SPAN_LEN)
        for head in range(width // HEAD_DIM):
            low, high = head * HEAD_DIM, (head + 1) * HEAD_DIM
            keys = span_rows(key_parts, span, low, high)
            values = span_rows(value_parts, span, low, high)
            found = chances[span * (width // HEAD_DIM) + head]
            attended[tokens, low:high] = jnp.dot(
                found.astype(jnp.bfloat16), values, preferred_element_type=jnp.float32
            ).astype(jnp.bfloat16)
            slope = lax.dot_general(
                cotangent[tokens, low:high], values, (((1,), (1,)), ((), ())),
                preferred_element_type=jnp.float32,
            )
            centre = jnp.sum(found * slope, axis=-1, keepdims=True)
            score_grad = (found * (slope - centre)).astype(jnp.bfloat16)
            query_grad[tokens, low:high] = (
                jnp.dot(score_grad, keys, preferred_element_type=jnp.float32) * scale
            ).astype(jnp.bfloat16)


def attend(cotangent, chances, key_parts, value_parts):
    tokens, width = cotangent.shape
    rows = sum(part.shape[0] for part in key_parts)
    vmem = pl.BlockSpec(memory_space=pltpu.VMEM)
    return pl.pallas_call(
        functools.partial(attend_kernel, len(key_parts)),
        name="attend",
        out_shape=(
            jax.ShapeDtypeStruct((tokens, width), jnp.bfloat16),
            jax.ShapeDtypeStruct((tokens, width), jnp.bfloat16),
        ),
        in_specs=[vmem] * (2 + 2 * len(key_parts)),
        out_specs=(vmem, vmem),
        compiler_params=pltpu.CompilerParams(vmem_limit_bytes=VMEM_LIMIT),
        cost_estimate=pl.CostEstimate(
            flops=6 * tokens * (rows // 4) * width,
            bytes_accessed=8 * rows * width,
            transcendentals=0,
        ),
    )(cotangent, chances, *key_parts, *value_parts)


def term_kernel(chunks, adds, *refs):
    gradient = refs[1]
    encoded_parts = refs[2:2 + chunks]
    output = refs[-1]
    total, base = None, 0
    for encoded in encoded_parts:
        rows = encoded.shape[1]
        part = jnp.dot(
            gradient[:, base:base + rows], encoded[0], preferred_element_type=jnp.float32
        )
        total = part if total is None else total + part
        base += rows
    total = total.astype(jnp.bfloat16)
    if adds:
        total = (total.astype(jnp.float32) + refs[2 + chunks][0].astype(jnp.float32)).astype(
            jnp.bfloat16
        )
    output[0] = total


def weight_terms(blocks, gradient, encoded_parts, arrived=None, offset=0):
    count = blocks.shape[0] - 1
    width, rows = gradient.shape
    depth = encoded_parts[0].shape[2] // 2
    in_specs = [pl.BlockSpec((width, rows), lambda n, blocks: (0, 0))]
    for part in encoded_parts:
        in_specs.append(
            pl.BlockSpec(
                (1, part.shape[1], depth), lambda n, blocks: (blocks[n], 0, blocks[count])
            )
        )
    operands = [gradient, *encoded_parts]
    if arrived is not None:
        in_specs.append(pl.BlockSpec((1, width, depth), lambda n, blocks: (offset + n, 0, 0)))
        operands.append(arrived)
    return pl.pallas_call(
        functools.partial(term_kernel, len(encoded_parts), arrived is not None),
        name="terms",
        out_shape=jax.ShapeDtypeStruct((count, width, depth), jnp.bfloat16),
        grid_spec=pltpu.PrefetchScalarGridSpec(
            num_scalar_prefetch=1,
            grid=(count,),
            in_specs=in_specs,
            out_specs=pl.BlockSpec((1, width, depth), lambda n, blocks: (n, 0, 0)),
        ),
        compiler_params=pltpu.CompilerParams(vmem_limit_bytes=VMEM_LIMIT),
        cost_estimate=pl.CostEstimate(
            flops=2 * count * width * rows * depth,
            bytes_accessed=2 * rows * width + 2 * count * depth * (rows + 2 * width),
            transcendentals=0,
        ),
    )(blocks, *operands)


def total_kernel(*refs):
    output = refs[-1]
    total = refs[0][0].astype(jnp.float32)
    for block in refs[1:-1]:
        total += block[0].astype(jnp.float32)
    output[...] = total.T


def add_blocks(blocks):
    width, depth = blocks[0].shape[1:]
    vmem = pl.BlockSpec(memory_space=pltpu.VMEM)
    return pl.pallas_call(
        total_kernel,
        name="total",
        out_shape=jax.ShapeDtypeStruct((depth, width), jnp.float32),
        in_specs=[vmem] * len(blocks),
        out_specs=vmem,
        compiler_params=pltpu.CompilerParams(vmem_limit_bytes=VMEM_LIMIT),
        cost_estimate=pl.CostEstimate(
            flops=len(blocks) * width * depth,
            bytes_accessed=(2 * len(blocks) + 4) * width * depth,
            transcendentals=0,
        ),
    )(*blocks)


def per_device(
    queries, database, neighbor_owner, neighbor_slot, key_weight, value_weight, cotangent
):
    z, ylo, core = lax.axis_index("z"), lax.axis_index("ylo"), lax.axis_index("core")
    x, yhi = lax.axis_index("x"), lax.axis_index("yhi")
    place = jnp.stack([z, ylo, core, x, yhi]).astype(jnp.int32)
    count = neighbor_owner.shape[0] * neighbor_owner.shape[1]
    width = database.shape[2]
    wanted = jnp.concatenate(
        [neighbor_owner.reshape(1, count), neighbor_slot.reshape(1, count)], axis=1
    )
    asked = [wanted] + [ring(wanted, "z", -n, 4) for n in (1, 2, 3)]
    across = ring(database, "core", 1, 2)

    key_parts, value_parts, encoded_parts = [], [], []
    first = 0
    for rows in CHUNKS:
        beside = ring(database[:, first:first + rows], "ylo", 1, 2)
        corner = ring(beside, "core", 1, 2)
        pools = (database, beside, across, corner)
        packets = [
            ring(
                copies_call(
                    functools.partial(pack_kernel, first, rows), "pack", count, rows, width,
                    place, asked[n], pools,
                ),
                "z", n, 4,
            )
            for n in (1, 2, 3)
        ]
        own = copies_call(
            functools.partial(merge_kernel, first, rows), "merge", count, rows, width,
            place, wanted, (*pools, packets[2], packets[1], packets[0]),
        ).reshape(1, count * rows, width)
        other = ring(own, "yhi", 1, 2)
        pair = jnp.where(
            yhi == 0,
            jnp.concatenate([own, other], axis=0),
            jnp.concatenate([other, own], axis=0),
        )
        left = ring(pair, "x", 1, 4)
        right = ring(pair, "x", -1, 4)
        far0 = ring(left[0:1], "x", 1, 4)
        far1 = ring(right[1:2], "x", -1, 4)
        keys, values, encoded = project(
            place, (pair, left, right, far0, far1), key_weight, value_weight
        )
        key_parts.append(keys)
        value_parts.append(values)
        encoded_parts.append(encoded)
        first += rows

    chances, gradient = weigh(queries, cotangent, key_parts)

    order = [(z + dz) % 4 * 2 + (ylo + dy) % 2 for dz, dy in TARGETS]
    sent = []
    for low, high in ((0, 4), (4, 8)):
        blocks = jnp.stack([*order[low:high], 1 - core]).astype(jnp.int32)
        terms = weight_terms(blocks, gradient, encoded_parts)
        sent.append(ring(terms, "core", 1, 2))
    totals = []
    for n, (dz, dy) in enumerate(TARGETS):
        blocks = jnp.stack([order[n], core]).astype(jnp.int32)
        block = weight_terms(blocks, gradient, encoded_parts, sent[n // 4], n % 4)
        if (dz, dy) != (0, 0):
            block = lax.ppermute(
                block, ("z", "ylo"),
                [
                    (a * 2 + b, (a + dz) % 4 * 2 + (b + dy) % 2)
                    for a in range(4) for b in range(2)
                ],
            )
        totals.append(block)
    value_weight_grad = add_blocks(totals)
    attended, query_grad = attend(cotangent, chances, key_parts, value_parts)
    return attended, query_grad, value_weight_grad


def solution(mesh):
    inner = Mesh(mesh.devices.reshape(4, 2, 2, 4, 2), (*DB, *MP))
    return jax.shard_map(
        per_device,
        mesh=inner,
        in_specs=(
            P(DB, MP),
            P(DB, None, MP),
            P(DB, None),
            P(DB, None),
            P(None, MP),
            P(None, MP),
            P(DB, MP),
        ),
        out_specs=(P(DB, MP), P(DB, MP), P(DB, MP)),
        check_vma=False,
    )
```

time: 475 us -> 528 us (1.11)
  Pallas kernels: 0 us -> 209 us
  waiting for transfers between devices: 346 us -> 161 us
  starting transfers between devices: 5.19 us -> 118 us
  matrix products: 61.6 us -> 0 us
  between operations: 14.2 us -> 1.84 us
  blocking collectives: 12.3 us -> 0 us
  local copies, waits for them, and re-layouts: 19.6 us -> 31.5 us
  other arithmetic: 15.1 us -> 6.18 us
    pallas_call x0 -> x33, Pallas kernels: none -> 209 us  [the longest x16 126 us: copies_call(): pl.pallas_call(kernel, name=name, out_shape=jax.ShapeDtypeStruct((count,...]
    all_gather x1 -> x0, waiting for transfers between devices: 183 us -> none  [per_device(): gathered = lax.all_gather(fetched, 'mp', axis=2, tiled=True)]
    ppermute x0 -> x53, waiting for transfers between devices: none -> 161 us  [the longest x46 145 us: ring(): lax.ppermute(values, axis, [(i, (i + shift) % size) for i in range(size)])]
    ppermute x0 -> x53, starting transfers between devices: none -> 118 us  [the longest x46 95.5 us: ring(): lax.ppermute(values, axis, [(i, (i + shift) % size) for i in range(size)])]
    all_to_all x1 -> x0, waiting for transfers between devices: 95 us -> none  [per_device(): lax.all_to_all(packed, 'db', split_axis=0, concat_axis=0, tiled=True)]
    reduce_scatter x1 -> x0, waiting for transfers between devices: 67.9 us -> none  [per_device(): lax.psum_scatter(weight_term(encoded_rows, value_grad).astype(jnp.bfloat1...]
    dot_general x8 -> x0, matrix products: 61.6 us -> none  [the longest x1 17.5 us: weight_term(): lax.dot_general(encoded_rows, gradient_rows, (((0,), (0,)), ((), ())), pr...]
    slice x0 -> x9, local copies, waits for them, and re-layouts: none -> 14.9 us  [the longest x4 5.91 us: per_device(): far0 = ring(left[0:1], 'x', 1, 4)]
  transfers between devices with their start and end apart: 3 -> 53, of which waited for: 3 -> 17; matrix products, arithmetic and copies ran while one was open for 6% -> 4% of each run, Pallas kernels for 0% -> 36%
where the time goes in v1:
time: 528 us
  Pallas kernels  209 us (40%)
  waiting for transfers between devices  161 us (30%)
  starting transfers between devices  118 us (22%)
  local copies, waits for them, and re-layouts  31.5 us (6%)
  other arithmetic  6.18 us (1%)
    ppermute x46, waiting for transfers between devices, ring(): lax.ppermute(values, axis, [(i, (i + shift) % size) for i in range(size)])  145 us
    pallas_call x16, Pallas kernels, copies_call(): pl.pallas_call(kernel, name=name, out_shape=jax.ShapeDtypeStruct((count,...  126 us
    ppermute x46, starting transfers between devices, ring(): lax.ppermute(values, axis, [(i, (i + shift) % size) for i in range(size)])  95.5 us
    pallas_call x4, Pallas kernels, project(): pl.pallas_call(project_kernel, name='project', out_shape=(jax.ShapeDtypeS...  48 us
    pallas_call x10, Pallas kernels, weight_terms(): pl.pallas_call(functools.partial(term_kernel, len(encoded_parts), arrived...  29.8 us
    ppermute x7, starting transfers between devices, per_device(): lax.ppermute(block, ('z', 'ylo'), [(a * 2 + b, (a + dz) % 4 * 2 + (b + dy...  22.6 us
    ppermute x7, waiting for transfers between devices, per_device(): lax.ppermute(block, ('z', 'ylo'), [(a * 2 + b, (a + dz) % 4 * 2 + (b + dy...  15.9 us
    unnamed x116, local copies, waits for them, and re-layouts  15.6 us
  transfers between devices with their start and end apart: 53, of which 17 were waited for; matrix products, arithmetic and copies ran while one was open for 4% of the time, Pallas kernels for 36%

profile of v1, /device:TPU:6, one launch (start us, length us, event | category | flops | bytes accessed | tf_op | source)
XLA Modules:
  0.0 527.6 jit_solution(2168119104726438525)
XLA Ops:
  14.9 16.2 %collective-permute-done.beside = bf16[16,32,1024]{2,1,0:T(8,128)(2,1)} collective-permute-done((bf16[16,32,1024]{2,1,0:T(8,128)(2,1)}, bf16[16,32,1024]{2,1,0:T(8,128)(2,1)}, u32[]{:S(2)}, u32[]{:S(2)}) %collective-permute-start) | collective-permute-done | bytes 1048608 | tf_op jit(solution)/shard_map/ppermute | solution.py:21
  31.1 22.5 %collective-permute-done.14.beside = bf16[16,32,1024]{2,1,0:T(8,128)(2,1)} collective-permute-done((bf16[16,32,1024]{2,1,0:T(8,128)(2,1)}, bf16[16,32,1024]{2,1,0:T(8,128)(2,1)}, u32[]{:S(2)}, u32[]{:S(2)}) %collective-permute-start.14) | collective-permute-done | bytes 1048608 | tf_op jit(solution)/shard_map/ppermute | solution.py:21
  53.6 22.4 %collective-permute-done.24.beside = bf16[16,32,1024]{2,1,0:T(8,128)(2,1)S(1)} collective-permute-done((bf16[16,32,1024]{2,1,0:T(8,128)(2,1)}, bf16[16,32,1024]{2,1,0:T(8,128)(2,1)S(1)}, u32[]{:S(2)}, u32[]{:S(2)}) %collective-permute-start.24) | collective-permute-done | bytes 1048608 | tf_op jit(solution)/shard_map/ppermute | solution.py:21
  75.9 22.1 %collective-permute-done.34.beside = bf16[16,32,1024]{2,1,0:T(8,128)(2,1)S(1)} collective-permute-done((bf16[16,32,1024]{2,1,0:T(8,128)(2,1)S(1)}, bf16[16,32,1024]{2,1,0:T(8,128)(2,1)S(1)}, u32[]{:S(2)}, u32[]{:S(2)}) %collective-permute-start.34) | collective-permute-done | bytes 1048608 | tf_op jit(solution)/shard_map/ppermute | solution.py:21
  103.3 5.9 %pack.12 = bf16[8,32,1024]{2,1,0:T(8,128)(2,1)} custom-call(s32[5]{0:T(128)} %stack.97.place, s32[1,16]{1,0:T(1,128)} %copy-done.52, bf16[16,128,1024]{2,1,0:T(8,128)(2,1)} %own.31, bf16[16,32,1024]{2,1,0:T(8,128)(2,1)} %collective-permute-done.beside, bf16[16,128,1024]{2,1,0:T(8,128)(2,1)} %collective-permute-done.1.across, ...), custom_call_target="tpu_custom_call" | custom-call | bytes 1048576 | tf_op jit(solution)/shard_map/pack/pallas_call | solution.py:79
  122.7 8.2 %collective-permute-start.8 = (bf16[8,32,1024]{2,1,0:T(8,128)(2,1)}, bf16[8,32,1024]{2,1,0:T(8,128)(2,1)}, u32[]{:S(2)}, u32[]{:S(2)}) collective-permute-start(bf16[8,32,1024]{2,1,0:T(8,128)(2,1)} %pack.14), channel_id=1, source_target_pairs={{0,32},{32,64},{64,96},{96,0},{1,33},{33,65},{65,97},{97,1},{2,34}... | collective-permute-start | bytes 1572872 | tf_op jit(solution)/shard_map/ppermute | solution.py:21
  130.9 5.9 %pack.15 = bf16[8,32,1024]{2,1,0:T(8,128)(2,1)} custom-call(s32[5]{0:T(128)} %stack.97.place, s32[1,16]{1,0:T(1,128)} %copy-done.52, bf16[16,128,1024]{2,1,0:T(8,128)(2,1)} %own.31, bf16[16,32,1024]{2,1,0:T(8,128)(2,1)} %collective-permute-done.14.beside, bf16[16,128,1024]{2,1,0:T(8,128)(2,1)} %collective-permute-done.1.across, ...), custom_call_target="tpu_custom_call" | custom-call | bytes 1048576 | tf_op jit(solution)/shard_map/pack/pallas_call | solution.py:79
  149.0 8.2 %collective-permute-start.18 = (bf16[8,32,1024]{2,1,0:T(8,128)(2,1)}, bf16[8,32,1024]{2,1,0:T(8,128)(2,1)}, u32[]{:S(2)}, u32[]{:S(2)}) collective-permute-start(bf16[8,32,1024]{2,1,0:T(8,128)(2,1)} %pack.17), channel_id=1, source_target_pairs={{0,32},{32,64},{64,96},{96,0},{1,33},{33,65},{65,97},{97,1},{2,34}... | collective-permute-start | bytes 1572872 | tf_op jit(solution)/shard_map/ppermute | solution.py:21
  157.2 5.9 %pack.18 = bf16[8,32,1024]{2,1,0:T(8,128)(2,1)} custom-call(s32[5]{0:T(128)} %stack.97.place, s32[1,16]{1,0:T(1,128)} %copy-done.52, bf16[16,128,1024]{2,1,0:T(8,128)(2,1)} %own.31, bf16[16,32,1024]{2,1,0:T(8,128)(2,1)} %copy-done.39, bf16[16,128,1024]{2,1,0:T(8,128)(2,1)} %collective-permute-done.1.across, bf16[16,32,1024]{2,1,0:T(8,128)(2,1)} %collective-permute-done.25.corner), custom_call_target="tpu_custom_call" | custom-call | bytes 1048576 | tf_op jit(solution)/shard_map/pack/pallas_call | solution.py:79
  175.4 7.6 %collective-permute-start.28 = (bf16[8,32,1024]{2,1,0:T(8,128)(2,1)}, bf16[8,32,1024]{2,1,0:T(8,128)(2,1)S(1)}, u32[]{:S(2)}, u32[]{:S(2)}) collective-permute-start(bf16[8,32,1024]{2,1,0:T(8,128)(2,1)} %pack.20), channel_id=1, source_target_pairs={{0,32},{32,64},{64,96},{96,0},{1,33},{33,65},{65,97},{97,1},{2,34}... | collective-permute-start | bytes 1572872 | tf_op jit(solution)/shard_map/ppermute | solution.py:21
  183.0 17.8 %merge.4 = bf16[8,32,1024]{2,1,0:T(8,128)(2,1)} custom-call(s32[5]{0:T(128)} %stack.97.place, s32[1,16]{1,0:T(1,128)} %copy-done.51, bf16[16,128,1024]{2,1,0:T(8,128)(2,1)} %own.31, bf16[16,32,1024]{2,1,0:T(8,128)(2,1)} %collective-permute-done.beside, bf16[16,128,1024]{2,1,0:T(8,128)(2,1)} %collective-permute-done.1.across, ...), custom_call_target="tpu_custom_call" | custom-call | bytes 1048576 | tf_op jit(solution)/shard_map/merge/pallas_call | solution.py:79
  204.4 5.9 %pack.21 = bf16[8,32,1024]{2,1,0:T(8,128)(2,1)} custom-call(s32[5]{0:T(128)} %stack.97.place, s32[1,16]{1,0:T(1,128)} %copy-done.52, bf16[16,128,1024]{2,1,0:T(8,128)(2,1)} %own.31, bf16[16,32,1024]{2,1,0:T(8,128)(2,1)} %copy-done.38, bf16[16,128,1024]{2,1,0:T(8,128)(2,1)} %collective-permute-done.1.across, bf16[16,32,1024]{2,1,0:T(8,128)(2,1)} %copy-done.40), custom_call_target="tpu_custom_call" | custom-call | bytes 1048576 | tf_op jit(solution)/shard_map/pack/pallas_call | solution.py:79
  211.5 17.8 %merge.5 = bf16[8,32,1024]{2,1,0:T(8,128)(2,1)} custom-call(s32[5]{0:T(128)} %stack.97.place, s32[1,16]{1,0:T(1,128)} %copy-done.51, bf16[16,128,1024]{2,1,0:T(8,128)(2,1)} %own.31, bf16[16,32,1024]{2,1,0:T(8,128)(2,1)} %collective-permute-done.14.beside, bf16[16,128,1024]{2,1,0:T(8,128)(2,1)} %collective-permute-done.1.across, ...), custom_call_target="tpu_custom_call" | custom-call | bytes 1048576 | tf_op jit(solution)/shard_map/merge/pallas_call | solution.py:79
  240.6 7.7 %collective-permute-start.38 = (bf16[8,32,1024]{2,1,0:T(8,128)(2,1)}, bf16[8,32,1024]{2,1,0:T(8,128)(2,1)}, u32[]{:S(2)}, u32[]{:S(2)}) collective-permute-start(bf16[8,32,1024]{2,1,0:T(8,128)(2,1)} %pack.23), channel_id=1, source_target_pairs={{0,32},{32,64},{64,96},{96,0},{1,33},{33,65},{65,97},{97,1},{2,34}... | collective-permute-start | bytes 1572872 | tf_op jit(solution)/shard_map/ppermute | solution.py:21
  248.4 17.9 %merge.6 = bf16[8,32,1024]{2,1,0:T(8,128)(2,1)} custom-call(s32[5]{0:T(128)} %stack.97.place, s32[1,16]{1,0:T(1,128)} %copy-done.51, bf16[16,128,1024]{2,1,0:T(8,128)(2,1)} %own.31, bf16[16,32,1024]{2,1,0:T(8,128)(2,1)} %copy-done.39, bf16[16,128,1024]{2,1,0:T(8,128)(2,1)} %collective-permute-done.1.across, ...), custom_call_target="tpu_custom_call" | custom-call | bytes 1048576 | tf_op jit(solution)/shard_map/merge/pallas_call | solution.py:79
  276.9 17.8 %merge.7 = bf16[8,32,1024]{2,1,0:T(8,128)(2,1)} custom-call(s32[5]{0:T(128)} %stack.97.place, s32[1,16]{1,0:T(1,128)} %copy-done.51, bf16[16,128,1024]{2,1,0:T(8,128)(2,1)} %own.31, bf16[16,32,1024]{2,1,0:T(8,128)(2,1)} %copy-done.38, bf16[16,128,1024]{2,1,0:T(8,128)(2,1)} %collective-permute-done.1.across, bf16[16,32,1024]{2,1,0:T(8,128)(2,1)} %copy-done.40, ...), custom_call_target="tpu_custom_call" | custom-call | bytes 1048576 | tf_op jit(solution)/shard_map/merge/pallas_call | solution.py:79
  296.8 8.8 %collective-permute-done.39 = bf16[1,256,1024]{2,1,0:T(8,128)(2,1)S(1)} collective-permute-done((bf16[1,256,1024]{2,1,0:T(8,128)(2,1)}, bf16[1,256,1024]{2,1,0:T(8,128)(2,1)S(1)}, u32[]{:S(2)}, u32[]{:S(2)}) %collective-permute-start.39) | collective-permute-done | bytes 524320 | tf_op jit(solution)/shard_map/ppermute | solution.py:21
  310.7 5.4 %collective-permute-done.20.left = bf16[2,256,1024]{2,1,0:T(8,128)(2,1)} collective-permute-done((bf16[2,256,1024]{2,1,0:T(8,128)(2,1)S(1)}, bf16[2,256,1024]{2,1,0:T(8,128)(2,1)}, u32[]{:S(2)}, u32[]{:S(2)}) %collective-permute-start.20) | collective-permute-done | bytes 1048608 | tf_op jit(solution)/shard_map/ppermute | solution.py:21
  323.1 15.4 %collective-permute-done.30.left = bf16[2,256,1024]{2,1,0:T(8,128)(2,1)S(1)} collective-permute-done((bf16[2,256,1024]{2,1,0:T(8,128)(2,1)S(1)}, bf16[2,256,1024]{2,1,0:T(8,128)(2,1)S(1)}, u32[]{:S(2)}, u32[]{:S(2)}) %collective-permute-start.30) | collective-permute-done | bytes 1048608 | tf_op jit(solution)/shard_map/ppermute | solution.py:21
  344.9 16.1 %collective-permute-done.40.left = bf16[2,256,1024]{2,1,0:T(8,128)(2,1)S(1)} collective-permute-done((bf16[2,256,1024]{2,1,0:T(8,128)(2,1)S(1)}, bf16[2,256,1024]{2,1,0:T(8,128)(2,1)S(1)}, u32[]{:S(2)}, u32[]{:S(2)}) %collective-permute-start.40) | collective-permute-done | bytes 1048608 | tf_op jit(solution)/shard_map/ppermute | solution.py:21
  373.0 5.3 %collective-permute-done.13.far1 = bf16[1,256,1024]{2,1,0:T(8,128)(2,1)} collective-permute-done((bf16[1,256,1024]{2,1,0:T(8,128)(2,1)}, bf16[1,256,1024]{2,1,0:T(8,128)(2,1)}, u32[]{:S(2)}, u32[]{:S(2)}) %collective-permute-start.13) | collective-permute-done | bytes 524320 | tf_op jit(solution)/shard_map/ppermute | solution.py:21
  378.2 10.2 %collective-permute-start.42 = (bf16[1,256,1024]{2,1,0:T(8,128)(2,1)S(1)}, bf16[1,256,1024]{2,1,0:T(8,128)(2,1)S(1)}, u32[]{:S(2)}, u32[]{:S(2)}) collective-permute-start(bf16[1,256,1024]{2,1,0:T(8,128)(2,1)S(1)} %slice.54), channel_id=1, source_target_pairs={{0,2},{2,4},{4,6},{6,0},{1,3},{3,5},{5,7},{7,1},{8,10},{10,12},{12... | collective-permute-start | bytes 1572872 | tf_op jit(solution)/shard_map/ppermute | solution.py:21
  388.4 12.1 %project.4 = (bf16[256,512]{1,0:T(8,128)(2,1)S(1)}, bf16[256,512]{1,0:T(8,128)(2,1)S(1)}, bf16[8,256,1024]{2,1,0:T(8,128)(2,1)S(1)}) custom-call(s32[5]{0:T(128)S(1)} %copy-done.37, bf16[2,256,1024]{2,1,0:T(8,128)(2,1)S(1)} %maximum_select_fusion.own, bf16[2,256,1024]{2,1,0:T(8,128)(2,1)} %collective-permute-done.10.left, ...), custom_call_target="tpu_custom_call" | custom-call | flops 4294967296 | bytes 25165824 | tf_op jit(solution)/shard_map/project/pallas_call | solution.py:141
  403.3 12.0 %project.5 = (bf16[256,512]{1,0:T(8,128)(2,1)S(1)}, bf16[256,512]{1,0:T(8,128)(2,1)S(1)}, bf16[8,256,1024]{2,1,0:T(8,128)(2,1)S(1)}) custom-call(s32[5]{0:T(128)S(1)} %copy-done.37, bf16[2,256,1024]{2,1,0:T(8,128)(2,1)S(1)} %maximum_select_fusion.1.own, bf16[2,256,1024]{2,1,0:T(8,128)(2,1)} %collective-permute-done.20.left, ...), custom_call_target="tpu_custom_call" | custom-call | flops 4294967296 | bytes 25165824 | tf_op jit(solution)/shard_map/project/pallas_call | solution.py:141
  416.1 12.4 %project.6 = (bf16[256,512]{1,0:T(8,128)(2,1)S(1)}, bf16[256,512]{1,0:T(8,128)(2,1)S(1)}, bf16[8,256,1024]{2,1,0:T(8,128)(2,1)S(1)}) custom-call(s32[5]{0:T(128)S(1)} %copy-done.37, bf16[2,256,1024]{2,1,0:T(8,128)(2,1)S(1)} %copy-done.8, bf16[2,256,1024]{2,1,0:T(8,128)(2,1)S(1)} %copy-done.10, bf16[2,256,1024]{2,1,0:T(8,128)(2,1)S(1)} %copy-done.16, ...), custom_call_target="tpu_custom_call" | custom-call | flops 4294967296 | bytes 25165824 | tf_op jit(solution)/shard_map/project/pallas_call | solution.py:141
  431.4 11.5 %project.7 = (bf16[256,512]{1,0:T(8,128)(2,1)S(1)}, bf16[256,512]{1,0:T(8,128)(2,1)S(1)}, bf16[8,256,1024]{2,1,0:T(8,128)(2,1)S(1)}) custom-call(s32[5]{0:T(128)S(1)} %copy-done.37, bf16[2,256,1024]{2,1,0:T(8,128)(2,1)S(1)} %maximum_select_fusion.3.own, bf16[2,256,1024]{2,1,0:T(8,128)(2,1)S(1)} %copy-done.12, ...), custom_call_target="tpu_custom_call" | custom-call | flops 4294967296 | bytes 25165824 | tf_op jit(solution)/shard_map/project/pallas_call | solution.py:141
  447.9 5.9 %terms.10 = bf16[4,512,512]{2,1,0:T(8,128)(2,1)} custom-call(s32[5]{0:T(128)S(1)} %stack.104.refs_0_, bf16[512,1024]{1,0:T(8,128)(2,1)S(1)} %get-tuple-element.30.refs_1_, bf16[8,256,1024]{2,1,0:T(8,128)(2,1)S(1)} %get-tuple-element.31.refs_2_, bf16[8,256,1024]{2,1,0:T(8,128)(2,1)S(1)} %get-tuple-element.32.refs_3_, bf16[8,256,1024]{2,1,0:T(8,128)(2,1)} %copy-done.5, ...), custom_call_target="tpu_custom_call" | custom-call | flops 2147483648 | bytes 9437184 | tf_op jit(solution)/shard_map/terms/pallas_call | solution.py:318
  458.5 5.0 terms.15
  466.7 8.4 %collective-permute-start.45 = (bf16[1,512,512]{2,1,0:T(8,128)(2,1)S(1)}, bf16[1,512,512]{2,1,0:T(8,128)(2,1)S(1)}, u32[]{:S(2)}, u32[]{:S(2)}) collective-permute-start(bf16[1,512,512]{2,1,0:T(8,128)(2,1)S(1)} %terms.11), channel_id=1, source_target_pairs={{0,80},{16,64},{32,112},{48,96},{64,16},{80,0},{96,48},{112,32},{1... | collective-permute-start | bytes 1572872 | tf_op jit(solution)/shard_map/ppermute | solution.py:428
  485.5 4.2 collective-permute-start.48
  500.4 10.0 %collective-permute-done.46.refs_1_ = bf16[1,512,512]{2,1,0:T(8,128)(2,1)S(1)} collective-permute-done((bf16[1,512,512]{2,1,0:T(8,128)(2,1)S(1)}, bf16[1,512,512]{2,1,0:T(8,128)(2,1)S(1)}, u32[]{:S(2)}, u32[]{:S(2)}) %collective-permute-start.46) | collective-permute-done | bytes 524320 | tf_op jit(solution)/shard_map/ppermute | solution.py:428
  521.3 4.6 collective-permute-done.52.refs_6_
  (250 shorter events, 169.0 us)
Async XLA Ops:
  0.7 101.9 %collective-permute-start.1 = (bf16[16,128,1024]{2,1,0:T(8,128)(2,1)}, bf16[16,128,1024]{2,1,0:T(8,128)(2,1)}, u32[]{:S(2)}, u32[]{:S(2)}) collective-permute-start(bf16[16,128,1024]{2,1,0:T(8,128)(2,1)} %own.31), channel_id=1, source_target_pairs={{0,8},{8,0},{1,9},{9,1},{2,10},{10,2},{3,11},{11,3},{4,12},{12,4},... | collective-permute-start | bytes 12582920 | tf_op jit(solution)/shard_map/ppermute | solution.py:21
  6.4 47.2 %collective-permute-start.14 = (bf16[16,32,1024]{2,1,0:T(8,128)(2,1)}, bf16[16,32,1024]{2,1,0:T(8,128)(2,1)}, u32[]{:S(2)}, u32[]{:S(2)}) collective-permute-start(bf16[16,32,1024]{2,1,0:T(8,128)(2,1)} %get-tuple-element.37), channel_id=1, source_target_pairs={{0,16},{16,0},{1,17},{17,1},{2,18},{18,2},{3,19},{19,3},{4,20},{20... | collective-permute-start | bytes 3145736 | tf_op jit(solution)/shard_map/ppermute | solution.py:21
  6.9 69.1 %collective-permute-start.24 = (bf16[16,32,1024]{2,1,0:T(8,128)(2,1)}, bf16[16,32,1024]{2,1,0:T(8,128)(2,1)S(1)}, u32[]{:S(2)}, u32[]{:S(2)}) collective-permute-start(bf16[16,32,1024]{2,1,0:T(8,128)(2,1)} %get-tuple-element.36), channel_id=1, source_target_pairs={{0,16},{16,0},{1,17},{17,1},{2,18},{18,2},{3,19},{19,3},{4,20},{20... | collective-permute-start | bytes 3145736 | tf_op jit(solution)/shard_map/ppermute | solution.py:21
  14.5 83.5 %collective-permute-start.34 = (bf16[16,32,1024]{2,1,0:T(8,128)(2,1)S(1)}, bf16[16,32,1024]{2,1,0:T(8,128)(2,1)S(1)}, u32[]{:S(2)}, u32[]{:S(2)}) collective-permute-start(bf16[16,32,1024]{2,1,0:T(8,128)(2,1)S(1)} %get-tuple-element.35), channel_id=1, source_target_pairs={{0,16},{16,0},{1,17},{17,1},{2,18},{18,2},{3,19},{19,3},{4,20},{20... | collective-permute-start | bytes 3145736 | tf_op jit(solution)/shard_map/ppermute | solution.py:21
  31.1 67.6 %collective-permute-start.2 = (bf16[16,32,1024]{2,1,0:T(8,128)(2,1)}, bf16[16,32,1024]{2,1,0:T(8,128)(2,1)}, u32[]{:S(2)}, u32[]{:S(2)}) collective-permute-start(bf16[16,32,1024]{2,1,0:T(8,128)(2,1)} %collective-permute-done.beside), channel_id=1, source_target_pairs={{0,8},{8,0},{1,9},{9,1},{2,10},{10,2},{3,11},{11,3},{4,12},{12,4},... | collective-permute-start | bytes 3145736 | tf_op jit(solution)/shard_map/ppermute | solution.py:21
  53.6 69.1 %collective-permute-start.15 = (bf16[16,32,1024]{2,1,0:T(8,128)(2,1)}, bf16[16,32,1024]{2,1,0:T(8,128)(2,1)}, u32[]{:S(2)}, u32[]{:S(2)}) collective-permute-start(bf16[16,32,1024]{2,1,0:T(8,128)(2,1)} %collective-permute-done.14.beside), channel_id=1, source_target_pairs={{0,8},{8,0},{1,9},{9,1},{2,10},{10,2},{3,11},{11,3},{4,12},{12,4},... | collective-permute-start | bytes 3145736 | tf_op jit(solution)/shard_map/ppermute | solution.py:21
  75.9 60.9 %collective-permute-start.25 = (bf16[16,32,1024]{2,1,0:T(8,128)(2,1)S(1)}, bf16[16,32,1024]{2,1,0:T(8,128)(2,1)}, u32[]{:S(2)}, u32[]{:S(2)}) collective-permute-start(bf16[16,32,1024]{2,1,0:T(8,128)(2,1)S(1)} %collective-permute-done.24.beside), channel_id=1, source_target_pairs={{0,8},{8,0},{1,9},{9,1},{2,10},{10,2},{3,11},{11,3},{4,12},{12,4},... | collective-permute-start | bytes 3145736 | tf_op jit(solution)/shard_map/ppermute | solution.py:21
  98.0 44.4 %collective-permute-start.35 = (bf16[16,32,1024]{2,1,0:T(8,128)(2,1)S(1)}, bf16[16,32,1024]{2,1,0:T(8,128)(2,1)S(1)}, u32[]{:S(2)}, u32[]{:S(2)}) collective-permute-start(bf16[16,32,1024]{2,1,0:T(8,128)(2,1)S(1)} %collective-permute-done.34.beside), channel_id=1, source_target_pairs={{0,8},{8,0},{1,9},{9,1},{2,10},{10,2},{3,11},{11,3},{4,12},{12,4},... | collective-permute-start | bytes 3145736 | tf_op jit(solution)/shard_map/ppermute | solution.py:21
  109.2 39.8 %collective-permute-start.4 = (bf16[8,32,1024]{2,1,0:T(8,128)(2,1)}, bf16[8,32,1024]{2,1,0:T(8,128)(2,1)}, u32[]{:S(2)}, u32[]{:S(2)}) collective-permute-start(bf16[8,32,1024]{2,1,0:T(8,128)(2,1)} %pack.12), channel_id=1, source_target_pairs={{0,96},{32,0},{64,32},{96,64},{1,97},{33,1},{65,33},{97,65},{2,98}... | collective-permute-start | bytes 1572872 | tf_op jit(solution)/shard_map/ppermute | solution.py:21
  115.3 47.8 %collective-permute-start.6 = (bf16[8,32,1024]{2,1,0:T(8,128)(2,1)}, bf16[8,32,1024]{2,1,0:T(8,128)(2,1)}, u32[]{:S(2)}, u32[]{:S(2)}) collective-permute-start(bf16[8,32,1024]{2,1,0:T(8,128)(2,1)} %pack.13), channel_id=1, source_target_pairs={{0,64},{32,96},{64,0},{96,32},{1,65},{33,97},{65,1},{97,33},{2,66}... | collective-permute-start | bytes 1572872 | tf_op jit(solution)/shard_map/ppermute | solution.py:21
  122.7 49.6 %collective-permute-start.8 = (bf16[8,32,1024]{2,1,0:T(8,128)(2,1)}, bf16[8,32,1024]{2,1,0:T(8,128)(2,1)}, u32[]{:S(2)}, u32[]{:S(2)}) collective-permute-start(bf16[8,32,1024]{2,1,0:T(8,128)(2,1)} %pack.14), channel_id=1, source_target_pairs={{0,32},{32,64},{64,96},{96,0},{1,33},{33,65},{65,97},{97,1},{2,34}... | collective-permute-start | bytes 1572872 | tf_op jit(solution)/shard_map/ppermute | solution.py:21
  136.8 38.6 %collective-permute-start.16 = (bf16[8,32,1024]{2,1,0:T(8,128)(2,1)}, bf16[8,32,1024]{2,1,0:T(8,128)(2,1)S(1)}, u32[]{:S(2)}, u32[]{:S(2)}) collective-permute-start(bf16[8,32,1024]{2,1,0:T(8,128)(2,1)} %pack.15), channel_id=1, source_target_pairs={{0,96},{32,0},{64,32},{96,64},{1,97},{33,1},{65,33},{97,65},{2,98}... | collective-permute-start | bytes 1572872 | tf_op jit(solution)/shard_map/ppermute | solution.py:21
  142.4 58.4 %collective-permute-start.17 = (bf16[8,32,1024]{2,1,0:T(8,128)(2,1)}, bf16[8,32,1024]{2,1,0:T(8,128)(2,1)}, u32[]{:S(2)}, u32[]{:S(2)}) collective-permute-start(bf16[8,32,1024]{2,1,0:T(8,128)(2,1)} %pack.16), channel_id=1, source_target_pairs={{0,64},{32,96},{64,0},{96,32},{1,65},{33,97},{65,1},{97,33},{2,66}... | collective-permute-start | bytes 1572872 | tf_op jit(solution)/shard_map/ppermute | solution.py:21
  149.0 61.2 %collective-permute-start.18 = (bf16[8,32,1024]{2,1,0:T(8,128)(2,1)}, bf16[8,32,1024]{2,1,0:T(8,128)(2,1)}, u32[]{:S(2)}, u32[]{:S(2)}) collective-permute-start(bf16[8,32,1024]{2,1,0:T(8,128)(2,1)} %pack.17), channel_id=1, source_target_pairs={{0,32},{32,64},{64,96},{96,0},{1,33},{33,65},{65,97},{97,1},{2,34}... | collective-permute-start | bytes 1572872 | tf_op jit(solution)/shard_map/ppermute | solution.py:21
  163.1 66.2 %collective-permute-start.26 = (bf16[8,32,1024]{2,1,0:T(8,128)(2,1)}, bf16[8,32,1024]{2,1,0:T(8,128)(2,1)S(1)}, u32[]{:S(2)}, u32[]{:S(2)}) collective-permute-start(bf16[8,32,1024]{2,1,0:T(8,128)(2,1)} %pack.18), channel_id=1, source_target_pairs={{0,96},{32,0},{64,32},{96,64},{1,97},{33,1},{65,33},{97,65},{2,98}... | collective-permute-start | bytes 1572872 | tf_op jit(solution)/shard_map/ppermute | solution.py:21
  172.3 65.3 %collective-permute-start.27 = (bf16[8,32,1024]{2,1,0:T(8,128)(2,1)S(1)}, bf16[8,32,1024]{2,1,0:T(8,128)(2,1)S(1)}, u32[]{:S(2)}, u32[]{:S(2)}) collective-permute-start(bf16[8,32,1024]{2,1,0:T(8,128)(2,1)S(1)} %copy-done.50), channel_id=1, source_target_pairs={{0,64},{32,96},{64,0},{96,32},{1,65},{33,97},{65,1},{97,33},{2,66}... | collective-permute-start | bytes 1572872 | tf_op jit(solution)/shard_map/ppermute | solution.py:21
  175.4 65.2 %collective-permute-start.28 = (bf16[8,32,1024]{2,1,0:T(8,128)(2,1)}, bf16[8,32,1024]{2,1,0:T(8,128)(2,1)S(1)}, u32[]{:S(2)}, u32[]{:S(2)}) collective-permute-start(bf16[8,32,1024]{2,1,0:T(8,128)(2,1)} %pack.20), channel_id=1, source_target_pairs={{0,32},{32,64},{64,96},{96,0},{1,33},{33,65},{65,97},{97,1},{2,34}... | collective-permute-start | bytes 1572872 | tf_op jit(solution)/shard_map/ppermute | solution.py:21
  200.8 65.5 %collective-permute-start.9 = (bf16[1,256,1024]{2,1,0:T(8,128)(2,1)}, bf16[1,256,1024]{2,1,0:T(8,128)(2,1)S(1)}, u32[]{:S(2)}, u32[]{:S(2)}) collective-permute-start(bf16[1,256,1024]{2,1,0:T(8,128)(2,1)} %bitcast.18), channel_id=1, source_target_pairs={{0,1},{1,0},{2,3},{3,2},{4,5},{5,4},{6,7},{7,6},{8,9},{9,8},{10,11... | collective-permute-start | bytes 1572872 | tf_op jit(solution)/shard_map/ppermute | solution.py:21
  210.2 61.4 %collective-permute-start.36 = (bf16[8,32,1024]{2,1,0:T(8,128)(2,1)}, bf16[8,32,1024]{2,1,0:T(8,128)(2,1)S(1)}, u32[]{:S(2)}, u32[]{:S(2)}) collective-permute-start(bf16[8,32,1024]{2,1,0:T(8,128)(2,1)} %pack.21), channel_id=1, source_target_pairs={{0,96},{32,0},{64,32},{96,64},{1,97},{33,1},{65,33},{97,65},{2,98}... | collective-permute-start | bytes 1572872 | tf_op jit(solution)/shard_map/ppermute | solution.py:21
  229.3 42.9 %collective-permute-start.19 = (bf16[1,256,1024]{2,1,0:T(8,128)(2,1)}, bf16[1,256,1024]{2,1,0:T(8,128)(2,1)}, u32[]{:S(2)}, u32[]{:S(2)}) collective-permute-start(bf16[1,256,1024]{2,1,0:T(8,128)(2,1)} %bitcast.20), channel_id=1, source_target_pairs={{0,1},{1,0},{2,3},{3,2},{4,5},{5,4},{6,7},{7,6},{8,9},{9,8},{10,11... | collective-permute-start | bytes 1572872 | tf_op jit(solution)/shard_map/ppermute | solution.py:21
  237.7 37.5 %collective-permute-start.37 = (bf16[8,32,1024]{2,1,0:T(8,128)(2,1)}, bf16[8,32,1024]{2,1,0:T(8,128)(2,1)}, u32[]{:S(2)}, u32[]{:S(2)}) collective-permute-start(bf16[8,32,1024]{2,1,0:T(8,128)(2,1)} %pack.22), channel_id=1, source_target_pairs={{0,64},{32,96},{64,0},{96,32},{1,65},{33,97},{65,1},{97,33},{2,66}... | collective-permute-start | bytes 1572872 | tf_op jit(solution)/shard_map/ppermute | solution.py:21
  275.2 41.0 %collective-permute-start.20 = (bf16[2,256,1024]{2,1,0:T(8,128)(2,1)S(1)}, bf16[2,256,1024]{2,1,0:T(8,128)(2,1)}, u32[]{:S(2)}, u32[]{:S(2)}) collective-permute-start(bf16[2,256,1024]{2,1,0:T(8,128)(2,1)S(1)} %maximum_select_fusion.1.own), channel_id=1, source_target_pairs={{0,2},{2,4},{4,6},{6,0},{1,3},{3,5},{5,7},{7,1},{8,10},{10,12},{12... | collective-permute-start | bytes 3145736 | tf_op jit(solution)/shard_map/ppermute | solution.py:21
  307.4 37.5 %collective-permute-start.31 = (bf16[2,256,1024]{2,1,0:T(8,128)(2,1)S(1)}, bf16[2,256,1024]{2,1,0:T(8,128)(2,1)S(1)}, u32[]{:S(2)}, u32[]{:S(2)}) collective-permute-start(bf16[2,256,1024]{2,1,0:T(8,128)(2,1)S(1)} %maximum_select_fusion.2.own), channel_id=1, source_target_pairs={{0,6},{2,0},{4,2},{6,4},{1,7},{3,1},{5,3},{7,5},{8,14},{10,8},{12,... | collective-permute-start | bytes 3145736 | tf_op jit(solution)/shard_map/ppermute | solution.py:21
  309.2 51.7 %collective-permute-start.40 = (bf16[2,256,1024]{2,1,0:T(8,128)(2,1)S(1)}, bf16[2,256,1024]{2,1,0:T(8,128)(2,1)S(1)}, u32[]{:S(2)}, u32[]{:S(2)}) collective-permute-start(bf16[2,256,1024]{2,1,0:T(8,128)(2,1)S(1)} %maximum_select_fusion.3.own), channel_id=1, source_target_pairs={{0,2},{2,4},{4,6},{6,0},{1,3},{3,5},{5,7},{7,1},{8,10},{10,12},{12... | collective-permute-start | bytes 3145736 | tf_op jit(solution)/shard_map/ppermute | solution.py:21
  316.1 51.3 %collective-permute-start.41 = (bf16[2,256,1024]{2,1,0:T(8,128)(2,1)S(1)}, bf16[2,256,1024]{2,1,0:T(8,128)(2,1)}, u32[]{:S(2)}, u32[]{:S(2)}) collective-permute-start(bf16[2,256,1024]{2,1,0:T(8,128)(2,1)S(1)} %maximum_select_fusion.3.own), channel_id=1, source_target_pairs={{0,6},{2,0},{4,2},{6,4},{1,7},{3,1},{5,3},{7,5},{8,14},{10,8},{12,... | collective-permute-start | bytes 3145736 | tf_op jit(solution)/shard_map/ppermute | solution.py:21
  322.4 49.9 %collective-permute-start.12 = (bf16[1,256,1024]{2,1,0:T(8,128)(2,1)}, bf16[1,256,1024]{2,1,0:T(8,128)(2,1)}, u32[]{:S(2)}, u32[]{:S(2)}) collective-permute-start(bf16[1,256,1024]{2,1,0:T(8,128)(2,1)} %slice.48), channel_id=1, source_target_pairs={{0,2},{2,4},{4,6},{6,0},{1,3},{3,5},{5,7},{7,1},{8,10},{10,12},{12... | collective-permute-start | bytes 1572872 | tf_op jit(solution)/shard_map/ppermute | solution.py:21
  338.5 39.7 %collective-permute-start.13 = (bf16[1,256,1024]{2,1,0:T(8,128)(2,1)}, bf16[1,256,1024]{2,1,0:T(8,128)(2,1)}, u32[]{:S(2)}, u32[]{:S(2)}) collective-permute-start(bf16[1,256,1024]{2,1,0:T(8,128)(2,1)} %slice.49), channel_id=1, source_target_pairs={{0,6},{2,0},{4,2},{6,4},{1,7},{3,1},{5,3},{7,5},{8,14},{10,8},{12,... | collective-permute-start | bytes 1572872 | tf_op jit(solution)/shard_map/ppermute | solution.py:21
  344.9 56.3 %collective-permute-start.22 = (bf16[1,256,1024]{2,1,0:T(8,128)(2,1)}, bf16[1,256,1024]{2,1,0:T(8,128)(2,1)}, u32[]{:S(2)}, u32[]{:S(2)}) collective-permute-start(bf16[1,256,1024]{2,1,0:T(8,128)(2,1)} %slice.50), channel_id=1, source_target_pairs={{0,2},{2,4},{4,6},{6,0},{1,3},{3,5},{5,7},{7,1},{8,10},{10,12},{12... | collective-permute-start | bytes 1572872 | tf_op jit(solution)/shard_map/ppermute | solution.py:21
  362.0 41.3 %collective-permute-start.23 = (bf16[1,256,1024]{2,1,0:T(8,128)(2,1)}, bf16[1,256,1024]{2,1,0:T(8,128)(2,1)}, u32[]{:S(2)}, u32[]{:S(2)}) collective-permute-start(bf16[1,256,1024]{2,1,0:T(8,128)(2,1)} %slice.51), channel_id=1, source_target_pairs={{0,6},{2,0},{4,2},{6,4},{1,7},{3,1},{5,3},{7,5},{8,14},{10,8},{12,... | collective-permute-start | bytes 1572872 | tf_op jit(solution)/shard_map/ppermute | solution.py:21
  367.5 48.6 %collective-permute-start.32 = (bf16[1,256,1024]{2,1,0:T(8,128)(2,1)S(1)}, bf16[1,256,1024]{2,1,0:T(8,128)(2,1)S(1)}, u32[]{:S(2)}, u32[]{:S(2)}) collective-permute-start(bf16[1,256,1024]{2,1,0:T(8,128)(2,1)S(1)} %slice.52), channel_id=1, source_target_pairs={{0,2},{2,4},{4,6},{6,0},{1,3},{3,5},{5,7},{7,1},{8,10},{10,12},{12... | collective-permute-start | bytes 1572872 | tf_op jit(solution)/shard_map/ppermute | solution.py:21
  372.3 43.8 %collective-permute-start.33 = (bf16[1,256,1024]{2,1,0:T(8,128)(2,1)S(1)}, bf16[1,256,1024]{2,1,0:T(8,128)(2,1)S(1)}, u32[]{:S(2)}, u32[]{:S(2)}) collective-permute-start(bf16[1,256,1024]{2,1,0:T(8,128)(2,1)S(1)} %slice.53), channel_id=1, source_target_pairs={{0,6},{2,0},{4,2},{6,4},{1,7},{3,1},{5,3},{7,5},{8,14},{10,8},{12,... | collective-permute-start | bytes 1572872 | tf_op jit(solution)/shard_map/ppermute | solution.py:21
  378.2 53.1 %collective-permute-start.42 = (bf16[1,256,1024]{2,1,0:T(8,128)(2,1)S(1)}, bf16[1,256,1024]{2,1,0:T(8,128)(2,1)S(1)}, u32[]{:S(2)}, u32[]{:S(2)}) collective-permute-start(bf16[1,256,1024]{2,1,0:T(8,128)(2,1)S(1)} %slice.54), channel_id=1, source_target_pairs={{0,2},{2,4},{4,6},{6,0},{1,3},{3,5},{5,7},{7,1},{8,10},{10,12},{12... | collective-permute-start | bytes 1572872 | tf_op jit(solution)/shard_map/ppermute | solution.py:21
  (78 other events, 1620.4 us)

commit v2 on v1

v2 whole, which is shorter than its diff:
```python
import functools

import jax
import jax.numpy as jnp
from jax import lax
from jax.experimental import pallas as pl
from jax.experimental.pallas import tpu as pltpu
from jax.sharding import Mesh
from jax.sharding import PartitionSpec as P

HEAD_DIM = 128
SPAN_LEN = 64
CHUNKS = (32, 32, 32, 32)
DB = ("z", "ylo", "core")
MP = ("x", "yhi")
VMEM_LIMIT = 60 * 1024 * 1024
SMALL = pl.CostEstimate(flops=1, bytes_accessed=1, transcendentals=0)
GROUPS = ((0, 2), (2, 8))
TARGETS = ((2, 1), (2, 0), (1, 1), (3, 1), (1, 0), (3, 0), (0, 1), (0, 0))


def ring(values, axis, shift, size):
    return lax.ppermute(values, axis, [(i, (i + shift) % size) for i in range(size)])


def tie(values, *others):
    return lax.optimization_barrier((values, *others))[0]


def run_copies(copies):
    for act in ("start", "wait"):
        for condition, source, target, sem in copies:
            copy = pltpu.make_async_copy(source, target, sem)
            pl.when(condition)(getattr(copy, act))


def run_copies(copies):
    for act in ("start", "wait"):
        for condition, source, target, sem in copies:
            copy = pltpu.make_async_copy(source, target, sem)
            pl.when(condition)(getattr(copy, act))


def planes_kernel(first, rows, place, one, two, three, own, across, packets, sems):
    chip = place[0] * 2 + place[1]
    count = one.shape[1] // 4
    copies = []
    for n, asked in enumerate((one, two, three)):
        base = (place[0] + n + 1) % 4 * 8
        for group in range(2):
            for i in range(count):
                here = asked[group, i] == chip
                mine = asked[group, count + i] == place[2]
                slot, rank = asked[group, 2 * count + i], asked[group, 3 * count + i]
                sem = sems.at[(n * 2 + group) * count + i]
                target = packets.at[base + group * 4 + rank]
                cut = (slot, pl.ds(first, rows))
                copies.append((here & mine, own.at[cut], target, sem))
                copies.append((here & ~mine, across.at[cut], target, sem))
    run_copies(copies)


def collect_kernel(first, rows, group, place, both, own, across, packets, *refs):
    output, sems = refs[-2:]
    count = both.shape[1] // 4
    copies = []
    for i in range(count):
        chip = both[group, i]
        plane = chip // 2
        side, near = chip % 2 == place[1], plane == place[0]
        mine = both[group, count + i] == place[2]
        slot, rank = both[group, 2 * count + i], both[group, 3 * count + i]
        sem, target = sems.at[i], output.at[i]
        cut = (slot, pl.ds(first, rows))
        copies.append((side & near & mine, own.at[cut], target, sem))
        copies.append((side & near & ~mine, across.at[cut], target, sem))
        copies.append((side & ~near, packets.at[plane * 8 + group * 4 + rank], target, sem))
        if group == 0:
            copies.append((~side, refs[0].at[i], target, sem))
    run_copies(copies)


def pack_kernel(first, rows, place, both, one, two, three, own, across, packets, sems):
    chip = place[0] * 2 + place[1]
    count = both.shape[1] // 4
    copies = []
    for n, asked in enumerate((both, one, two, three)):
        for group in range(2):
            base = ((place[0] + n) % 4 * 2 + (place[1] + group) % 2) * 4
            for i in range(count):
                here = asked[group, i] == chip
                mine = asked[group, count + i] == place[2]
                slot, rank = asked[group, 2 * count + i], asked[group, 3 * count + i]
                sem = sems.at[(n * 2 + group) * count + i]
                cut = (slot, pl.ds(first, rows))
                copies.append((here & mine, own.at[cut], packets.at[base + rank], sem))
                copies.append((here & ~mine, across.at[cut], packets.at[base + rank], sem))
    run_copies(copies)


def merge_kernel(wanted, packets, output, sems):
    count = wanted.shape[1] // 4
    copies = [
        pltpu.make_async_copy(
            packets.at[wanted[0, i] * 4 + wanted[0, 3 * count + i]], output.at[i], sems.at[i]
        )
        for i in range(count)
    ]
    for copy in copies:
        copy.start()
    for copy in copies:
        copy.wait()


def copies_call(kernel, name, shape, scalars, arrays, sems):
    return pl.pallas_call(
        kernel,
        name=name,
        out_shape=jax.ShapeDtypeStruct(shape, jnp.bfloat16),
        grid_spec=pltpu.PrefetchScalarGridSpec(
            num_scalar_prefetch=len(scalars),
            grid=(1,),
            in_specs=[pl.BlockSpec(memory_space=pl.ANY)] * len(arrays),
            out_specs=pl.BlockSpec(shape, lambda *_: (0, 0, 0)),
            scratch_shapes=[pltpu.SemaphoreType.DMA((sems,))],
        ),
        compiler_params=pltpu.CompilerParams(vmem_limit_bytes=VMEM_LIMIT),
        cost_estimate=SMALL,
    )(*scalars, *arrays)


def project_kernel(hops, first, starts, ends, joins, place, *refs):
    count = len(hops)
    pieces, key_weight = refs[:count], refs[count]
    refs = refs[count + 1:]
    if not starts:
        begun, refs = refs[0], refs[1:]
    refs = refs[sum(joins):]
    keys, mine, theirs, held, weights, piece_sems, weight_sems, mine_sems, their_sems = refs
    rows, depth = pieces[0].shape
    half = depth // 2
    columns = [
        pl.ds(pl.multiple_of(core * half, half), half) for core in (place[2], 1 - place[2])
    ]
    piece_reads, weight_reads, writes = [], [], []
    for n, (hop, side) in enumerate(hops):
        at = (place[3] + hop) % 4 * 2 + (place[4] + side) % 2
        cut = pl.ds(pl.multiple_of(at * depth, depth), depth)
        piece_reads.append(pltpu.make_async_copy(pieces[n], held.at[n], piece_sems.at[n]))
        weight_reads.append(
            pltpu.make_async_copy(key_weight.at[cut], weights.at[n], weight_sems.at[n])
        )
        writes.append((
            pltpu.make_async_copy(
                held.at[n, :, columns[0]], mine.at[at, pl.ds(first, rows)], mine_sems.at[n]
            ),
            pltpu.make_async_copy(
                held.at[n, :, columns[1]], theirs.at[at], their_sems.at[n]
            ),
        ))
    for n in range(count):
        piece_reads[n].start()
        weight_reads[n].start()
    total = None if starts else begun[...]
    for n in range(count):
        piece_reads[n].wait()
        for copy in writes[n]:
            copy.start()
        weight_reads[n].wait()
        part = jnp.dot(held[n], weights[n], preferred_element_type=jnp.float32)
        total = part if total is None else total + part
    keys[...] = total.astype(keys.dtype)
    for pair in writes:
        for copy in pair:
            copy.wait()


def project(place, pieces, hops, first, key_weight, mine=None, theirs=None, begun=None, ends=True):
    rows, depth = pieces[0].shape
    width = key_weight.shape[1]
    count = len(pieces)
    whole = pl.BlockSpec((rows, width), lambda step, place: (0, 0))
    anywhere = pl.BlockSpec(memory_space=pl.ANY)
    kind = jnp.bfloat16 if ends else jnp.float32
    operands = [place, *pieces, key_weight]
    in_specs = [anywhere] * (count + 1)
    aliases = {}
    if begun is not None:
        operands.append(begun)
        in_specs.append(whole)
    for n, joined in enumerate((mine, theirs)):
        if joined is not None:
            operands.append(joined)
            in_specs.append(anywhere)
            aliases[len(operands) - 1] = n + 1
    sems = pltpu.SemaphoreType.DMA((count,))
    return pl.pallas_call(
        functools.partial(
            project_kernel, hops, first, begun is None, ends,
            (mine is not None, theirs is not None),
        ),
        name="project",
        out_shape=(
            jax.ShapeDtypeStruct((rows, width), kind),
            jax.ShapeDtypeStruct((8, 8 * sum(CHUNKS), depth // 2), jnp.bfloat16),
            jax.ShapeDtypeStruct((8, rows, depth // 2), jnp.bfloat16),
        ),
        grid_spec=pltpu.PrefetchScalarGridSpec(
            num_scalar_prefetch=1,
            grid=(1,),
            in_specs=in_specs,
            out_specs=(whole, anywhere, anywhere),
            scratch_shapes=[
                pltpu.VMEM((count, rows, depth), jnp.bfloat16),
                pltpu.VMEM((count, depth, width), jnp.bfloat16),
                sems, sems, sems, sems,
            ],
        ),
        input_output_aliases=aliases,
        compiler_params=pltpu.CompilerParams(vmem_limit_bytes=VMEM_LIMIT),
        cost_estimate=SMALL,
    )(*operands)


def value_kernel(place, mine, *refs):
    step = pl.program_id(0)
    other_parts, (weight, values, total) = refs[:-3], refs[-3:]
    half = weight.shape[0] // 2
    near, away = [
        weight[pl.ds(pl.multiple_of(core * half, half), half), :]
        for core in (place[2], 1 - place[2])
    ]

    @pl.when(step == 0)
    def _():
        total[...] = jnp.zeros_like(total)

    total[...] += jnp.dot(mine[0], near, preferred_element_type=jnp.float32)
    start = 0
    for part in other_parts:
        rows = part.shape[1]
        total[start:start + rows] += jnp.dot(part[0], away, preferred_element_type=jnp.float32)
        start += rows

    @pl.when(step == 7)
    def _():
        values[...] = total[...].astype(values.dtype)


def project_values(place, mine, other_parts, value_weight):
    rows, half = mine.shape[1:]
    width = value_weight.shape[1]
    return pl.pallas_call(
        value_kernel,
        name="values",
        out_shape=jax.ShapeDtypeStruct((rows, width), jnp.bfloat16),
        grid_spec=pltpu.PrefetchScalarGridSpec(
            num_scalar_prefetch=1,
            grid=(8,),
            in_specs=[pl.BlockSpec((1, rows, half), lambda step, place: (step, 0, 0))]
            + [
                pl.BlockSpec((1, part.shape[1], half), lambda step, place: (step, 0, 0))
                for part in other_parts
            ]
            + [pl.BlockSpec((2 * half, width), lambda step, place: (step, 0))],
            out_specs=pl.BlockSpec((rows, width), lambda step, place: (0, 0)),
            scratch_shapes=[pltpu.VMEM((rows, width), jnp.float32)],
        ),
        compiler_params=pltpu.CompilerParams(vmem_limit_bytes=VMEM_LIMIT),
        cost_estimate=SMALL,
    )(place, mine, *other_parts, value_weight)


def span_rows(parts, span, low, high):
    pieces = []
    for part in parts:
        size = part.shape[0] // 4
        pieces.append(part[span * size:(span + 1) * size, low:high])
    return jnp.concatenate(pieces, axis=0)


def parts_of(rows, sizes):
    parts, start = [], 0
    for size in sizes:
        parts.append(rows.at[start:start + size])
        start += size
    return parts


def weigh_kernel(chunks, *refs):
    queries, cotangent = refs[0], refs[1]
    key_parts = refs[2:2 + chunks]
    chances, gradient, stacked = refs[2 + chunks:]
    width = queries.shape[1]
    scale = HEAD_DIM ** (-0.5)
    for span in range(4):
        tokens = slice(span * SPAN_LEN, (span + 1) * SPAN_LEN)
        for head in range(width // HEAD_DIM):
            low, high = head * HEAD_DIM, (head + 1) * HEAD_DIM
            keys = span_rows(key_parts, span, low, high)
            scores = lax.dot_general(
                queries[tokens, low:high], keys, (((1,), (1,)), ((), ())),
                preferred_element_type=jnp.float32,
            ) * scale
            raised = jnp.exp(scores - jnp.max(scores, axis=-1, keepdims=True))
            found = raised / jnp.sum(raised, axis=-1, keepdims=True)
            chances[span * (width // HEAD_DIM) + head] = found
            part = lax.dot_general(
                found.astype(jnp.bfloat16), cotangent[tokens, low:high], (((0,), (0,)), ((), ())),
                preferred_element_type=jnp.float32,
            ).astype(jnp.bfloat16)
            base, start = 0, 0
            for key_part in key_parts:
                size = key_part.shape[0] // 4
                at = base + span * size
                stacked[at:at + size, low:high] = part[start:start + size]
                start += size
                base += key_part.shape[0]
    gradient[...] = stacked[...].T


def weigh(queries, cotangent, key_parts):
    tokens, width = queries.shape
    rows = sum(part.shape[0] for part in key_parts)
    heads = width // HEAD_DIM
    vmem = pl.BlockSpec(memory_space=pltpu.VMEM)
    return pl.pallas_call(
        functools.partial(weigh_kernel, len(key_parts)),
        name="weigh",
        out_shape=(
            jax.ShapeDtypeStruct((4 * heads, SPAN_LEN, rows // 4), jnp.float32),
            jax.ShapeDtypeStruct((width, rows), jnp.bfloat16),
        ),
        in_specs=[vmem] * (2 + len(key_parts)),
        out_specs=(vmem, vmem),
        scratch_shapes=[pltpu.VMEM((rows, width), jnp.bfloat16)],
        compiler_params=pltpu.CompilerParams(vmem_limit_bytes=VMEM_LIMIT),
        cost_estimate=SMALL,
    )(queries, cotangent, *key_parts)


def attend_kernel(chunks, *refs):
    cotangent, chances, value_rows = refs[:3]
    key_parts = refs[3:3 + chunks]
    attended, query_grad = refs[3 + chunks:]
    value_parts = parts_of(value_rows, [part.shape[0] for part in key_parts])
    width = cotangent.shape[1]
    scale = HEAD_DIM ** (-0.5)
    for span in range(4):
        tokens = slice(span * SPAN_LEN, (span + 1) * SPAN_LEN)
        for head in range(width // HEAD_DIM):
            low, high = head * HEAD_DIM, (head + 1) * HEAD_DIM
            keys = span_rows(key_parts, span, low, high)
            values = span_rows(value_parts, span, low, high)
            found = chances[span * (width // HEAD_DIM) + head]
            attended[tokens, low:high] = jnp.dot(
                found.astype(jnp.bfloat16), values, preferred_element_type=jnp.float32
            ).astype(jnp.bfloat16)
            slope = lax.dot_general(
                cotangent[tokens, low:high], values, (((1,), (1,)), ((), ())),
                preferred_element_type=jnp.float32,
            )
            centre = jnp.sum(found * slope, axis=-1, keepdims=True)
            score_grad = (found * (slope - centre)).astype(jnp.bfloat16)
            query_grad[tokens, low:high] = (
                jnp.dot(score_grad, keys, preferred_element_type=jnp.float32) * scale
            ).astype(jnp.bfloat16)


def attend(cotangent, chances, key_parts, values):
    tokens, width = cotangent.shape
    rows = sum(part.shape[0] for part in key_parts)
    vmem = pl.BlockSpec(memory_space=pltpu.VMEM)
    return pl.pallas_call(
        functools.partial(attend_kernel, len(key_parts)),
        name="attend",
        out_shape=(
            jax.ShapeDtypeStruct((tokens, width), jnp.bfloat16),
            jax.ShapeDtypeStruct((tokens, width), jnp.bfloat16),
        ),
        in_specs=[vmem] * (3 + len(key_parts)),
        out_specs=(vmem, vmem),
        compiler_params=pltpu.CompilerParams(vmem_limit_bytes=VMEM_LIMIT),
        cost_estimate=SMALL,
    )(cotangent, chances, values, *key_parts)


def term_kernel(chunks, place, gradient, mine, their_gradient, *refs):
    step = pl.program_id(0)
    their_parts, outputs = refs[:chunks], refs[chunks:]
    total = jnp.dot(gradient[...], mine[0], preferred_element_type=jnp.float32)
    theirs, start = None, 0
    for part in their_parts:
        rows = part.shape[1]
        term = jnp.dot(
            their_gradient[:, start:start + rows], part[0], preferred_element_type=jnp.float32
        )
        theirs = term if theirs is None else theirs + term
        start += rows
    both = total.astype(jnp.bfloat16).astype(jnp.float32) + theirs.astype(jnp.bfloat16).astype(
        jnp.float32
    )
    for n, output in enumerate(outputs):
        @pl.when(step == n)
        def _():
            output[...] = both.astype(jnp.bfloat16)


def weight_terms(place, targets, gradient, mine, their_gradient, their_parts):
    count = len(targets)
    width, rows = gradient.shape
    half = mine.shape[2]

    def block_of(n, place):
        dz, dy = jnp.int32(targets[0][0]), jnp.int32(targets[0][1])
        for m in range(1, count):
            dz = jnp.where(n == m, targets[m][0], dz)
            dy = jnp.where(n == m, targets[m][1], dy)
        return (place[0] + dz) % 4 * 2 + (place[1] + dy) % 2, 0, 0

    whole = pl.BlockSpec((width, rows), lambda n, place: (0, 0))
    return pl.pallas_call(
        functools.partial(term_kernel, len(their_parts)),
        name="terms",
        out_shape=[jax.ShapeDtypeStruct((width, half), jnp.bfloat16)] * count,
        grid_spec=pltpu.PrefetchScalarGridSpec(
            num_scalar_prefetch=1,
            grid=(count,),
            in_specs=[whole, pl.BlockSpec((1, rows, half), block_of), whole]
            + [pl.BlockSpec((1, part.shape[1], half), block_of) for part in their_parts],
            out_specs=[pl.BlockSpec((width, half), lambda n, place: (0, 0))] * count,
        ),
        compiler_params=pltpu.CompilerParams(vmem_limit_bytes=VMEM_LIMIT),
        cost_estimate=SMALL,
    )(place, gradient, mine, their_gradient, *their_parts)


def total_kernel(*refs):
    output = refs[-1]
    total = refs[0][...].astype(jnp.float32)
    for block in refs[1:-1]:
        total += block[...].astype(jnp.float32)
    output[...] = total.T


def add_blocks(blocks):
    width, depth = blocks[0].shape
    vmem = pl.BlockSpec(memory_space=pltpu.VMEM)
    return pl.pallas_call(
        total_kernel,
        name="total",
        out_shape=jax.ShapeDtypeStruct((depth, width), jnp.float32),
        in_specs=[vmem] * len(blocks),
        out_specs=vmem,
        compiler_params=pltpu.CompilerParams(vmem_limit_bytes=VMEM_LIMIT),
        cost_estimate=SMALL,
    )(*blocks)


def per_device(
    queries, database, neighbor_owner, neighbor_slot, key_weight, value_weight, cotangent
):
    z, ylo, core = lax.axis_index("z"), lax.axis_index("ylo"), lax.axis_index("core")
    x, yhi = lax.axis_index("x"), lax.axis_index("yhi")
    place = jnp.stack([z, ylo, core, x, yhi]).astype(jnp.int32)
    count = neighbor_owner.shape[0] * neighbor_owner.shape[1]
    width = database.shape[2]
    owners = neighbor_owner.reshape(1, count)
    chips = owners // 2
    earlier = jnp.arange(count)[:, None] > jnp.arange(count)[None, :]
    ranks = jnp.sum((chips.reshape(count, 1) == chips) & earlier, axis=1).reshape(1, count)
    wanted = jnp.concatenate(
        [chips, owners % 2, neighbor_slot.reshape(1, count), ranks.astype(jnp.int32)], axis=1
    )
    both = jnp.concatenate([wanted, ring(wanted, "ylo", 1, 2)], axis=0)
    asked = [ring(both, "z", -n, 4) for n in (1, 2, 3)]
    across = ring(database, "core", 1, 2)

    last = len(CHUNKS) - 1
    firsts = [sum(CHUNKS[:k]) for k in range(last + 1)]

    near_hops = ((0, 0), (3, 0), (1, 0), (0, 1), (3, 1), (1, 1))
    far_hops = ((2, 0), (2, 1))

    def shape(k):
        return count, CHUNKS[k], width

    def hand(k, packets, *after):
        given = copies_call(
            functools.partial(collect_kernel, firsts[k], CHUNKS[k], 1), "hand", shape(k),
            [tie(place, *after), both], [database, across, packets], count,
        )
        return given, ring(given, "ylo", 1, 2)

    def merge(k, packets, given, *after):
        return copies_call(
            functools.partial(collect_kernel, firsts[k], CHUNKS[k], 0), "merge", shape(k),
            [tie(place, *after), both], [database, across, packets, given], count,
        )

    def spread(own, *after):
        own = own.reshape(-1, width)
        left, right = ring(own, "x", 1, 4), ring(own, "x", -1, 4)
        other = ring(own, "yhi", 1, 2)
        sent = tie(other, left, right, *after)
        near = (own, left, right, other, ring(sent, "x", 1, 4), ring(sent, "x", -1, 4))
        return near, (near[1], near[5])

    def pass_on(ends):
        return ring(ends[0], "x", 1, 4), ring(ends[1], "x", -1, 4)

    def send_planes(packets, *after):
        return lax.all_to_all(tie(packets, *after), "z", 0, 0, tiled=True)

    packets = copies_call(
        functools.partial(pack_kernel, 0, CHUNKS[0]), "pack", (32, CHUNKS[0], width),
        [place, both, *asked], [database, across], 8 * count,
    )
    arrived = lax.all_to_all(packets, ("z", "ylo"), 0, 0, tiled=True)
    planes = [packets]
    for k in range(1, last + 1):
        planes.append(
            copies_call(
                functools.partial(planes_kernel, firsts[k], CHUNKS[k]), "planes",
                (32, CHUNKS[k], width), [tie(place, planes[-1]), *asked], [database, across],
                6 * count,
            )
        )
    own = copies_call(merge_kernel, "merge", shape(0), [tie(wanted, planes[-1])], [arrived], count)
    by_plane = send_planes(planes[1], own)
    near, ends = spread(own)
    key_parts, their_parts, sent_parts, mine, waiting = [], [], [], None, None

    def finish(k, ready, pieces, hops, **begun):
        keys, mine_now, theirs = project(
            ready, pieces, hops, firsts[k] * count, key_weight, mine, **begun
        )
        key_parts.append(keys)
        sent_parts.append(theirs)
        their_parts.append(ring(theirs, "core", 1, 2))
        return mine_now

    for k in range(1, last + 1):
        handed, given = hand(k, by_plane, *(near[1:] if k == 1 else near[1:4]))
        here = by_plane
        if k < last:
            by_plane = send_planes(planes[k + 1], handed)
        far = pass_on(ends)
        if waiting is not None:
            mine = finish(k - 2, tie(place, handed), waiting, near_hops + far_hops)
        waiting = (*near, *far)
        own = merge(k, here, given, *near[4:])
        near, ends = spread(own, *key_parts[-1:])
    mine = finish(last - 1, tie(place, near[3]), waiting, near_hops + far_hops)
    far = pass_on(ends)
    begun, mine, theirs = project(
        tie(place, key_parts[-1]), near, near_hops, firsts[-1] * count, key_weight, mine,
        ends=False,
    )
    mine = finish(last, place, far, far_hops, theirs=theirs, begun=begun)

    chances, gradient = weigh(queries, cotangent, key_parts)
    their_gradient = ring(gradient, "core", 1, 2)
    totals = []
    summed = ()
    for low, high in GROUPS:
        blocks = weight_terms(
            tie(place, *summed), TARGETS[low:high], gradient, mine, their_gradient, their_parts
        )
        summed = blocks[:1]
        for (dz, dy), block in zip(TARGETS[low:high], blocks):
            if (dz, dy) != (0, 0):
                block = lax.ppermute(
                    block, ("z", "ylo"),
                    [
                        (a * 2 + b, (a + dz) % 4 * 2 + (b + dy) % 2)
                        for a in range(4) for b in range(2)
                    ],
                )
            totals.append(block)
    values = project_values(tie(place, *summed, *totals[:GROUPS[0][1]]), mine, sent_parts, value_weight)
    attended, query_grad = attend(cotangent, chances, key_parts, values)
    value_weight_grad = add_blocks([*totals[:-1], tie(totals[-1], attended)])
    return attended, query_grad, value_weight_grad


def solution(mesh):
    inner = Mesh(mesh.devices.reshape(4, 2, 2, 4, 2), (*DB, *MP))
    return jax.shard_map(
        per_device,
        mesh=inner,
        in_specs=(
            P(DB, MP),
            P(DB, None, MP),
            P(DB, None),
            P(DB, None),
            P(None, MP),
            P(None, MP),
            P(DB, MP),
        ),
        out_specs=(P(DB, MP), P(DB, MP), P(DB, MP)),
        check_vma=False,
    )
```

time: 528 us -> 330 us (0.62)
  Pallas kernels: 209 us -> 117 us
  waiting for transfers between devices: 161 us -> 114 us
  starting transfers between devices: 118 us -> 77.3 us
  local copies, waits for them, and re-layouts: 31.5 us -> 18.1 us
  other arithmetic: 6.18 us -> 0.36 us
    pallas_call x30 -> x19, Pallas kernels: 204 us -> 105 us  [the longest x5 36.5 us: project(): pl.pallas_call(functools.partial(project_kernel, hops, first, begun is No...]
    ppermute x46 -> x41, waiting for transfers between devices: 145 us -> 84.2 us  [ring(): lax.ppermute(values, axis, [(i, (i + shift) % size) for i in range(size)])]
    ppermute x46 -> x41, starting transfers between devices: 95.5 us -> 48.3 us  [ring(): lax.ppermute(values, axis, [(i, (i + shift) % size) for i in range(size)])]
    all_to_all x0 -> x4, starting transfers between devices: none -> 17.9 us  [the longest x3 13.5 us: send_planes(): return lax.all_to_all(tie(packets, *after), 'z', 0, 0, tiled=True)]
    slice x9 -> x0, local copies, waits for them, and re-layouts: 14.9 us -> none  [the longest x4 5.91 us: per_device(): far0 = ring(left[0:1], 'x', 1, 4)]
    all_to_all x0 -> x4, waiting for transfers between devices: none -> 14.1 us  [the longest x1 14.1 us: per_device(): arrived = lax.all_to_all(packets, ('z', 'ylo'), 0, 0, tiled=True)]
    ppermute x7, starting transfers between devices: 22.6 us -> 11.2 us  [per_device(): lax.ppermute(block, ('z', 'ylo'), [(a * 2 + b, (a + dz) % 4 * 2 + (b + dy...]
    select_n x4 -> x2, other arithmetic: 5.5 us -> 0.02 us  [per_device(): chips = owners // 2]
  transfers between devices with their start and end apart: 53 -> 52, of which waited for: 17 -> 24; matrix products, arithmetic and copies ran while one was open for 4% -> 1% of each run, Pallas kernels for 36% -> 29%
where the time goes in v2:
time: 330 us; the launch traced here: 328 us
  Pallas kernels  117 us (35%)
  waiting for transfers between devices  114 us (35%)
  starting transfers between devices  77.3 us (23%)
  local copies, waits for them, and re-layouts  18.1 us (5%)
    ppermute x41, waiting for transfers between devices, ring(): lax.ppermute(values, axis, [(i, (i + shift) % size) for i in range(size)])  84.2 us
    ppermute x41, starting transfers between devices, ring(): lax.ppermute(values, axis, [(i, (i + shift) % size) for i in range(size)])  48.3 us
    pallas_call x5, Pallas kernels, project(): pl.pallas_call(functools.partial(project_kernel, hops, first, begun is No...  36.5 us
    pallas_call x11, Pallas kernels, copies_call(): pl.pallas_call(kernel, name=name, out_shape=jax.ShapeDtypeStruct(shape, j...  32.9 us
    pallas_call x2, Pallas kernels, weight_terms(): pl.pallas_call(functools.partial(term_kernel, len(their_parts)), name='te...  19.9 us
    unnamed x84, local copies, waits for them, and re-layouts  17.3 us
    pallas_call x1, Pallas kernels, project_values(): pl.pallas_call(value_kernel, name='values', out_shape=jax.ShapeDtypeStruc...  16.2 us
    ppermute x7, waiting for transfers between devices, per_device(): lax.ppermute(block, ('z', 'ylo'), [(a * 2 + b, (a + dz) % 4 * 2 + (b + dy...  15.5 us
  transfers between devices with their start and end apart: 52, of which 24 were waited for; matrix products, arithmetic and copies ran while one was open for 1% of the time, Pallas kernels for 29%

profile of v2, /device:TPU:6, one launch (start us, length us, event | category | flops | bytes accessed | tf_op | source)
XLA Modules:
  0.0 327.9 jit_solution(7560937538439943156)
XLA Ops:
  6.5 4.1 %collective-permute-start.1 = (s32[2,32]{1,0:T(2,128)S(1)}, s32[2,32]{1,0:T(2,128)S(1)}, u32[]{:S(2)}, u32[]{:S(2)}) collective-permute-start(s32[2,32]{1,0:T(2,128)S(1)} %pad_add_fusion.both), channel_id=1, source_target_pairs={{0,96},{32,0},{64,32},{96,64},{1,97},{33,1},{65,33},{97,65},{2,98}... | collective-permute-start | bytes 776 | tf_op jit(solution)/shard_map/ppermute | solution.py:23
  16.1 3.9 %pack.1 = bf16[32,32,1024]{2,1,0:T(8,128)(2,1)} custom-call(s32[5]{0:T(128)} %stack.23.place, s32[2,32]{1,0:T(2,128)} %copy-done.36, s32[2,32]{1,0:T(2,128)} %copy-done.37, s32[2,32]{1,0:T(2,128)} %copy-done.38, s32[2,32]{1,0:T(2,128)} %copy-done.39, bf16[16,128,1024]{2,1,0:T(8,128)(2,1)} %own.19, bf16[16,128,1024]{2,1,0:T(8,128)(2,1)} %collective-permute-done.4.across), custom_call_target="tpu_custom_call" | custom-call | flops 1 | bytes 1 | tf_op jit(solution)/shard_map/pack/pallas_call | solution.py:116
  20.0 4.4 %all-to-all-start = ((bf16[32,32,1024]{2,1,0:T(8,128)(2,1)}), bf16[32,32,1024]{2,1,0:T(8,128)(2,1)S(1)}, u32[]{:S(2)}, u32[]{:S(2)}) async-start(bf16[32,32,1024]{2,1,0:T(8,128)(2,1)} %pack.1), calls=%async_computation | async-start | bytes 4194304 | tf_op jit(solution)/shard_map/all_to_all | solution.py:519
  24.4 3.6 %planes.3 = bf16[32,32,1024]{2,1,0:T(8,128)(2,1)} custom-call(s32[5]{0:T(128)} %stack.23.place, s32[2,32]{1,0:T(2,128)} %copy-done.37, s32[2,32]{1,0:T(2,128)} %copy-done.38, s32[2,32]{1,0:T(2,128)} %copy-done.39, bf16[16,128,1024]{2,1,0:T(8,128)(2,1)} %own.19, bf16[16,128,1024]{2,1,0:T(8,128)(2,1)} %collective-permute-done.4.across), custom_call_target="tpu_custom_call" | custom-call | flops 1 | bytes 1 | tf_op jit(solution)/shard_map/planes/pallas_call | solution.py:116
  28.0 3.6 %planes.4 = bf16[32,32,1024]{2,1,0:T(8,128)(2,1)} custom-call(s32[5]{0:T(128)} %stack.23.place, s32[2,32]{1,0:T(2,128)} %copy-done.37, s32[2,32]{1,0:T(2,128)} %copy-done.38, s32[2,32]{1,0:T(2,128)} %copy-done.39, bf16[16,128,1024]{2,1,0:T(8,128)(2,1)} %own.19, bf16[16,128,1024]{2,1,0:T(8,128)(2,1)} %collective-permute-done.4.across), custom_call_target="tpu_custom_call" | custom-call | flops 1 | bytes 1 | tf_op jit(solution)/shard_map/planes/pallas_call | solution.py:116
  31.6 3.6 %planes.5 = bf16[32,32,1024]{2,1,0:T(8,128)(2,1)} custom-call(s32[5]{0:T(128)} %stack.23.place, s32[2,32]{1,0:T(2,128)} %copy-done.37, s32[2,32]{1,0:T(2,128)} %copy-done.38, s32[2,32]{1,0:T(2,128)} %copy-done.39, bf16[16,128,1024]{2,1,0:T(8,128)(2,1)} %own.19, bf16[16,128,1024]{2,1,0:T(8,128)(2,1)} %collective-permute-done.4.across), custom_call_target="tpu_custom_call" | custom-call | flops 1 | bytes 1 | tf_op jit(solution)/shard_map/planes/pallas_call | solution.py:116
  35.2 14.1 %all-to-all-done.packets = bf16[32,32,1024]{2,1,0:T(8,128)(2,1)S(1)} async-done(((bf16[32,32,1024]{2,1,0:T(8,128)(2,1)}), bf16[32,32,1024]{2,1,0:T(8,128)(2,1)S(1)}, u32[]{:S(2)}, u32[]{:S(2)}) %all-to-all-start) | async-done | bytes 2097184 | tf_op jit(solution)/shard_map/all_to_all | solution.py:519
  53.3 3.8 %all-to-all-start.1 = ((bf16[32,32,1024]{2,1,0:T(8,128)(2,1)}), bf16[32,32,1024]{2,1,0:T(8,128)(2,1)S(1)}, u32[]{:S(2)}, u32[]{:S(2)}) async-start(bf16[32,32,1024]{2,1,0:T(8,128)(2,1)} %planes.3), calls=%async_computation.1 | async-start | bytes 4194304 | tf_op jit(solution)/shard_map/all_to_all | solution.py:513
  62.0 6.8 %collective-permute-done.5.refs_3_ = bf16[256,1024]{1,0:T(8,128)(2,1)S(1)} collective-permute-done((bf16[256,1024]{1,0:T(8,128)(2,1)S(1)}, bf16[256,1024]{1,0:T(8,128)(2,1)S(1)}, u32[]{:S(2)}, u32[]{:S(2)}) %collective-permute-start.5) | collective-permute-done | bytes 524320 | tf_op jit(solution)/shard_map/ppermute | solution.py:23
  74.3 7.2 %collective-permute-done.8.refs_4_ = bf16[256,1024]{1,0:T(8,128)(2,1)S(1)} collective-permute-done((bf16[256,1024]{1,0:T(8,128)(2,1)S(1)}, bf16[256,1024]{1,0:T(8,128)(2,1)S(1)}, u32[]{:S(2)}, u32[]{:S(2)}) %collective-permute-start.8) | collective-permute-done | bytes 524320 | tf_op jit(solution)/shard_map/ppermute | solution.py:23
  87.2 4.9 %all-to-all-start.2 = ((bf16[32,32,1024]{2,1,0:T(8,128)(2,1)}), bf16[32,32,1024]{2,1,0:T(8,128)(2,1)S(1)}, u32[]{:S(2)}, u32[]{:S(2)}) async-start(bf16[32,32,1024]{2,1,0:T(8,128)(2,1)} %planes.4), calls=%async_computation.2 | async-start | bytes 4194304 | tf_op jit(solution)/shard_map/all_to_all | solution.py:513
  93.4 7.9 %collective-permute-done.10.refs_0_ = bf16[8,32,1024]{2,1,0:T(8,128)(2,1)S(1)} collective-permute-done((bf16[8,32,1024]{2,1,0:T(8,128)(2,1)S(1)}, bf16[8,32,1024]{2,1,0:T(8,128)(2,1)S(1)}, u32[]{:S(2)}, u32[]{:S(2)}) %collective-permute-start.10) | collective-permute-done | bytes 524320 | tf_op jit(solution)/shard_map/ppermute | solution.py:23
  108.0 6.2 %collective-permute-done.11.refs_1_ = bf16[256,1024]{1,0:T(8,128)(2,1)S(1)} collective-permute-done((bf16[256,1024]{1,0:T(8,128)(2,1)}, bf16[256,1024]{1,0:T(8,128)(2,1)S(1)}, u32[]{:S(2)}, u32[]{:S(2)}) %collective-permute-start.11) | collective-permute-done | bytes 524320 | tf_op jit(solution)/shard_map/ppermute | solution.py:23
  121.6 4.9 %all-to-all-start.3 = ((bf16[32,32,1024]{2,1,0:T(8,128)(2,1)}), bf16[32,32,1024]{2,1,0:T(8,128)(2,1)S(1)}, u32[]{:S(2)}, u32[]{:S(2)}) async-start(bf16[32,32,1024]{2,1,0:T(8,128)(2,1)} %planes.5), calls=%async_computation.3 | async-start | bytes 4194304 | tf_op jit(solution)/shard_map/all_to_all | solution.py:513
  133.1 6.1 %collective-permute-done.16.refs_4_ = bf16[256,1024]{1,0:T(8,128)(2,1)S(1)} collective-permute-done((bf16[256,1024]{1,0:T(8,128)(2,1)S(1)}, bf16[256,1024]{1,0:T(8,128)(2,1)S(1)}, u32[]{:S(2)}, u32[]{:S(2)}) %collective-permute-start.16) | collective-permute-done | bytes 524320 | tf_op jit(solution)/shard_map/ppermute | solution.py:23
  139.2 3.4 %collective-permute-done.17.refs_5_ = bf16[256,1024]{1,0:T(8,128)(2,1)S(1)} collective-permute-done((bf16[256,1024]{1,0:T(8,128)(2,1)S(1)}, bf16[256,1024]{1,0:T(8,128)(2,1)S(1)}, u32[]{:S(2)}, u32[]{:S(2)}) %collective-permute-start.17) | collective-permute-done | bytes 524320 | tf_op jit(solution)/shard_map/ppermute | solution.py:23
  152.1 8.2 %project.5 = (bf16[256,512]{1,0:T(8,128)(2,1)}, bf16[8,1024,512]{2,1,0:T(8,128)(2,1)}, bf16[8,256,512]{2,1,0:T(8,128)(2,1)}) custom-call(s32[5]{0:T(128)} %stack.23.place, bf16[256,1024]{1,0:T(8,128)(2,1)} %bitcast.22, bf16[256,1024]{1,0:T(8,128)(2,1)} %copy-done.13, bf16[256,1024]{1,0:T(8,128)(2,1)} %copy-done.14, bf16[256,1024]{1,0:T(8,128)(2,1)} %copy-done.12, ...), custom_call_target="tpu_custom_call" | custom-call | flops 1 | bytes 1 | tf_op jit(solution)/shard_map/project/pallas_call | solution.py:197
  175.6 7.8 %collective-permute-done.26.refs_0_ = bf16[8,32,1024]{2,1,0:T(8,128)(2,1)S(1)} collective-permute-done((bf16[8,32,1024]{2,1,0:T(8,128)(2,1)}, bf16[8,32,1024]{2,1,0:T(8,128)(2,1)S(1)}, u32[]{:S(2)}, u32[]{:S(2)}) %collective-permute-start.26) | collective-permute-done | bytes 524320 | tf_op jit(solution)/shard_map/ppermute | solution.py:23
  191.7 8.2 %project.6 = (bf16[256,512]{1,0:T(8,128)(2,1)}, bf16[8,1024,512]{2,1,0:T(8,128)(2,1)}, bf16[8,256,512]{2,1,0:T(8,128)(2,1)}) custom-call(s32[5]{0:T(128)} %stack.23.place, bf16[256,1024]{1,0:T(8,128)(2,1)} %bitcast.13, bf16[256,1024]{1,0:T(8,128)(2,1)} %copy-done.7, bf16[256,1024]{1,0:T(8,128)(2,1)} %copy-done.9, ...), custom_call_target="tpu_custom_call", output_to_operand_aliasing={{1}: (10, {})} | custom-call | flops 1 | bytes 1 | tf_op jit(solution)/shard_map/project/pallas_call | solution.py:197
  199.9 3.6 %collective-permute-done.30.refs_1_ = bf16[256,1024]{1,0:T(8,128)(2,1)} collective-permute-done((bf16[256,1024]{1,0:T(8,128)(2,1)}, bf16[256,1024]{1,0:T(8,128)(2,1)}, u32[]{:S(2)}, u32[]{:S(2)}) %collective-permute-start.30) | collective-permute-done | bytes 524320 | tf_op jit(solution)/shard_map/ppermute | solution.py:23
  213.5 7.1 %collective-permute-done.33.refs_5_ = bf16[256,1024]{1,0:T(8,128)(2,1)S(1)} collective-permute-done((bf16[256,1024]{1,0:T(8,128)(2,1)S(1)}, bf16[256,1024]{1,0:T(8,128)(2,1)S(1)}, u32[]{:S(2)}, u32[]{:S(2)}) %collective-permute-start.33) | collective-permute-done | bytes 524320 | tf_op jit(solution)/shard_map/ppermute | solution.py:23
  221.5 4.8 %collective-permute-done.29.refs_7_ = bf16[256,1024]{1,0:T(8,128)(2,1)} collective-permute-done((bf16[256,1024]{1,0:T(8,128)(2,1)}, bf16[256,1024]{1,0:T(8,128)(2,1)}, u32[]{:S(2)}, u32[]{:S(2)}) %collective-permute-start.29) | collective-permute-done | bytes 524320 | tf_op jit(solution)/shard_map/ppermute | solution.py:23
  226.4 8.2 %project.7 = (bf16[256,512]{1,0:T(8,128)(2,1)}, bf16[8,1024,512]{2,1,0:T(8,128)(2,1)}, bf16[8,256,512]{2,1,0:T(8,128)(2,1)}) custom-call(s32[5]{0:T(128)} %stack.23.place, bf16[256,1024]{1,0:T(8,128)(2,1)} %bitcast.17, bf16[256,1024]{1,0:T(8,128)(2,1)} %copy-done.8, bf16[256,1024]{1,0:T(8,128)(2,1)} %copy-done.10, ...), custom_call_target="tpu_custom_call", output_to_operand_aliasing={{1}: (10, {})} | custom-call | flops 1 | bytes 1 | tf_op jit(solution)/shard_map/project/pallas_call | solution.py:197
  235.4 6.7 %project.8 = (f32[256,512]{1,0:T(8,128)}, bf16[8,1024,512]{2,1,0:T(8,128)(2,1)}, bf16[8,256,512]{2,1,0:T(8,128)(2,1)}) custom-call(s32[5]{0:T(128)} %stack.23.place, bf16[256,1024]{1,0:T(8,128)(2,1)} %bitcast.21, bf16[256,1024]{1,0:T(8,128)(2,1)} %collective-permute-done.30.refs_1_, bf16[256,1024]{1,0:T(8,128)(2,1)} %copy-done.20, ...), custom_call_target="tpu_custom_call", output_to_operand_aliasing={{1}: (8, {})} | custom-call | flops 1 | bytes 1 | tf_op jit(solution)/shard_map/project/pallas_call | solution.py:197
  242.1 5.2 %project.9 = (bf16[256,512]{1,0:T(8,128)(2,1)}, bf16[8,1024,512]{2,1,0:T(8,128)(2,1)}, bf16[8,256,512]{2,1,0:T(8,128)(2,1)}) custom-call(s32[5]{0:T(128)} %stack.23.place, bf16[256,1024]{1,0:T(8,128)(2,1)} %collective-permute-done.31.refs_0_, bf16[256,1024]{1,0:T(8,128)(2,1)} %collective-permute-done.34.refs_1_, ...), custom_call_target="tpu_custom_call", output_to_operand_aliasing={{1}: (5, {}), {2}: (6, {})} | custom-call | flops 1 | bytes 1 | tf_op jit(solution)/shard_map/project/pallas_call | solution.py:197
  247.4 4.4 %weigh.1 = (f32[16,64,256]{2,1,0:T(8,128)}, bf16[512,1024]{1,0:T(8,128)(2,1)}) custom-call(bf16[256,512]{1,0:T(8,128)(2,1)} %refs_0_.2, bf16[256,512]{1,0:T(8,128)(2,1)} %refs_0_.3, bf16[256,512]{1,0:T(8,128)(2,1)} %get-tuple-element.65.refs_2_.refs_3_, bf16[256,512]{1,0:T(8,128)(2,1)} %get-tuple-element.72.refs_3_.refs_4_, ...), custom_call_target="tpu_custom_call" | custom-call | flops 1 | bytes 1 | tf_op jit(solution)/shard_map/weigh/pallas_call | solution.py:327
  255.7 6.6 %terms.2 = (bf16[512,512]{1,0:T(8,128)(2,1)}, bf16[512,512]{1,0:T(8,128)(2,1)}) custom-call(s32[5]{0:T(128)} %stack.23.place, bf16[512,1024]{1,0:T(8,128)(2,1)} %get-tuple-element.86.gradient, bf16[8,1024,512]{2,1,0:T(8,128)(2,1)} %get-tuple-element.87.mine, bf16[512,1024]{1,0:T(8,128)(2,1)} %copy-done.5, bf16[8,256,512]{2,1,0:T(8,128)(2,1)} %copy-done.4, ...), custom_call_target="tpu_custom_call" | custom-call | flops 1 | bytes 1 | tf_op jit(solution)/shard_map/terms/pallas_call | solution.py:422
  265.6 13.3 %terms.3 = (bf16[512,512]{1,0:T(8,128)(2,1)}, bf16[512,512]{1,0:T(8,128)(2,1)}, bf16[512,512]{1,0:T(8,128)(2,1)}, bf16[512,512]{1,0:T(8,128)(2,1)}, bf16[512,512]{1,0:T(8,128)(2,1)}, /*index=5*/bf16[512,512]{1,0:T(8,128)(2,1)}) custom-call(s32[5]{0:T(128)} %stack.23.place, bf16[512,1024]{1,0:T(8,128)(2,1)} %get-tuple-element.86.gradient, ...), custom_call_target="tpu_custom_call" | custom-call | flops 1 | bytes 1 | tf_op jit(solution)/shard_map/terms/pallas_call | solution.py:422
  286.3 15.5 %collective-permute-done.42.refs_1_ = bf16[512,512]{1,0:T(8,128)(2,1)S(1)} collective-permute-done((bf16[512,512]{1,0:T(8,128)(2,1)}, bf16[512,512]{1,0:T(8,128)(2,1)S(1)}, u32[]{:S(2)}, u32[]{:S(2)}) %collective-permute-start.42) | collective-permute-done | bytes 524320 | tf_op jit(solution)/shard_map/ppermute | solution.py:573
  302.3 16.2 %values.1.refs_2_ = bf16[1024,512]{1,0:T(8,128)(2,1)} custom-call(s32[5]{0:T(128)} %stack.23.place, bf16[8,1024,512]{2,1,0:T(8,128)(2,1)} %get-tuple-element.87.mine, bf16[8,256,512]{2,1,0:T(8,128)(2,1)} %get-tuple-element.88.refs_0_, bf16[8,256,512]{2,1,0:T(8,128)(2,1)} %get-tuple-element.89.refs_1_, bf16[8,256,512]{2,1,0:T(8,128)(2,1)} %get-tuple-element.90.refs_2_, ...), custom_call_target="tpu_custom_call" | custom-call | flops 1 | bytes 1 | tf_op jit(solution)/shard_map/values/pallas_call | solution.py:253
  318.5 3.6 %attend.1 = (bf16[256,512]{1,0:T(8,128)(2,1)}, bf16[256,512]{1,0:T(8,128)(2,1)}) custom-call(bf16[256,512]{1,0:T(8,128)(2,1)} %refs_0_.3, f32[16,64,256]{2,1,0:T(8,128)} %get-tuple-element.85.refs_1_, bf16[1024,512]{1,0:T(8,128)(2,1)} %values.1.refs_2_, bf16[256,512]{1,0:T(8,128)(2,1)} %get-tuple-element.65.refs_2_.refs_3_, ...), custom_call_target="tpu_custom_call" | custom-call | flops 1 | bytes 1 | tf_op jit(solution)/shard_map/attend/pallas_call | solution.py:374
  324.2 3.7 %total.1 = f32[512,512]{1,0:T(8,128)} custom-call(bf16[512,512]{1,0:T(8,128)(2,1)} %copy-done.21, bf16[512,512]{1,0:T(8,128)(2,1)} %copy-done.22, bf16[512,512]{1,0:T(8,128)(2,1)} %copy-done.24, bf16[512,512]{1,0:T(8,128)(2,1)} %copy-done.25, bf16[512,512]{1,0:T(8,128)(2,1)} %copy-done.26, bf16[512,512]{1,0:T(8,128)(2,1)} %copy-done.27, ...), custom_call_target="tpu_custom_call" | custom-call | flops 1 | bytes 1 | tf_op jit(solution)/shard_map/total/pallas_call | solution.py:449
  (187 shorter events, 115.4 us)
Async XLA Ops:
  0.6 15.0 %collective-permute-start.4 = (bf16[16,128,1024]{2,1,0:T(8,128)(2,1)}, bf16[16,128,1024]{2,1,0:T(8,128)(2,1)}, u32[]{:S(2)}, u32[]{:S(2)}) collective-permute-start(bf16[16,128,1024]{2,1,0:T(8,128)(2,1)} %own.19), channel_id=1, source_target_pairs={{0,8},{8,0},{1,9},{9,1},{2,10},{10,2},{3,11},{11,3},{4,12},{12,4},... | collective-permute-start | bytes 12582920 | tf_op jit(solution)/shard_map/ppermute | solution.py:23
  20.0 29.3 %all-to-all-start = ((bf16[32,32,1024]{2,1,0:T(8,128)(2,1)}), bf16[32,32,1024]{2,1,0:T(8,128)(2,1)S(1)}, u32[]{:S(2)}, u32[]{:S(2)}) async-start(bf16[32,32,1024]{2,1,0:T(8,128)(2,1)} %pack.1), calls=%async_computation | async-start | bytes 4194304 | tf_op jit(solution)/shard_map/all_to_all | solution.py:519
  53.3 30.1 %all-to-all-start.1 = ((bf16[32,32,1024]{2,1,0:T(8,128)(2,1)}), bf16[32,32,1024]{2,1,0:T(8,128)(2,1)S(1)}, u32[]{:S(2)}, u32[]{:S(2)}) async-start(bf16[32,32,1024]{2,1,0:T(8,128)(2,1)} %planes.3), calls=%async_computation.1 | async-start | bytes 4194304 | tf_op jit(solution)/shard_map/all_to_all | solution.py:513
  87.2 30.5 %all-to-all-start.2 = ((bf16[32,32,1024]{2,1,0:T(8,128)(2,1)}), bf16[32,32,1024]{2,1,0:T(8,128)(2,1)S(1)}, u32[]{:S(2)}, u32[]{:S(2)}) async-start(bf16[32,32,1024]{2,1,0:T(8,128)(2,1)} %planes.4), calls=%async_computation.2 | async-start | bytes 4194304 | tf_op jit(solution)/shard_map/all_to_all | solution.py:513
  121.6 42.6 %all-to-all-start.3 = ((bf16[32,32,1024]{2,1,0:T(8,128)(2,1)}), bf16[32,32,1024]{2,1,0:T(8,128)(2,1)S(1)}, u32[]{:S(2)}, u32[]{:S(2)}) async-start(bf16[32,32,1024]{2,1,0:T(8,128)(2,1)} %planes.5), calls=%async_computation.3 | async-start | bytes 4194304 | tf_op jit(solution)/shard_map/all_to_all | solution.py:513
  128.4 14.3 %collective-permute-start.17 = (bf16[256,1024]{1,0:T(8,128)(2,1)S(1)}, bf16[256,1024]{1,0:T(8,128)(2,1)S(1)}, u32[]{:S(2)}, u32[]{:S(2)}) collective-permute-start(bf16[256,1024]{1,0:T(8,128)(2,1)S(1)} %collective-permute-done.13.refs_3_), channel_id=1, source_target_pairs={{0,6},{2,0},{4,2},{6,4},{1,7},{3,1},{5,3},{7,5},{8,14},{10,8},{12,... | collective-permute-start | bytes 1572872 | tf_op jit(solution)/shard_map/ppermute | solution.py:23
  128.5 15.0 %collective-permute-start.18 = (bf16[8,32,1024]{2,1,0:T(8,128)(2,1)}, bf16[8,32,1024]{2,1,0:T(8,128)(2,1)S(1)}, u32[]{:S(2)}, u32[]{:S(2)}) collective-permute-start(bf16[8,32,1024]{2,1,0:T(8,128)(2,1)} %hand.4), channel_id=1, source_target_pairs={{0,16},{16,0},{1,17},{17,1},{2,18},{18,2},{3,19},{19,3},{4,20},{20... | collective-permute-start | bytes 1572872 | tf_op jit(solution)/shard_map/ppermute | solution.py:23
  129.9 21.2 %collective-permute-start.14 = (bf16[256,1024]{1,0:T(8,128)(2,1)}, bf16[256,1024]{1,0:T(8,128)(2,1)}, u32[]{:S(2)}, u32[]{:S(2)}) collective-permute-start(bf16[256,1024]{1,0:T(8,128)(2,1)} %copy-done.13), channel_id=1, source_target_pairs={{0,2},{2,4},{4,6},{6,0},{1,3},{3,5},{5,7},{7,1},{8,10},{10,12},{12... | collective-permute-start | bytes 1572872 | tf_op jit(solution)/shard_map/ppermute | solution.py:23
  133.1 19.0 %collective-permute-start.15 = (bf16[256,1024]{1,0:T(8,128)(2,1)}, bf16[256,1024]{1,0:T(8,128)(2,1)}, u32[]{:S(2)}, u32[]{:S(2)}) collective-permute-start(bf16[256,1024]{1,0:T(8,128)(2,1)} %collective-permute-done.9.refs_5_), channel_id=1, source_target_pairs={{0,6},{2,0},{4,2},{6,4},{1,7},{3,1},{5,3},{7,5},{8,14},{10,8},{12,... | collective-permute-start | bytes 1572872 | tf_op jit(solution)/shard_map/ppermute | solution.py:23
  146.9 13.4 %collective-permute-start.19 = (bf16[256,1024]{1,0:T(8,128)(2,1)}, bf16[256,1024]{1,0:T(8,128)(2,1)S(1)}, u32[]{:S(2)}, u32[]{:S(2)}) collective-permute-start(bf16[256,1024]{1,0:T(8,128)(2,1)} %bitcast.14), channel_id=1, source_target_pairs={{0,2},{2,4},{4,6},{6,0},{1,3},{3,5},{5,7},{7,1},{8,10},{10,12},{12... | collective-permute-start | bytes 1572872 | tf_op jit(solution)/shard_map/ppermute | solution.py:23
  148.1 14.1 %collective-permute-start.20 = (bf16[256,1024]{1,0:T(8,128)(2,1)}, bf16[256,1024]{1,0:T(8,128)(2,1)S(1)}, u32[]{:S(2)}, u32[]{:S(2)}) collective-permute-start(bf16[256,1024]{1,0:T(8,128)(2,1)} %bitcast.15), channel_id=1, source_target_pairs={{0,6},{2,0},{4,2},{6,4},{1,7},{3,1},{5,3},{7,5},{8,14},{10,8},{12,... | collective-permute-start | bytes 1572872 | tf_op jit(solution)/shard_map/ppermute | solution.py:23
  168.2 15.2 %collective-permute-start.26 = (bf16[8,32,1024]{2,1,0:T(8,128)(2,1)}, bf16[8,32,1024]{2,1,0:T(8,128)(2,1)S(1)}, u32[]{:S(2)}, u32[]{:S(2)}) collective-permute-start(bf16[8,32,1024]{2,1,0:T(8,128)(2,1)} %hand.5), channel_id=1, source_target_pairs={{0,16},{16,0},{1,17},{17,1},{2,18},{18,2},{3,19},{19,3},{4,20},{20... | collective-permute-start | bytes 1572872 | tf_op jit(solution)/shard_map/ppermute | solution.py:23
  171.0 19.7 %collective-permute-start.22 = (bf16[256,1024]{1,0:T(8,128)(2,1)S(1)}, bf16[256,1024]{1,0:T(8,128)(2,1)S(1)}, u32[]{:S(2)}, u32[]{:S(2)}) collective-permute-start(bf16[256,1024]{1,0:T(8,128)(2,1)S(1)} %collective-permute-done.11.refs_1_), channel_id=1, source_target_pairs={{0,2},{2,4},{4,6},{6,0},{1,3},{3,5},{5,7},{7,1},{8,10},{10,12},{12... | collective-permute-start | bytes 1572872 | tf_op jit(solution)/shard_map/ppermute | solution.py:23
  173.6 17.1 %collective-permute-start.23 = (bf16[256,1024]{1,0:T(8,128)(2,1)S(1)}, bf16[256,1024]{1,0:T(8,128)(2,1)S(1)}, u32[]{:S(2)}, u32[]{:S(2)}) collective-permute-start(bf16[256,1024]{1,0:T(8,128)(2,1)S(1)} %copy-done.17), channel_id=1, source_target_pairs={{0,6},{2,0},{4,2},{6,4},{1,7},{3,1},{5,3},{7,5},{8,14},{10,8},{12,... | collective-permute-start | bytes 1572872 | tf_op jit(solution)/shard_map/ppermute | solution.py:23
  188.5 15.1 %collective-permute-start.30 = (bf16[256,1024]{1,0:T(8,128)(2,1)}, bf16[256,1024]{1,0:T(8,128)(2,1)}, u32[]{:S(2)}, u32[]{:S(2)}) collective-permute-start(bf16[256,1024]{1,0:T(8,128)(2,1)} %bitcast.19), channel_id=1, source_target_pairs={{0,2},{2,4},{4,6},{6,0},{1,3},{3,5},{5,7},{7,1},{8,10},{10,12},{12... | collective-permute-start | bytes 1572872 | tf_op jit(solution)/shard_map/ppermute | solution.py:23
  190.7 16.3 %collective-permute-start.32 = (bf16[256,1024]{1,0:T(8,128)(2,1)}, bf16[256,1024]{1,0:T(8,128)(2,1)S(1)}, u32[]{:S(2)}, u32[]{:S(2)}) collective-permute-start(bf16[256,1024]{1,0:T(8,128)(2,1)} %bitcast.20), channel_id=1, source_target_pairs={{0,6},{2,0},{4,2},{6,4},{1,7},{3,1},{5,3},{7,5},{8,14},{10,8},{12,... | collective-permute-start | bytes 1572872 | tf_op jit(solution)/shard_map/ppermute | solution.py:23
  207.0 13.6 %collective-permute-start.33 = (bf16[256,1024]{1,0:T(8,128)(2,1)S(1)}, bf16[256,1024]{1,0:T(8,128)(2,1)S(1)}, u32[]{:S(2)}, u32[]{:S(2)}) collective-permute-start(bf16[256,1024]{1,0:T(8,128)(2,1)S(1)} %collective-permute-done.27.refs_3_), channel_id=1, source_target_pairs={{0,6},{2,0},{4,2},{6,4},{1,7},{3,1},{5,3},{7,5},{8,14},{10,8},{12,... | collective-permute-start | bytes 1572872 | tf_op jit(solution)/shard_map/ppermute | solution.py:23
  207.0 13.6 %collective-permute-start.28 = (bf16[256,1024]{1,0:T(8,128)(2,1)S(1)}, bf16[256,1024]{1,0:T(8,128)(2,1)S(1)}, u32[]{:S(2)}, u32[]{:S(2)}) collective-permute-start(bf16[256,1024]{1,0:T(8,128)(2,1)S(1)} %collective-permute-done.19.refs_1_), channel_id=1, source_target_pairs={{0,2},{2,4},{4,6},{6,0},{1,3},{3,5},{5,7},{7,1},{8,10},{10,12},{12... | collective-permute-start | bytes 1572872 | tf_op jit(solution)/shard_map/ppermute | solution.py:23
  210.2 16.1 %collective-permute-start.29 = (bf16[256,1024]{1,0:T(8,128)(2,1)}, bf16[256,1024]{1,0:T(8,128)(2,1)}, u32[]{:S(2)}, u32[]{:S(2)}) collective-permute-start(bf16[256,1024]{1,0:T(8,128)(2,1)} %collective-permute-done.25.refs_5_), channel_id=1, source_target_pairs={{0,6},{2,0},{4,2},{6,4},{1,7},{3,1},{5,3},{7,5},{8,14},{10,8},{12,... | collective-permute-start | bytes 1572872 | tf_op jit(solution)/shard_map/ppermute | solution.py:23
  210.3 24.4 %collective-permute-start.35 = (bf16[256,1024]{1,0:T(8,128)(2,1)S(1)}, bf16[256,1024]{1,0:T(8,128)(2,1)}, u32[]{:S(2)}, u32[]{:S(2)}) collective-permute-start(bf16[256,1024]{1,0:T(8,128)(2,1)S(1)} %collective-permute-done.27.refs_3_), channel_id=1, source_target_pairs={{0,2},{2,4},{4,6},{6,0},{1,3},{3,5},{5,7},{7,1},{8,10},{10,12},{12... | collective-permute-start | bytes 1572872 | tf_op jit(solution)/shard_map/ppermute | solution.py:23
  213.5 28.6 %collective-permute-start.31 = (bf16[256,1024]{1,0:T(8,128)(2,1)}, bf16[256,1024]{1,0:T(8,128)(2,1)}, u32[]{:S(2)}, u32[]{:S(2)}) collective-permute-start(bf16[256,1024]{1,0:T(8,128)(2,1)} %collective-permute-done.30.refs_1_), channel_id=1, source_target_pairs={{0,2},{2,4},{4,6},{6,0},{1,3},{3,5},{5,7},{7,1},{8,10},{10,12},{12... | collective-permute-start | bytes 1572872 | tf_op jit(solution)/shard_map/ppermute | solution.py:23
  220.6 21.5 %collective-permute-start.34 = (bf16[256,1024]{1,0:T(8,128)(2,1)S(1)}, bf16[256,1024]{1,0:T(8,128)(2,1)}, u32[]{:S(2)}, u32[]{:S(2)}) collective-permute-start(bf16[256,1024]{1,0:T(8,128)(2,1)S(1)} %collective-permute-done.33.refs_5_), channel_id=1, source_target_pairs={{0,6},{2,0},{4,2},{6,4},{1,7},{3,1},{5,3},{7,5},{8,14},{10,8},{12,... | collective-permute-start | bytes 1572872 | tf_op jit(solution)/shard_map/ppermute | solution.py:23
  221.5 30.7 %collective-permute-start.37 = (bf16[8,256,512]{2,1,0:T(8,128)(2,1)}, bf16[8,256,512]{2,1,0:T(8,128)(2,1)S(1)}, u32[]{:S(2)}, u32[]{:S(2)}) collective-permute-start(bf16[8,256,512]{2,1,0:T(8,128)(2,1)} %get-tuple-element.88.refs_0_), channel_id=1, source_target_pairs={{0,8},{8,0},{1,9},{9,1},{2,10},{10,2},{3,11},{11,3},{4,12},{12,4},... | collective-permute-start | bytes 6291464 | tf_op jit(solution)/shard_map/ppermute | solution.py:23
  226.4 25.9 %collective-permute-start.38 = (bf16[8,256,512]{2,1,0:T(8,128)(2,1)}, bf16[8,256,512]{2,1,0:T(8,128)(2,1)}, u32[]{:S(2)}, u32[]{:S(2)}) collective-permute-start(bf16[8,256,512]{2,1,0:T(8,128)(2,1)} %get-tuple-element.89.refs_1_), channel_id=1, source_target_pairs={{0,8},{8,0},{1,9},{9,1},{2,10},{10,2},{3,11},{11,3},{4,12},{12,4},... | collective-permute-start | bytes 6291464 | tf_op jit(solution)/shard_map/ppermute | solution.py:23
  234.6 17.6 %collective-permute-start.39 = (bf16[8,256,512]{2,1,0:T(8,128)(2,1)}, bf16[8,256,512]{2,1,0:T(8,128)(2,1)}, u32[]{:S(2)}, u32[]{:S(2)}) collective-permute-start(bf16[8,256,512]{2,1,0:T(8,128)(2,1)} %get-tuple-element.90.refs_2_), channel_id=1, source_target_pairs={{0,8},{8,0},{1,9},{9,1},{2,10},{10,2},{3,11},{11,3},{4,12},{12,4},... | collective-permute-start | bytes 6291464 | tf_op jit(solution)/shard_map/ppermute | solution.py:23
  262.3 20.9 %collective-permute-start.41 = (bf16[512,512]{1,0:T(8,128)(2,1)}, bf16[512,512]{1,0:T(8,128)(2,1)S(1)}, u32[]{:S(2)}, u32[]{:S(2)}) collective-permute-start(bf16[512,512]{1,0:T(8,128)(2,1)} %get-tuple-element.92), channel_id=1, source_target_pairs={{0,80},{16,64},{32,112},{48,96},{64,16},{80,0},{96,48},{112,32},{1... | collective-permute-start | bytes 1572872 | tf_op jit(solution)/shard_map/ppermute | solution.py:573
  264.2 37.5 %collective-permute-start.42 = (bf16[512,512]{1,0:T(8,128)(2,1)}, bf16[512,512]{1,0:T(8,128)(2,1)S(1)}, u32[]{:S(2)}, u32[]{:S(2)}) collective-permute-start(bf16[512,512]{1,0:T(8,128)(2,1)} %get-tuple-element.95), channel_id=1, source_target_pairs={{0,64},{16,80},{32,96},{48,112},{64,0},{80,16},{96,32},{112,48},{1... | collective-permute-start | bytes 1572872 | tf_op jit(solution)/shard_map/ppermute | solution.py:573
  278.9 43.2 %collective-permute-start.43 = (bf16[512,512]{1,0:T(8,128)(2,1)}, bf16[512,512]{1,0:T(8,128)(2,1)S(1)}, u32[]{:S(2)}, u32[]{:S(2)}) collective-permute-start(bf16[512,512]{1,0:T(8,128)(2,1)} %get-tuple-element.94), channel_id=1, source_target_pairs={{0,48},{16,32},{32,80},{48,64},{64,112},{80,96},{96,16},{112,0},{1... | collective-permute-start | bytes 1572872 | tf_op jit(solution)/shard_map/ppermute | solution.py:573
  282.0 40.1 %collective-permute-start.44 = (bf16[512,512]{1,0:T(8,128)(2,1)}, bf16[512,512]{1,0:T(8,128)(2,1)S(1)}, u32[]{:S(2)}, u32[]{:S(2)}) collective-permute-start(bf16[512,512]{1,0:T(8,128)(2,1)} %get-tuple-element.99), channel_id=1, source_target_pairs={{0,112},{16,96},{32,16},{48,0},{64,48},{80,32},{96,80},{112,64},{1... | collective-permute-start | bytes 1572872 | tf_op jit(solution)/shard_map/ppermute | solution.py:573
  283.0 39.1 %collective-permute-start.45 = (bf16[512,512]{1,0:T(8,128)(2,1)}, bf16[512,512]{1,0:T(8,128)(2,1)S(1)}, u32[]{:S(2)}, u32[]{:S(2)}) collective-permute-start(bf16[512,512]{1,0:T(8,128)(2,1)} %get-tuple-element.100), channel_id=1, source_target_pairs={{0,32},{16,48},{32,64},{48,80},{64,96},{80,112},{96,0},{112,16},{1... | collective-permute-start | bytes 1572872 | tf_op jit(solution)/shard_map/ppermute | solution.py:573
  283.2 38.9 %collective-permute-start.46 = (bf16[512,512]{1,0:T(8,128)(2,1)}, bf16[512,512]{1,0:T(8,128)(2,1)S(1)}, u32[]{:S(2)}, u32[]{:S(2)}) collective-permute-start(bf16[512,512]{1,0:T(8,128)(2,1)} %get-tuple-element.101), channel_id=1, source_target_pairs={{0,96},{16,112},{32,0},{48,16},{64,32},{80,48},{96,64},{112,80},{1... | collective-permute-start | bytes 1572872 | tf_op jit(solution)/shard_map/ppermute | solution.py:573
  301.7 20.4 %collective-permute-start.47 = (bf16[512,512]{1,0:T(8,128)(2,1)}, bf16[512,512]{1,0:T(8,128)(2,1)S(1)}, u32[]{:S(2)}, u32[]{:S(2)}) collective-permute-start(bf16[512,512]{1,0:T(8,128)(2,1)} %get-tuple-element.102), channel_id=1, source_target_pairs={{0,16},{16,0},{32,48},{48,32},{64,80},{80,64},{96,112},{112,96},{1... | collective-permute-start | bytes 1572872 | tf_op jit(solution)/shard_map/ppermute | solution.py:573
  (61 other events, 520.9 us)

commit v3 on v2

--- a/solution.py
+++ b/solution.py
@@ -10,13 +10,11 @@
 
 HEAD_DIM = 128
 SPAN_LEN = 64
-CHUNKS = (32, 32, 32, 32)
+CHUNKS = (64, 64)
 DB = ("z", "ylo", "core")
 MP = ("x", "yhi")
 VMEM_LIMIT = 60 * 1024 * 1024
 SMALL = pl.CostEstimate(flops=1, bytes_accessed=1, transcendentals=0)
-GROUPS = ((0, 2), (2, 8))
-TARGETS = ((2, 1), (2, 0), (1, 1), (3, 1), (1, 0), (3, 0), (0, 1), (0, 0))
 
 
 def ring(values, axis, shift, size):
@@ -129,14 +127,16 @@
     )(*scalars, *arrays)
 
 
-def project_kernel(hops, first, starts, ends, joins, place, *refs):
+def project_kernel(hops, first, starts, ends, joins, valued, place, *refs):
     count = len(hops)
-    pieces, key_weight = refs[:count], refs[count]
-    refs = refs[count + 1:]
+    pieces, matrices = refs[:count], refs[count:count + 1 + valued]
+    refs = refs[count + 1 + valued:]
     if not starts:
-        begun, refs = refs[0], refs[1:]
+        begun, refs = refs[:1 + valued], refs[1 + valued:]
     refs = refs[sum(joins):]
-    keys, mine, theirs, held, weights, piece_sems, weight_sems, mine_sems, their_sems = refs
+    keys, mine, theirs, refs = refs[0], refs[1], refs[2], refs[3:]
+    results = (keys, *refs[:valued])
+    held, weights, piece_sems, weight_sems, mine_sems, their_sems = refs[valued:]
     rows, depth = pieces[0].shape
     half = depth // 2
     columns = [
@@ -144,12 +144,13 @@
     ]
     piece_reads, weight_reads, writes = [], [], []
     for n, (hop, side) in enumerate(hops):
-        at = (place[3] + hop) % 4 * 2 + (place[4] + side) % 2
+        at = (place[3] + hop * (2 * place[2] - 1) + 4) % 4 * 2 + (place[4] + side) % 2
         cut = pl.ds(pl.multiple_of(at * depth, depth), depth)
         piece_reads.append(pltpu.make_async_copy(pieces[n], held.at[n], piece_sems.at[n]))
-        weight_reads.append(
-            pltpu.make_async_copy(key_weight.at[cut], weights.at[n], weight_sems.at[n])
-        )
+        weight_reads.append([
+            pltpu.make_async_copy(matrix.at[cut], weights.at[m, n], weight_sems.at[m, n])
+            for m, matrix in enumerate(matrices)
+        ])
         writes.append((
             pltpu.make_async_copy(
                 held.at[n, :, columns[0]], mine.at[at, pl.ds(first, rows)], mine_sems.at[n]
@@ -160,115 +161,72 @@
         ))
     for n in range(count):
         piece_reads[n].start()
-        weight_reads[n].start()
-    total = None if starts else begun[...]
+        for copy in weight_reads[n]:
+            copy.start()
+    totals = [None] * len(matrices) if starts else [sums[...] for sums in begun]
     for n in range(count):
         piece_reads[n].wait()
         for copy in writes[n]:
             copy.start()
-        weight_reads[n].wait()
-        part = jnp.dot(held[n], weights[n], preferred_element_type=jnp.float32)
-        total = part if total is None else total + part
-    keys[...] = total.astype(keys.dtype)
+        for m in range(len(matrices)):
+            weight_reads[n][m].wait()
+            part = jnp.dot(held[n], weights[m, n], preferred_element_type=jnp.float32)
+            totals[m] = part if totals[m] is None else totals[m] + part
+    for result, total in zip(results, totals):
+        result[...] = total.astype(result.dtype)
     for pair in writes:
         for copy in pair:
             copy.wait()
 
 
-def project(place, pieces, hops, first, key_weight, mine=None, theirs=None, begun=None, ends=True):
+def project(place, pieces, hops, first, matrices, mine=None, theirs=None, begun=None, ends=True):
     rows, depth = pieces[0].shape
-    width = key_weight.shape[1]
+    width = matrices[0].shape[1]
     count = len(pieces)
+    valued = len(matrices) - 1
     whole = pl.BlockSpec((rows, width), lambda step, place: (0, 0))
     anywhere = pl.BlockSpec(memory_space=pl.ANY)
     kind = jnp.bfloat16 if ends else jnp.float32
-    operands = [place, *pieces, key_weight]
-    in_specs = [anywhere] * (count + 1)
+    operands = [place, *pieces, *matrices]
+    in_specs = [anywhere] * (count + 1 + valued)
     aliases = {}
     if begun is not None:
-        operands.append(begun)
-        in_specs.append(whole)
+        operands.extend(begun)
+        in_specs.extend([whole] * len(begun))
     for n, joined in enumerate((mine, theirs)):
         if joined is not None:
             operands.append(joined)
             in_specs.append(anywhere)
             aliases[len(operands) - 1] = n + 1
     sems = pltpu.SemaphoreType.DMA((count,))
+    result = jax.ShapeDtypeStruct((rows, width), kind)
     return pl.pallas_call(
         functools.partial(
             project_kernel, hops, first, begun is None, ends,
-            (mine is not None, theirs is not None),
+            (mine is not None, theirs is not None), valued,
         ),
         name="project",
         out_shape=(
-            jax.ShapeDtypeStruct((rows, width), kind),
+            result,
             jax.ShapeDtypeStruct((8, 8 * sum(CHUNKS), depth // 2), jnp.bfloat16),
             jax.ShapeDtypeStruct((8, rows, depth // 2), jnp.bfloat16),
+            *[result] * valued,
         ),
         grid_spec=pltpu.PrefetchScalarGridSpec(
             num_scalar_prefetch=1,
             grid=(1,),
             in_specs=in_specs,
-            out_specs=(whole, anywhere, anywhere),
+            out_specs=(whole, anywhere, anywhere, *[whole] * valued),
             scratch_shapes=[
                 pltpu.VMEM((count, rows, depth), jnp.bfloat16),
-                pltpu.VMEM((count, depth, width), jnp.bfloat16),
-                sems, sems, sems, sems,
+                pltpu.VMEM((1 + valued, count, depth, width), jnp.bfloat16),
+                sems, pltpu.SemaphoreType.DMA((1 + valued, count)), sems, sems,
             ],
         ),
         input_output_aliases=aliases,
         compiler_params=pltpu.CompilerParams(vmem_limit_bytes=VMEM_LIMIT),
         cost_estimate=SMALL,
     )(*operands)
-
-
-def value_kernel(place, mine, *refs):
-    step = pl.program_id(0)
-    other_parts, (weight, values, total) = refs[:-3], refs[-3:]
-    half = weight.shape[0] // 2
-    near, away = [
-        weight[pl.ds(pl.multiple_of(core * half, half), half), :]
-        for core in (place[2], 1 - place[2])
-    ]
-
-    @pl.when(step == 0)
-    def _():
-        total[...] = jnp.zeros_like(total)
-
-    total[...] += jnp.dot(mine[0], near, preferred_element_type=jnp.float32)
-    start = 0
-    for part in other_parts:
-        rows = part.shape[1]
-        total[start:start + rows] += jnp.dot(part[0], away, preferred_element_type=jnp.float32)
-        start += rows
-
-    @pl.when(step == 7)
-    def _():
-        values[...] = total[...].astype(values.dtype)
-
-
-def project_values(place, mine, other_parts, value_weight):
-    rows, half = mine.shape[1:]
-    width = value_weight.shape[1]
-    return pl.pallas_call(
-        value_kernel,
-        name="values",
-        out_shape=jax.ShapeDtypeStruct((rows, width), jnp.bfloat16),
-        grid_spec=pltpu.PrefetchScalarGridSpec(
-            num_scalar_prefetch=1,
-            grid=(8,),
-            in_specs=[pl.BlockSpec((1, rows, half), lambda step, place: (step, 0, 0))]
-            + [
-                pl.BlockSpec((1, part.shape[1], half), lambda step, place: (step, 0, 0))
-                for part in other_parts
-            ]
-            + [pl.BlockSpec((2 * half, width), lambda step, place: (step, 0))],
-            out_specs=pl.BlockSpec((rows, width), lambda step, place: (0, 0)),
-            scratch_shapes=[pltpu.VMEM((rows, width), jnp.float32)],
-        ),
-        compiler_params=pltpu.CompilerParams(vmem_limit_bytes=VMEM_LIMIT),
-        cost_estimate=SMALL,
-    )(place, mine, *other_parts, value_weight)
 
 
 def span_rows(parts, span, low, high):
@@ -277,14 +235,6 @@
         size = part.shape[0] // 4
         pieces.append(part[span * size:(span + 1) * size, low:high])
     return jnp.concatenate(pieces, axis=0)
-
-
-def parts_of(rows, sizes):
-    parts, start = [], 0
-    for size in sizes:
-        parts.append(rows.at[start:start + size])
-        start += size
-    return parts
 
 
 def weigh_kernel(chunks, *refs):
@@ -340,10 +290,9 @@
 
 
 def attend_kernel(chunks, *refs):
-    cotangent, chances, value_rows = refs[:3]
-    key_parts = refs[3:3 + chunks]
-    attended, query_grad = refs[3 + chunks:]
-    value_parts = parts_of(value_rows, [part.shape[0] for part in key_parts])
+    cotangent, chances = refs[:2]
+    key_parts, value_parts = refs[2:2 + chunks], refs[2 + chunks:2 + 2 * chunks]
+    attended, query_grad = refs[2 + 2 * chunks:]
     width = cotangent.shape[1]
     scale = HEAD_DIM ** (-0.5)
     for span in range(4):
@@ -367,7 +316,7 @@
             ).astype(jnp.bfloat16)
 
 
-def attend(cotangent, chances, key_parts, values):
+def attend(cotangent, chances, key_parts, value_parts):
     tokens, width = cotangent.shape
     rows = sum(part.shape[0] for part in key_parts)
     vmem = pl.BlockSpec(memory_space=pltpu.VMEM)
@@ -378,16 +327,16 @@
             jax.ShapeDtypeStruct((tokens, width), jnp.bfloat16),
             jax.ShapeDtypeStruct((tokens, width), jnp.bfloat16),
         ),
-        in_specs=[vmem] * (3 + len(key_parts)),
+        in_specs=[vmem] * (2 + 2 * len(key_parts)),
         out_specs=(vmem, vmem),
         compiler_params=pltpu.CompilerParams(vmem_limit_bytes=VMEM_LIMIT),
         cost_estimate=SMALL,
-    )(cotangent, chances, values, *key_parts)
-
-
-def term_kernel(chunks, place, gradient, mine, their_gradient, *refs):
+    )(cotangent, chances, *key_parts, *value_parts)
+
+
+def term_kernel(chunks, sizes, adds, place, gradient, mine, their_gradient, *refs):
     step = pl.program_id(0)
-    their_parts, outputs = refs[:chunks], refs[chunks:]
+    their_parts, outputs = refs[:chunks], refs[chunks + adds:]
     total = jnp.dot(gradient[...], mine[0], preferred_element_type=jnp.float32)
     theirs, start = None, 0
     for part in their_parts:
@@ -400,13 +349,18 @@
     both = total.astype(jnp.bfloat16).astype(jnp.float32) + theirs.astype(jnp.bfloat16).astype(
         jnp.float32
     )
-    for n, output in enumerate(outputs):
-        @pl.when(step == n)
+    low = 0
+    for n, (size, output) in enumerate(zip(sizes, outputs)):
+        @pl.when((step >= low) & (step < low + size))
         def _():
-            output[...] = both.astype(jnp.bfloat16)
-
-
-def weight_terms(place, targets, gradient, mine, their_gradient, their_parts):
+            result = both
+            if adds and n == 0:
+                result = both + refs[chunks][0].astype(jnp.float32)
+            output[0] = result.astype(jnp.bfloat16)
+        low += size
+
+
+def weight_terms(place, targets, sizes, gradient, mine, their_gradient, their_parts, arrived=()):
     count = len(targets)
     width, rows = gradient.shape
     half = mine.shape[2]
@@ -418,40 +372,48 @@
             dy = jnp.where(n == m, targets[m][1], dy)
         return (place[0] + dz) % 4 * 2 + (place[1] + dy) % 2, 0, 0
 
+    def result_of(low, size):
+        return pl.BlockSpec(
+            (1, width, half), lambda n, place: (jnp.clip(n - low, 0, size - 1), 0, 0)
+        )
+
     whole = pl.BlockSpec((width, rows), lambda n, place: (0, 0))
     return pl.pallas_call(
-        functools.partial(term_kernel, len(their_parts)),
+        functools.partial(term_kernel, len(their_parts), sizes, len(arrived)),
         name="terms",
-        out_shape=[jax.ShapeDtypeStruct((width, half), jnp.bfloat16)] * count,
+        out_shape=[jax.ShapeDtypeStruct((size, width, half), jnp.bfloat16) for size in sizes],
         grid_spec=pltpu.PrefetchScalarGridSpec(
             num_scalar_prefetch=1,
             grid=(count,),
             in_specs=[whole, pl.BlockSpec((1, rows, half), block_of), whole]
-            + [pl.BlockSpec((1, part.shape[1], half), block_of) for part in their_parts],
-            out_specs=[pl.BlockSpec((width, half), lambda n, place: (0, 0))] * count,
+            + [pl.BlockSpec((1, part.shape[1], half), block_of) for part in their_parts]
+            + [pl.BlockSpec((1, width, half), lambda n, place: (0, 0, 0))] * len(arrived),
+            out_specs=[
+                result_of(sum(sizes[:n]), size) for n, size in enumerate(sizes)
+            ],
         ),
         compiler_params=pltpu.CompilerParams(vmem_limit_bytes=VMEM_LIMIT),
         cost_estimate=SMALL,
-    )(place, gradient, mine, their_gradient, *their_parts)
+    )(place, gradient, mine, their_gradient, *their_parts, *arrived)
 
 
 def total_kernel(*refs):
     output = refs[-1]
-    total = refs[0][...].astype(jnp.float32)
+    total = refs[0][0].astype(jnp.float32)
     for block in refs[1:-1]:
-        total += block[...].astype(jnp.float32)
+        total += block[0].astype(jnp.float32)
     output[...] = total.T
 
 
 def add_blocks(blocks):
-    width, depth = blocks[0].shape
-    vmem = pl.BlockSpec(memory_space=pltpu.VMEM)
+    width, depth = blocks[0].shape[1:]
     return pl.pallas_call(
         total_kernel,
         name="total",
         out_shape=jax.ShapeDtypeStruct((depth, width), jnp.float32),
-        in_specs=[vmem] * len(blocks),
-        out_specs=vmem,
+        grid=(1,),
+        in_specs=[pl.BlockSpec((1, width, depth), lambda n: (0, 0, 0))] * len(blocks),
+        out_specs=pl.BlockSpec((depth, width), lambda n: (0, 0)),
         compiler_params=pltpu.CompilerParams(vmem_limit_bytes=VMEM_LIMIT),
         cost_estimate=SMALL,
     )(*blocks)
@@ -476,10 +438,9 @@
     asked = [ring(both, "z", -n, 4) for n in (1, 2, 3)]
     across = ring(database, "core", 1, 2)
 
-    last = len(CHUNKS) - 1
-    firsts = [sum(CHUNKS[:k]) for k in range(last + 1)]
-
-    near_hops = ((0, 0), (3, 0), (1, 0), (0, 1), (3, 1), (1, 1))
+    firsts = [sum(CHUNKS[:k]) for k in range(len(CHUNKS))]
+
+    near_hops = ((0, 0), (1, 0), (-1, 0), (0, 1), (1, 1), (-1, 1))
     far_hops = ((2, 0), (2, 1))
 
     def shape(k):
@@ -498,16 +459,22 @@
             [tie(place, *after), both], [database, across, packets, given], count,
         )
 
-    def spread(own, *after):
+    def along(values, way):
+        steps = (way, -way)
+        return lax.ppermute(
+            values, ("core", "x"),
+            [(c * 4 + i, c * 4 + (i + steps[c]) % 4) for c in range(2) for i in range(4)],
+        )
+
+    def spread_sides(own):
         own = own.reshape(-1, width)
-        left, right = ring(own, "x", 1, 4), ring(own, "x", -1, 4)
+        ahead, behind = along(own, 1), along(own, -1)
         other = ring(own, "yhi", 1, 2)
-        sent = tie(other, left, right, *after)
-        near = (own, left, right, other, ring(sent, "x", 1, 4), ring(sent, "x", -1, 4))
-        return near, (near[1], near[5])
-
-    def pass_on(ends):
-        return ring(ends[0], "x", 1, 4), ring(ends[1], "x", -1, 4)
+        return (own, ahead, behind, other), tie(other, ahead, behind)
+
+    def spread(own):
+        near, sent = spread_sides(own)
+        return *near, along(sent, 1), along(sent, -1)
 
     def send_planes(packets, *after):
         return lax.all_to_all(tie(packets, *after), "z", 0, 0, tiled=True)
@@ -518,7 +485,7 @@
     )
     arrived = lax.all_to_all(packets, ("z", "ylo"), 0, 0, tiled=True)
     planes = [packets]
-    for k in range(1, last + 1):
+    for k in range(1, len(CHUNKS)):
         planes.append(
             copies_call(
                 functools.partial(planes_kernel, firsts[k], CHUNKS[k]), "planes",
@@ -528,59 +495,55 @@
         )
     own = copies_call(merge_kernel, "merge", shape(0), [tie(wanted, planes[-1])], [arrived], count)
     by_plane = send_planes(planes[1], own)
-    near, ends = spread(own)
-    key_parts, their_parts, sent_parts, mine, waiting = [], [], [], None, None
-
-    def finish(k, ready, pieces, hops, **begun):
-        keys, mine_now, theirs = project(
-            ready, pieces, hops, firsts[k] * count, key_weight, mine, **begun
-        )
-        key_parts.append(keys)
-        sent_parts.append(theirs)
-        their_parts.append(ring(theirs, "core", 1, 2))
-        return mine_now
-
-    for k in range(1, last + 1):
-        handed, given = hand(k, by_plane, *(near[1:] if k == 1 else near[1:4]))
-        here = by_plane
-        if k < last:
-            by_plane = send_planes(planes[k + 1], handed)
-        far = pass_on(ends)
-        if waiting is not None:
-            mine = finish(k - 2, tie(place, handed), waiting, near_hops + far_hops)
-        waiting = (*near, *far)
-        own = merge(k, here, given, *near[4:])
-        near, ends = spread(own, *key_parts[-1:])
-    mine = finish(last - 1, tie(place, near[3]), waiting, near_hops + far_hops)
-    far = pass_on(ends)
-    begun, mine, theirs = project(
-        tie(place, key_parts[-1]), near, near_hops, firsts[-1] * count, key_weight, mine,
-        ends=False,
+    near = spread(own)
+    far = (along(near[1], 1),)
+    handed, given = hand(1, by_plane, *near[1:4])
+    far += (along(tie(near[5], handed), -1),)
+    own = merge(1, by_plane, given, *near[4:], far[0])
+    matrices = (key_weight, value_weight)
+    keys, mine, theirs, values = project(
+        tie(place, own), (*near, *far), near_hops + far_hops, 0, matrices
     )
-    mine = finish(last, place, far, far_hops, theirs=theirs, begun=begun)
+    near, other = spread_sides(own)
+    far = along(tie(near[1], keys), 1)
+    steps = [(near, near_hops[:4]), ((far,), far_hops[:1])]
+    begun, last_theirs = None, None
+    for n in range(3):
+        if n == 1:
+            sent = tie(other, far, key_sum)
+            steps.append((
+                (along(sent, 1), along(sent, -1), ring(far, "yhi", 1, 2)),
+                near_hops[4:] + far_hops[1:],
+            ))
+        pieces, hops = steps[n]
+        key_sum, mine, last_theirs, value_sum = project(
+            place, pieces, hops, firsts[1] * count, matrices, mine, last_theirs, begun, n == 2
+        )
+        begun = key_sum, value_sum
+    key_parts, value_parts = [keys, key_sum], [values, value_sum]
+    their_parts = [ring(theirs, "core", 1, 2), ring(last_theirs, "core", 1, 2)]
 
     chances, gradient = weigh(queries, cotangent, key_parts)
     their_gradient = ring(gradient, "core", 1, 2)
-    totals = []
-    summed = ()
-    for low, high in GROUPS:
-        blocks = weight_terms(
-            tie(place, *summed), TARGETS[low:high], gradient, mine, their_gradient, their_parts
-        )
-        summed = blocks[:1]
-        for (dz, dy), block in zip(TARGETS[low:high], blocks):
-            if (dz, dy) != (0, 0):
-                block = lax.ppermute(
-                    block, ("z", "ylo"),
-                    [
-                        (a * 2 + b, (a + dz) % 4 * 2 + (b + dy) % 2)
-                        for a in range(4) for b in range(2)
-                    ],
-                )
-            totals.append(block)
-    values = project_values(tie(place, *summed, *totals[:GROUPS[0][1]]), mine, sent_parts, value_weight)
-    attended, query_grad = attend(cotangent, chances, key_parts, values)
-    value_weight_grad = add_blocks([*totals[:-1], tie(totals[-1], attended)])
+    def terms(targets, sizes, arrived=(), after=()):
+        return weight_terms(
+            tie(place, *after), targets, sizes, gradient, mine, their_gradient, their_parts,
+            arrived,
+        )
+
+    ahead, behind = terms(((1, 0), (1, 1), (3, 0), (3, 1)), (2, 2))
+    corner, = terms(((2, 1),), (1,), (), (behind,))
+    beside, here = terms(((0, 1), (0, 0)), (1, 1), (), (corner,))
+    far, = terms(((2, 0),), (1,), (ring(corner, "ylo", 1, 2),), (here,))
+    beside = tie(beside, far)
+    ahead, behind = ring(ahead, "z", 1, 4), ring(behind, "z", -1, 4)
+    far = ring(far, "z", 2, 4)
+    beside = beside.astype(jnp.float32) + ahead[1:] + behind[1:]
+    beside = ring(beside.astype(jnp.bfloat16), "ylo", 1, 2)
+    attended, query_grad = attend(cotangent, chances, key_parts, value_parts)
+    value_weight_grad = add_blocks(
+        [ahead, behind, far, here, tie(beside, attended)]
+    )
     return attended, query_grad, value_weight_grad
 
 

time: 330 us -> 300 us (0.909)
  waiting for transfers between devices: 114 us -> 135 us
  starting transfers between devices: 77.3 us -> 56.6 us
  Pallas kernels: 117 us -> 98.1 us
  local copies, waits for them, and re-layouts: 18.1 us -> 8.49 us
    ppermute x41 -> x17, waiting for transfers between devices: 84.2 us -> 46 us  [ring(): lax.ppermute(values, axis, [(i, (i + shift) % size) for i in range(size)])]
    all_to_all x1, waiting for transfers between devices: 14.1 us -> 43.3 us  [per_device(): arrived = lax.all_to_all(packets, ('z', 'ylo'), 0, 0, tiled=True)]
    ppermute x41 -> x17, starting transfers between devices: 48.3 us -> 29.6 us  [ring(): lax.ppermute(values, axis, [(i, (i + shift) % size) for i in range(size)])]
    all_to_all x3 -> x1, waiting for transfers between devices: 0.01 us -> 16.2 us  [send_planes(): return lax.all_to_all(tie(packets, *after), 'z', 0, 0, tiled=True)]
    pallas_call x11 -> x5, Pallas kernels: 32.9 us -> 18.1 us  [copies_call(): pl.pallas_call(kernel, name=name, out_shape=jax.ShapeDtypeStruct(shape, j...]
    ppermute x7 -> x11, waiting for transfers between devices: 15.5 us -> 29.2 us  [along(): lax.ppermute(values, ('core', 'x'), [(c * 4 + i, c * 4 + (i + steps[c]) %...]
    unnamed x84 -> x46, local copies, waits for them, and re-layouts: 17.3 us -> 7.65 us
    pallas_call x3 -> x4, Pallas kernels: 36.1 us -> 26.5 us  [weight_terms(): pl.pallas_call(functools.partial(term_kernel, len(their_parts), sizes, le...]
  transfers between devices with their start and end apart: 52 -> 30, of which waited for: 24 -> 17; matrix products, arithmetic and copies ran while one was open for 1% -> 1% of each run, Pallas kernels for 29% -> 26%
where the time goes in v3:
time: 300 us; the launch traced here: 299 us
  waiting for transfers between devices  135 us (45%)
  Pallas kernels  98.1 us (33%)
  starting transfers between devices  56.6 us (19%)
  local copies, waits for them, and re-layouts  8.49 us (3%)
    ppermute x17, waiting for transfers between devices, ring(): lax.ppermute(values, axis, [(i, (i + shift) % size) for i in range(size)])  46 us
    all_to_all x1, waiting for transfers between devices, per_device(): arrived = lax.all_to_all(packets, ('z', 'ylo'), 0, 0, tiled=True)  43.3 us
    pallas_call x4, Pallas kernels, project(): pl.pallas_call(functools.partial(project_kernel, hops, first, begun is No...  42.5 us
    ppermute x17, starting transfers between devices, ring(): lax.ppermute(values, axis, [(i, (i + shift) % size) for i in range(size)])  29.6 us
    ppermute x11, waiting for transfers between devices, along(): lax.ppermute(values, ('core', 'x'), [(c * 4 + i, c * 4 + (i + steps[c]) %...  29.2 us
    pallas_call x4, Pallas kernels, weight_terms(): pl.pallas_call(functools.partial(term_kernel, len(their_parts), sizes, le...  26.5 us
    pallas_call x5, Pallas kernels, copies_call(): pl.pallas_call(kernel, name=name, out_shape=jax.ShapeDtypeStruct(shape, j...  18.1 us
    ppermute x11, starting transfers between devices, along(): lax.ppermute(values, ('core', 'x'), [(c * 4 + i, c * 4 + (i + steps[c]) %...  17.3 us
  transfers between devices with their start and end apart: 30, of which 17 were waited for; matrix products, arithmetic and copies ran while one was open for 1% of the time, Pallas kernels for 26%

profile of v3, /device:TPU:6, one launch (start us, length us, event | category | flops | bytes accessed | tf_op | source)
XLA Modules:
  0.0 299.2 jit_solution(17779389054073505191)
XLA Ops:
  8.4 3.6 %collective-permute-start.2 = (s32[2,32]{1,0:T(2,128)S(1)}, s32[2,32]{1,0:T(2,128)S(1)}, u32[]{:S(2)}, u32[]{:S(2)}) collective-permute-start(s32[2,32]{1,0:T(2,128)S(1)} %pad_add_fusion.both), channel_id=1, source_target_pairs={{0,64},{32,96},{64,0},{96,32},{1,65},{33,97},{65,1},{97,33},{2,66}... | collective-permute-start | bytes 776 | tf_op jit(solution)/shard_map/ppermute | solution.py:21
  16.1 4.7 %pack.1 = bf16[32,64,1024]{2,1,0:T(8,128)(2,1)} custom-call(s32[5]{0:T(128)} %stack.23.place, s32[2,32]{1,0:T(2,128)} %copy-done.17, s32[2,32]{1,0:T(2,128)} %copy-done.20, s32[2,32]{1,0:T(2,128)} %copy-done.19, s32[2,32]{1,0:T(2,128)} %copy-done.18, bf16[16,128,1024]{2,1,0:T(8,128)(2,1)} %own.7, bf16[16,128,1024]{2,1,0:T(8,128)(2,1)} %collective-permute-done.4.across), custom_call_target="tpu_custom_call" | custom-call | flops 1 | bytes 1 | tf_op jit(solution)/shard_map/pack/pallas_call | solution.py:114
  20.8 4.6 %all-to-all-start = ((bf16[32,64,1024]{2,1,0:T(8,128)(2,1)}), bf16[32,64,1024]{2,1,0:T(8,128)(2,1)}, u32[]{:S(2)}, u32[]{:S(2)}) async-start(bf16[32,64,1024]{2,1,0:T(8,128)(2,1)} %pack.1), calls=%async_computation | async-start | bytes 8388608 | tf_op jit(solution)/shard_map/all_to_all | solution.py:486
  25.4 4.5 %planes.1 = bf16[32,64,1024]{2,1,0:T(8,128)(2,1)} custom-call(s32[5]{0:T(128)} %stack.23.place, s32[2,32]{1,0:T(2,128)} %copy-done.20, s32[2,32]{1,0:T(2,128)} %copy-done.19, s32[2,32]{1,0:T(2,128)} %copy-done.18, bf16[16,128,1024]{2,1,0:T(8,128)(2,1)} %own.7, bf16[16,128,1024]{2,1,0:T(8,128)(2,1)} %collective-permute-done.4.across), custom_call_target="tpu_custom_call" | custom-call | flops 1 | bytes 1 | tf_op jit(solution)/shard_map/planes/pallas_call | solution.py:114
  29.9 43.3 %all-to-all-done.packets = bf16[32,64,1024]{2,1,0:T(8,128)(2,1)} async-done(((bf16[32,64,1024]{2,1,0:T(8,128)(2,1)}), bf16[32,64,1024]{2,1,0:T(8,128)(2,1)}, u32[]{:S(2)}, u32[]{:S(2)}) %all-to-all-start) | async-done | bytes 4194336 | tf_op jit(solution)/shard_map/all_to_all | solution.py:486
  76.2 5.0 %all-to-all-start.1 = ((bf16[32,64,1024]{2,1,0:T(8,128)(2,1)}), bf16[32,64,1024]{2,1,0:T(8,128)(2,1)}, u32[]{:S(2)}, u32[]{:S(2)}) async-start(bf16[32,64,1024]{2,1,0:T(8,128)(2,1)} %planes.1), calls=%async_computation.1 | async-start | bytes 8388608 | tf_op jit(solution)/shard_map/all_to_all | solution.py:480
  84.5 3.2 %collective-permute-start.5 = (bf16[512,1024]{1,0:T(8,128)(2,1)S(1)}, bf16[512,1024]{1,0:T(8,128)(2,1)}, u32[]{:S(2)}, u32[]{:S(2)}) collective-permute-start(bf16[512,1024]{1,0:T(8,128)(2,1)S(1)} %bitcast.15), channel_id=1, source_target_pairs={{0,1},{1,0},{2,3},{3,2},{4,5},{5,4},{6,7},{7,6},{8,9},{9,8},{10,11... | collective-permute-start | bytes 3145736 | tf_op jit(solution)/shard_map/ppermute | solution.py:21
  87.7 17.0 %collective-permute-done.7.refs_2_ = bf16[512,1024]{1,0:T(8,128)(2,1)S(1)} collective-permute-done((bf16[512,1024]{1,0:T(8,128)(2,1)S(1)}, bf16[512,1024]{1,0:T(8,128)(2,1)S(1)}, u32[]{:S(2)}, u32[]{:S(2)}) %collective-permute-start.7) | collective-permute-done | bytes 1048608 | tf_op jit(solution)/shard_map/ppermute | solution.py:464
  111.3 16.2 %all-to-all-done.1.packets = bf16[32,64,1024]{2,1,0:T(8,128)(2,1)} async-done(((bf16[32,64,1024]{2,1,0:T(8,128)(2,1)}), bf16[32,64,1024]{2,1,0:T(8,128)(2,1)}, u32[]{:S(2)}, u32[]{:S(2)}) %all-to-all-start.1) | async-done | bytes 4194336 | tf_op jit(solution)/shard_map/all_to_all | solution.py:480
  132.2 3.4 %collective-permute-done.9.refs_5_ = bf16[512,1024]{1,0:T(8,128)(2,1)} collective-permute-done((bf16[512,1024]{1,0:T(8,128)(2,1)}, bf16[512,1024]{1,0:T(8,128)(2,1)}, u32[]{:S(2)}, u32[]{:S(2)}) %collective-permute-start.9) | collective-permute-done | bytes 1048608 | tf_op jit(solution)/shard_map/ppermute | solution.py:464
  135.7 3.3 %collective-permute-done.8.refs_4_ = bf16[512,1024]{1,0:T(8,128)(2,1)} collective-permute-done((bf16[512,1024]{1,0:T(8,128)(2,1)}, bf16[512,1024]{1,0:T(8,128)(2,1)}, u32[]{:S(2)}, u32[]{:S(2)}) %collective-permute-start.8) | collective-permute-done | bytes 1048608 | tf_op jit(solution)/shard_map/ppermute | solution.py:464
  140.0 11.8 %collective-permute-done.11.refs_0_ = bf16[8,64,1024]{2,1,0:T(8,128)(2,1)} collective-permute-done((bf16[8,64,1024]{2,1,0:T(8,128)(2,1)}, bf16[8,64,1024]{2,1,0:T(8,128)(2,1)}, u32[]{:S(2)}, u32[]{:S(2)}) %collective-permute-start.11) | collective-permute-done | bytes 1048608 | tf_op jit(solution)/shard_map/ppermute | solution.py:21
  151.8 3.1 %merge.3 = bf16[8,64,1024]{2,1,0:T(8,128)(2,1)} custom-call(s32[5]{0:T(128)} %stack.23.place, s32[2,32]{1,0:T(2,128)} %copy-done.17, bf16[16,128,1024]{2,1,0:T(8,128)(2,1)} %own.7, bf16[16,128,1024]{2,1,0:T(8,128)(2,1)} %collective-permute-done.4.across, bf16[32,64,1024]{2,1,0:T(8,128)(2,1)} %all-to-all-done.1.packets, ...), custom_call_target="tpu_custom_call" | custom-call | flops 1 | bytes 1 | tf_op jit(solution)/shard_map/merge/pallas_call | solution.py:114
  157.0 3.2 %collective-permute-start.13 = (bf16[512,1024]{1,0:T(8,128)(2,1)}, bf16[512,1024]{1,0:T(8,128)(2,1)S(1)}, u32[]{:S(2)}, u32[]{:S(2)}) collective-permute-start(bf16[512,1024]{1,0:T(8,128)(2,1)} %bitcast.10), channel_id=1, source_target_pairs={{0,1},{1,0},{2,3},{3,2},{4,5},{5,4},{6,7},{7,6},{8,9},{9,8},{10,11... | collective-permute-start | bytes 3145736 | tf_op jit(solution)/shard_map/ppermute | solution.py:21
  161.3 16.0 %project.4 = (bf16[512,512]{1,0:T(8,128)(2,1)}, bf16[8,1024,512]{2,1,0:T(8,128)(2,1)}, bf16[8,512,512]{2,1,0:T(8,128)(2,1)}, bf16[512,512]{1,0:T(8,128)(2,1)}) custom-call(s32[5]{0:T(128)} %stack.23.place, bf16[512,1024]{1,0:T(8,128)(2,1)} %bitcast.12, bf16[512,1024]{1,0:T(8,128)(2,1)} %copy-done.5, bf16[512,1024]{1,0:T(8,128)(2,1)} %copy-done.4, ...), custom_call_target="tpu_custom_call" | custom-call | flops 1 | bytes 1 | tf_op jit(solution)/shard_map/project/pallas_call | solution.py:203
  180.6 10.6 %project.5 = (f32[512,512]{1,0:T(8,128)}, bf16[8,1024,512]{2,1,0:T(8,128)(2,1)}, bf16[8,512,512]{2,1,0:T(8,128)(2,1)}, f32[512,512]{1,0:T(8,128)}) custom-call(s32[5]{0:T(128)} %stack.23.place, bf16[512,1024]{1,0:T(8,128)(2,1)} %bitcast.11, bf16[512,1024]{1,0:T(8,128)(2,1)} %copy-done.8, ...), custom_call_target="tpu_custom_call", output_to_operand_aliasing={{1}: (7, {})} | custom-call | flops 1 | bytes 1 | tf_op jit(solution)/shard_map/project/pallas_call | solution.py:203
  192.1 3.9 %collective-permute-start.19 = (bf16[512,1024]{1,0:T(8,128)(2,1)S(1)}, bf16[512,1024]{1,0:T(8,128)(2,1)S(1)}, u32[]{:S(2)}, u32[]{:S(2)}) collective-permute-start(bf16[512,1024]{1,0:T(8,128)(2,1)S(1)} %collective-permute-done.16.refs_0_), channel_id=1, source_target_pairs={{0,1},{1,0},{2,3},{3,2},{4,5},{5,4},{6,7},{7,6},{8,9},{9,8},{10,11... | collective-permute-start | bytes 3145736 | tf_op jit(solution)/shard_map/ppermute | solution.py:21
  196.1 3.7 %collective-permute-start.17 = (bf16[512,1024]{1,0:T(8,128)(2,1)}, bf16[512,1024]{1,0:T(8,128)(2,1)}, u32[]{:S(2)}, u32[]{:S(2)}) collective-permute-start(bf16[512,1024]{1,0:T(8,128)(2,1)} %copy-done.6), channel_id=1, source_target_pairs={{0,2},{2,4},{4,6},{6,0},{8,14},{10,8},{12,10},{14,12},{1,3},{3,5},... | collective-permute-start | bytes 3145736 | tf_op jit(solution)/shard_map/ppermute | solution.py:464
  199.7 6.6 %project.6 = (f32[512,512]{1,0:T(8,128)}, bf16[8,1024,512]{2,1,0:T(8,128)(2,1)}, bf16[8,512,512]{2,1,0:T(8,128)(2,1)}, f32[512,512]{1,0:T(8,128)}) custom-call(s32[5]{0:T(128)} %stack.23.place, bf16[512,1024]{1,0:T(8,128)(2,1)} %copy-done.9, bf16[8192,512]{1,0:T(8,128)(2,1)} %refs_3_.1, ...), custom_call_target="tpu_custom_call", output_to_operand_aliasing={{1}: (6, {}), {2}: (7, {})} | custom-call | flops 1 | bytes 1 | tf_op jit(solution)/shard_map/project/pallas_call | solution.py:203
  206.3 9.0 %collective-permute-done.19.refs_2_ = bf16[512,1024]{1,0:T(8,128)(2,1)S(1)} collective-permute-done((bf16[512,1024]{1,0:T(8,128)(2,1)S(1)}, bf16[512,1024]{1,0:T(8,128)(2,1)S(1)}, u32[]{:S(2)}, u32[]{:S(2)}) %collective-permute-start.19) | collective-permute-done | bytes 1048608 | tf_op jit(solution)/shard_map/ppermute | solution.py:21
  215.3 4.5 %collective-permute-done.18.refs_1_ = bf16[512,1024]{1,0:T(8,128)(2,1)S(1)} collective-permute-done((bf16[512,1024]{1,0:T(8,128)(2,1)}, bf16[512,1024]{1,0:T(8,128)(2,1)S(1)}, u32[]{:S(2)}, u32[]{:S(2)}) %collective-permute-start.18) | collective-permute-done | bytes 1048608 | tf_op jit(solution)/shard_map/ppermute | solution.py:464
  220.8 9.3 %project.7 = (bf16[512,512]{1,0:T(8,128)(2,1)}, bf16[8,1024,512]{2,1,0:T(8,128)(2,1)}, bf16[8,512,512]{2,1,0:T(8,128)(2,1)}, bf16[512,512]{1,0:T(8,128)(2,1)}) custom-call(s32[5]{0:T(128)} %stack.23.place, bf16[512,1024]{1,0:T(8,128)(2,1)} %collective-permute-done.17.refs_0_, ...), custom_call_target="tpu_custom_call", output_to_operand_aliasing={{1}: (8, {}), {2}: (9, {})} | custom-call | flops 1 | bytes 1 | tf_op jit(solution)/shard_map/project/pallas_call | solution.py:203
  230.2 4.4 %weigh.1 = (f32[16,64,256]{2,1,0:T(8,128)}, bf16[512,1024]{1,0:T(8,128)(2,1)}) custom-call(bf16[256,512]{1,0:T(8,128)(2,1)} %refs_0_.2, bf16[256,512]{1,0:T(8,128)(2,1)} %refs_0_.3, bf16[512,512]{1,0:T(8,128)(2,1)} %get-tuple-element.51.refs_2_, bf16[512,512]{1,0:T(8,128)(2,1)} %get-tuple-element.64.refs_3_), custom_call_target="tpu_custom_call" | custom-call | flops 1 | bytes 1 | tf_op jit(solution)/shard_map/weigh/pallas_call | solution.py:277
  235.1 3.9 %collective-permute-done.20.their_gradient = bf16[512,1024]{1,0:T(8,128)(2,1)S(1)} collective-permute-done((bf16[512,1024]{1,0:T(8,128)(2,1)}, bf16[512,1024]{1,0:T(8,128)(2,1)S(1)}, u32[]{:S(2)}, u32[]{:S(2)}) %collective-permute-start.20) | collective-permute-done | bytes 1048608 | tf_op jit(solution)/shard_map/ppermute | solution.py:21
  240.0 9.8 %terms.4 = (bf16[2,512,512]{2,1,0:T(8,128)(2,1)}, bf16[2,512,512]{2,1,0:T(8,128)(2,1)}) custom-call(s32[5]{0:T(128)} %stack.23.place, bf16[512,1024]{1,0:T(8,128)(2,1)} %get-tuple-element.70.gradient, bf16[8,1024,512]{2,1,0:T(8,128)(2,1)} %get-tuple-element.71.mine, bf16[512,1024]{1,0:T(8,128)(2,1)} %copy-done, ...), custom_call_target="tpu_custom_call" | custom-call | flops 1 | bytes 1 | tf_op jit(solution)/shard_map/terms/pallas_call | solution.py:381
  251.9 3.6 %collective-permute-start.24 = (bf16[2,512,512]{2,1,0:T(8,128)(2,1)}, bf16[2,512,512]{2,1,0:T(8,128)(2,1)S(1)}, u32[]{:S(2)}, u32[]{:S(2)}) collective-permute-start(bf16[2,512,512]{2,1,0:T(8,128)(2,1)} %get-tuple-element.75), channel_id=1, source_target_pairs={{0,96},{32,0},{64,32},{96,64},{1,97},{33,1},{65,33},{97,65},{2,98}... | collective-permute-start | bytes 3145736 | tf_op jit(solution)/shard_map/ppermute | solution.py:21
  255.5 4.9 %terms.5 = bf16[1,512,512]{2,1,0:T(8,128)(2,1)} custom-call(s32[5]{0:T(128)} %stack.23.place, bf16[512,1024]{1,0:T(8,128)(2,1)} %get-tuple-element.70.gradient, bf16[8,1024,512]{2,1,0:T(8,128)(2,1)} %get-tuple-element.71.mine, bf16[512,1024]{1,0:T(8,128)(2,1)} %copy-done, bf16[8,512,512]{2,1,0:T(8,128)(2,1)} %collective-permute-done.21.refs_0_, ...), custom_call_target="tpu_custom_call" | custom-call | flops 1 | bytes 1 | tf_op jit(solution)/shard_map/terms/pallas_call | solution.py:381
  260.9 6.7 %terms.6 = (bf16[1,512,512]{2,1,0:T(8,128)(2,1)}, bf16[1,512,512]{2,1,0:T(8,128)(2,1)}) custom-call(s32[5]{0:T(128)} %stack.23.place, bf16[512,1024]{1,0:T(8,128)(2,1)} %get-tuple-element.70.gradient, bf16[8,1024,512]{2,1,0:T(8,128)(2,1)} %get-tuple-element.71.mine, bf16[512,1024]{1,0:T(8,128)(2,1)} %copy-done, ...), custom_call_target="tpu_custom_call" | custom-call | flops 1 | bytes 1 | tf_op jit(solution)/shard_map/terms/pallas_call | solution.py:381
  267.6 6.7 %collective-permute-done.25.refs_2_ = bf16[1,512,512]{2,1,0:T(8,128)(2,1)S(1)} collective-permute-done((bf16[1,512,512]{2,1,0:T(8,128)(2,1)}, bf16[1,512,512]{2,1,0:T(8,128)(2,1)S(1)}, u32[]{:S(2)}, u32[]{:S(2)}) %collective-permute-start.25) | collective-permute-done | bytes 524320 | tf_op jit(solution)/shard_map/ppermute | solution.py:21
  275.1 5.1 %terms.7 = bf16[1,512,512]{2,1,0:T(8,128)(2,1)} custom-call(s32[5]{0:T(128)} %stack.23.place, bf16[512,1024]{1,0:T(8,128)(2,1)} %get-tuple-element.70.gradient, bf16[8,1024,512]{2,1,0:T(8,128)(2,1)} %get-tuple-element.71.mine, bf16[512,1024]{1,0:T(8,128)(2,1)} %copy-done, bf16[8,512,512]{2,1,0:T(8,128)(2,1)} %collective-permute-done.21.refs_0_, ...), custom_call_target="tpu_custom_call" | custom-call | flops 1 | bytes 1 | tf_op jit(solution)/shard_map/terms/pallas_call | solution.py:381
  282.8 3.6 %attend.1 = (bf16[256,512]{1,0:T(8,128)(2,1)}, bf16[256,512]{1,0:T(8,128)(2,1)}) custom-call(bf16[256,512]{1,0:T(8,128)(2,1)} %refs_0_.3, f32[16,64,256]{2,1,0:T(8,128)} %get-tuple-element.65.refs_1_, bf16[512,512]{1,0:T(8,128)(2,1)} %get-tuple-element.51.refs_2_, bf16[512,512]{1,0:T(8,128)(2,1)} %get-tuple-element.64.refs_3_, ...), custom_call_target="tpu_custom_call" | custom-call | flops 1 | bytes 1 | tf_op jit(solution)/shard_map/attend/pallas_call | solution.py:323
  286.4 6.9 %collective-permute-done.27.refs_4_ = bf16[1,512,512]{2,1,0:T(8,128)(2,1)S(1)} collective-permute-done((bf16[1,512,512]{2,1,0:T(8,128)(2,1)S(1)}, bf16[1,512,512]{2,1,0:T(8,128)(2,1)S(1)}, u32[]{:S(2)}, u32[]{:S(2)}) %collective-permute-start.27) | collective-permute-done | bytes 524320 | tf_op jit(solution)/shard_map/ppermute | solution.py:21
  (100 shorter events, 52.1 us)
Async XLA Ops:
  0.6 14.9 %collective-permute-start.4 = (bf16[16,128,1024]{2,1,0:T(8,128)(2,1)}, bf16[16,128,1024]{2,1,0:T(8,128)(2,1)}, u32[]{:S(2)}, u32[]{:S(2)}) collective-permute-start(bf16[16,128,1024]{2,1,0:T(8,128)(2,1)} %own.7), channel_id=1, source_target_pairs={{0,8},{8,0},{1,9},{9,1},{2,10},{10,2},{3,11},{11,3},{4,12},{12,4},... | collective-permute-start | bytes 12582920 | tf_op jit(solution)/shard_map/ppermute | solution.py:21
  2.8 3.6 %collective-permute-start = (s32[1,32]{1,0:T(1,128)S(1)}, s32[1,32]{1,0:T(1,128)S(1)}, u32[]{:S(2)}, u32[]{:S(2)}) collective-permute-start(s32[1,32]{1,0:T(1,128)S(1)} %pad_add_fusion.1.wanted), channel_id=1, source_target_pairs={{0,16},{16,0},{1,17},{17,1},{2,18},{18,2},{3,19},{19,3},{4,20},{20... | collective-permute-start | bytes 392 | tf_op jit(solution)/shard_map/ppermute | solution.py:21
  6.5 7.1 %collective-permute-start.3 = (s32[2,32]{1,0:T(2,128)S(1)}, s32[2,32]{1,0:T(2,128)S(1)}, u32[]{:S(2)}, u32[]{:S(2)}) collective-permute-start(s32[2,32]{1,0:T(2,128)S(1)} %pad_add_fusion.both), channel_id=1, source_target_pairs={{0,32},{32,64},{64,96},{96,0},{1,33},{33,65},{65,97},{97,1},{2,34}... | collective-permute-start | bytes 776 | tf_op jit(solution)/shard_map/ppermute | solution.py:21
  8.4 5.2 %collective-permute-start.2 = (s32[2,32]{1,0:T(2,128)S(1)}, s32[2,32]{1,0:T(2,128)S(1)}, u32[]{:S(2)}, u32[]{:S(2)}) collective-permute-start(s32[2,32]{1,0:T(2,128)S(1)} %pad_add_fusion.both), channel_id=1, source_target_pairs={{0,64},{32,96},{64,0},{96,32},{1,65},{33,97},{65,1},{97,33},{2,66}... | collective-permute-start | bytes 776 | tf_op jit(solution)/shard_map/ppermute | solution.py:21
  12.0 3.6 %collective-permute-start.1 = (s32[2,32]{1,0:T(2,128)S(1)}, s32[2,32]{1,0:T(2,128)S(1)}, u32[]{:S(2)}, u32[]{:S(2)}) collective-permute-start(s32[2,32]{1,0:T(2,128)S(1)} %pad_add_fusion.both), channel_id=1, source_target_pairs={{0,96},{32,0},{64,32},{96,64},{1,97},{33,1},{65,33},{97,65},{2,98}... | collective-permute-start | bytes 776 | tf_op jit(solution)/shard_map/ppermute | solution.py:21
  20.8 52.4 %all-to-all-start = ((bf16[32,64,1024]{2,1,0:T(8,128)(2,1)}), bf16[32,64,1024]{2,1,0:T(8,128)(2,1)}, u32[]{:S(2)}, u32[]{:S(2)}) async-start(bf16[32,64,1024]{2,1,0:T(8,128)(2,1)} %pack.1), calls=%async_computation | async-start | bytes 8388608 | tf_op jit(solution)/shard_map/all_to_all | solution.py:486
  76.2 51.3 %all-to-all-start.1 = ((bf16[32,64,1024]{2,1,0:T(8,128)(2,1)}), bf16[32,64,1024]{2,1,0:T(8,128)(2,1)}, u32[]{:S(2)}, u32[]{:S(2)}) async-start(bf16[32,64,1024]{2,1,0:T(8,128)(2,1)} %planes.1), calls=%async_computation.1 | async-start | bytes 8388608 | tf_op jit(solution)/shard_map/all_to_all | solution.py:480
  81.2 23.5 %collective-permute-start.7 = (bf16[512,1024]{1,0:T(8,128)(2,1)S(1)}, bf16[512,1024]{1,0:T(8,128)(2,1)S(1)}, u32[]{:S(2)}, u32[]{:S(2)}) collective-permute-start(bf16[512,1024]{1,0:T(8,128)(2,1)S(1)} %bitcast.13), channel_id=1, source_target_pairs={{0,6},{2,0},{4,2},{6,4},{8,10},{10,12},{12,14},{14,8},{1,7},{3,1},... | collective-permute-start | bytes 3145736 | tf_op jit(solution)/shard_map/ppermute | solution.py:464
  82.1 22.6 %collective-permute-start.6 = (bf16[512,1024]{1,0:T(8,128)(2,1)S(1)}, bf16[512,1024]{1,0:T(8,128)(2,1)S(1)}, u32[]{:S(2)}, u32[]{:S(2)}) collective-permute-start(bf16[512,1024]{1,0:T(8,128)(2,1)S(1)} %bitcast.14), channel_id=1, source_target_pairs={{0,2},{2,4},{4,6},{6,0},{8,14},{10,8},{12,10},{14,12},{1,3},{3,5},... | collective-permute-start | bytes 3145736 | tf_op jit(solution)/shard_map/ppermute | solution.py:464
  84.5 21.8 %collective-permute-start.5 = (bf16[512,1024]{1,0:T(8,128)(2,1)S(1)}, bf16[512,1024]{1,0:T(8,128)(2,1)}, u32[]{:S(2)}, u32[]{:S(2)}) collective-permute-start(bf16[512,1024]{1,0:T(8,128)(2,1)S(1)} %bitcast.15), channel_id=1, source_target_pairs={{0,1},{1,0},{2,3},{3,2},{4,5},{5,4},{6,7},{7,6},{8,9},{9,8},{10,11... | collective-permute-start | bytes 3145736 | tf_op jit(solution)/shard_map/ppermute | solution.py:21
  104.7 25.6 %copy-start.4 = (bf16[512,1024]{1,0:T(8,128)(2,1)}, bf16[512,1024]{1,0:T(8,128)(2,1)S(1)}, u32[]{:S(2)}) copy-start(bf16[512,1024]{1,0:T(8,128)(2,1)S(1)} %collective-permute-done.7.refs_2_) | copy-start | bytes 3145732
  104.7 25.6 %copy-start.5 = (bf16[512,1024]{1,0:T(8,128)(2,1)}, bf16[512,1024]{1,0:T(8,128)(2,1)S(1)}, u32[]{:S(2)}) copy-start(bf16[512,1024]{1,0:T(8,128)(2,1)S(1)} %collective-permute-done.6.refs_1_) | copy-start | bytes 3145732
  106.4 25.9 %collective-permute-start.10 = (bf16[512,1024]{1,0:T(8,128)(2,1)S(1)}, bf16[512,1024]{1,0:T(8,128)(2,1)S(1)}, u32[]{:S(2)}, u32[]{:S(2)}) collective-permute-start(bf16[512,1024]{1,0:T(8,128)(2,1)S(1)} %collective-permute-done.6.refs_1_), channel_id=1, source_target_pairs={{0,2},{2,4},{4,6},{6,0},{8,14},{10,8},{12,10},{14,12},{1,3},{3,5},... | collective-permute-start | bytes 3145736 | tf_op jit(solution)/shard_map/ppermute | solution.py:464
  108.1 27.6 %collective-permute-start.9 = (bf16[512,1024]{1,0:T(8,128)(2,1)}, bf16[512,1024]{1,0:T(8,128)(2,1)}, u32[]{:S(2)}, u32[]{:S(2)}) collective-permute-start(bf16[512,1024]{1,0:T(8,128)(2,1)} %collective-permute-done.5.refs_3_), channel_id=1, source_target_pairs={{0,6},{2,0},{4,2},{6,4},{8,10},{10,12},{12,14},{14,8},{1,7},{3,1},... | collective-permute-start | bytes 3145736 | tf_op jit(solution)/shard_map/ppermute | solution.py:464
  108.4 30.6 %collective-permute-start.8 = (bf16[512,1024]{1,0:T(8,128)(2,1)}, bf16[512,1024]{1,0:T(8,128)(2,1)}, u32[]{:S(2)}, u32[]{:S(2)}) collective-permute-start(bf16[512,1024]{1,0:T(8,128)(2,1)} %collective-permute-done.5.refs_3_), channel_id=1, source_target_pairs={{0,2},{2,4},{4,6},{6,0},{8,14},{10,8},{12,10},{14,12},{1,3},{3,5},... | collective-permute-start | bytes 3145736 | tf_op jit(solution)/shard_map/ppermute | solution.py:464
  130.3 21.5 %collective-permute-start.11 = (bf16[8,64,1024]{2,1,0:T(8,128)(2,1)}, bf16[8,64,1024]{2,1,0:T(8,128)(2,1)}, u32[]{:S(2)}, u32[]{:S(2)}) collective-permute-start(bf16[8,64,1024]{2,1,0:T(8,128)(2,1)} %hand.1), channel_id=1, source_target_pairs={{0,16},{16,0},{1,17},{17,1},{2,18},{18,2},{3,19},{19,3},{4,20},{20... | collective-permute-start | bytes 3145736 | tf_op jit(solution)/shard_map/ppermute | solution.py:21
  139.0 21.3 %collective-permute-start.12 = (bf16[512,1024]{1,0:T(8,128)(2,1)}, bf16[512,1024]{1,0:T(8,128)(2,1)S(1)}, u32[]{:S(2)}, u32[]{:S(2)}) collective-permute-start(bf16[512,1024]{1,0:T(8,128)(2,1)} %collective-permute-done.9.refs_5_), channel_id=1, source_target_pairs={{0,6},{2,0},{4,2},{6,4},{8,10},{10,12},{12,14},{14,8},{1,7},{3,1},... | collective-permute-start | bytes 3145736 | tf_op jit(solution)/shard_map/ppermute | solution.py:464
  154.9 22.3 %collective-permute-start.14 = (bf16[512,1024]{1,0:T(8,128)(2,1)}, bf16[512,1024]{1,0:T(8,128)(2,1)S(1)}, u32[]{:S(2)}, u32[]{:S(2)}) collective-permute-start(bf16[512,1024]{1,0:T(8,128)(2,1)} %bitcast.8), channel_id=1, source_target_pairs={{0,2},{2,4},{4,6},{6,0},{8,14},{10,8},{12,10},{14,12},{1,3},{3,5},... | collective-permute-start | bytes 3145736 | tf_op jit(solution)/shard_map/ppermute | solution.py:464
  155.5 24.1 %collective-permute-start.15 = (bf16[512,1024]{1,0:T(8,128)(2,1)}, bf16[512,1024]{1,0:T(8,128)(2,1)}, u32[]{:S(2)}, u32[]{:S(2)}) collective-permute-start(bf16[512,1024]{1,0:T(8,128)(2,1)} %bitcast.9), channel_id=1, source_target_pairs={{0,6},{2,0},{4,2},{6,4},{8,10},{10,12},{12,14},{14,8},{1,7},{3,1},... | collective-permute-start | bytes 3145736 | tf_op jit(solution)/shard_map/ppermute | solution.py:464
  157.0 22.7 %collective-permute-start.13 = (bf16[512,1024]{1,0:T(8,128)(2,1)}, bf16[512,1024]{1,0:T(8,128)(2,1)S(1)}, u32[]{:S(2)}, u32[]{:S(2)}) collective-permute-start(bf16[512,1024]{1,0:T(8,128)(2,1)} %bitcast.10), channel_id=1, source_target_pairs={{0,1},{1,0},{2,3},{3,2},{4,5},{5,4},{6,7},{7,6},{8,9},{9,8},{10,11... | collective-permute-start | bytes 3145736 | tf_op jit(solution)/shard_map/ppermute | solution.py:21
  177.3 14.9 %collective-permute-start.16 = (bf16[512,1024]{1,0:T(8,128)(2,1)S(1)}, bf16[512,1024]{1,0:T(8,128)(2,1)S(1)}, u32[]{:S(2)}, u32[]{:S(2)}) collective-permute-start(bf16[512,1024]{1,0:T(8,128)(2,1)S(1)} %collective-permute-done.14.refs_1_), channel_id=1, source_target_pairs={{0,2},{2,4},{4,6},{6,0},{8,14},{10,8},{12,10},{14,12},{1,3},{3,5},... | collective-permute-start | bytes 3145736 | tf_op jit(solution)/shard_map/ppermute | solution.py:464
  192.1 23.2 %collective-permute-start.19 = (bf16[512,1024]{1,0:T(8,128)(2,1)S(1)}, bf16[512,1024]{1,0:T(8,128)(2,1)S(1)}, u32[]{:S(2)}, u32[]{:S(2)}) collective-permute-start(bf16[512,1024]{1,0:T(8,128)(2,1)S(1)} %collective-permute-done.16.refs_0_), channel_id=1, source_target_pairs={{0,1},{1,0},{2,3},{3,2},{4,5},{5,4},{6,7},{7,6},{8,9},{9,8},{10,11... | collective-permute-start | bytes 3145736 | tf_op jit(solution)/shard_map/ppermute | solution.py:21
  196.0 23.8 %collective-permute-start.18 = (bf16[512,1024]{1,0:T(8,128)(2,1)}, bf16[512,1024]{1,0:T(8,128)(2,1)S(1)}, u32[]{:S(2)}, u32[]{:S(2)}) collective-permute-start(bf16[512,1024]{1,0:T(8,128)(2,1)} %copy-done.6), channel_id=1, source_target_pairs={{0,6},{2,0},{4,2},{6,4},{8,10},{10,12},{12,14},{14,8},{1,7},{3,1},... | collective-permute-start | bytes 3145736 | tf_op jit(solution)/shard_map/ppermute | solution.py:464
  196.1 23.8 %collective-permute-start.17 = (bf16[512,1024]{1,0:T(8,128)(2,1)}, bf16[512,1024]{1,0:T(8,128)(2,1)}, u32[]{:S(2)}, u32[]{:S(2)}) collective-permute-start(bf16[512,1024]{1,0:T(8,128)(2,1)} %copy-done.6), channel_id=1, source_target_pairs={{0,2},{2,4},{4,6},{6,0},{8,14},{10,8},{12,10},{14,12},{1,3},{3,5},... | collective-permute-start | bytes 3145736 | tf_op jit(solution)/shard_map/ppermute | solution.py:464
  199.7 35.4 %collective-permute-start.21 = (bf16[8,512,512]{2,1,0:T(8,128)(2,1)}, bf16[8,512,512]{2,1,0:T(8,128)(2,1)}, u32[]{:S(2)}, u32[]{:S(2)}) collective-permute-start(bf16[8,512,512]{2,1,0:T(8,128)(2,1)} %get-tuple-element.72), channel_id=1, source_target_pairs={{0,8},{8,0},{1,9},{9,1},{2,10},{10,2},{3,11},{11,3},{4,12},{12,4},... | collective-permute-start | bytes 12582920 | tf_op jit(solution)/shard_map/ppermute | solution.py:21
  230.1 9.0 %collective-permute-start.22 = (bf16[8,512,512]{2,1,0:T(8,128)(2,1)}, bf16[8,512,512]{2,1,0:T(8,128)(2,1)}, u32[]{:S(2)}, u32[]{:S(2)}) collective-permute-start(bf16[8,512,512]{2,1,0:T(8,128)(2,1)} %get-tuple-element.73), channel_id=1, source_target_pairs={{0,8},{8,0},{1,9},{9,1},{2,10},{10,2},{3,11},{11,3},{4,12},{12,4},... | collective-permute-start | bytes 12582920 | tf_op jit(solution)/shard_map/ppermute | solution.py:21
  234.6 4.4 %collective-permute-start.20 = (bf16[512,1024]{1,0:T(8,128)(2,1)}, bf16[512,1024]{1,0:T(8,128)(2,1)S(1)}, u32[]{:S(2)}, u32[]{:S(2)}) collective-permute-start(bf16[512,1024]{1,0:T(8,128)(2,1)} %get-tuple-element.70.gradient), channel_id=1, source_target_pairs={{0,8},{8,0},{1,9},{9,1},{2,10},{10,2},{3,11},{11,3},{4,12},{12,4},... | collective-permute-start | bytes 3145736 | tf_op jit(solution)/shard_map/ppermute | solution.py:21
  249.8 30.4 %collective-permute-start.23 = (bf16[2,512,512]{2,1,0:T(8,128)(2,1)}, bf16[2,512,512]{2,1,0:T(8,128)(2,1)S(1)}, u32[]{:S(2)}, u32[]{:S(2)}) collective-permute-start(bf16[2,512,512]{2,1,0:T(8,128)(2,1)} %get-tuple-element.74), channel_id=1, source_target_pairs={{0,32},{32,64},{64,96},{96,0},{1,33},{33,65},{65,97},{97,1},{2,34}... | collective-permute-start | bytes 3145736 | tf_op jit(solution)/shard_map/ppermute | solution.py:21
  251.9 28.4 %collective-permute-start.24 = (bf16[2,512,512]{2,1,0:T(8,128)(2,1)}, bf16[2,512,512]{2,1,0:T(8,128)(2,1)S(1)}, u32[]{:S(2)}, u32[]{:S(2)}) collective-permute-start(bf16[2,512,512]{2,1,0:T(8,128)(2,1)} %get-tuple-element.75), channel_id=1, source_target_pairs={{0,96},{32,0},{64,32},{96,64},{1,97},{33,1},{65,33},{97,65},{2,98}... | collective-permute-start | bytes 3145736 | tf_op jit(solution)/shard_map/ppermute | solution.py:21
  260.4 13.9 %collective-permute-start.25 = (bf16[1,512,512]{2,1,0:T(8,128)(2,1)}, bf16[1,512,512]{2,1,0:T(8,128)(2,1)S(1)}, u32[]{:S(2)}, u32[]{:S(2)}) collective-permute-start(bf16[1,512,512]{2,1,0:T(8,128)(2,1)} %terms.5), channel_id=1, source_target_pairs={{0,16},{16,0},{1,17},{17,1},{2,18},{18,2},{3,19},{19,3},{4,20},{20... | collective-permute-start | bytes 1572872 | tf_op jit(solution)/shard_map/ppermute | solution.py:21
  280.5 12.9 %collective-permute-start.27 = (bf16[1,512,512]{2,1,0:T(8,128)(2,1)S(1)}, bf16[1,512,512]{2,1,0:T(8,128)(2,1)S(1)}, u32[]{:S(2)}, u32[]{:S(2)}) collective-permute-start(bf16[1,512,512]{2,1,0:T(8,128)(2,1)S(1)} %add_convert_fusion), channel_id=1, source_target_pairs={{0,16},{16,0},{1,17},{17,1},{2,18},{18,2},{3,19},{19,3},{4,20},{20... | collective-permute-start | bytes 1572872 | tf_op jit(solution)/shard_map/ppermute | solution.py:21
  281.1 14.2 %collective-permute-start.26 = (bf16[1,512,512]{2,1,0:T(8,128)(2,1)}, bf16[1,512,512]{2,1,0:T(8,128)(2,1)S(1)}, u32[]{:S(2)}, u32[]{:S(2)}) collective-permute-start(bf16[1,512,512]{2,1,0:T(8,128)(2,1)} %terms.7), channel_id=1, source_target_pairs={{0,64},{32,96},{64,0},{96,32},{1,65},{33,97},{65,1},{97,33},{2,66}... | collective-permute-start | bytes 1572872 | tf_op jit(solution)/shard_map/ppermute | solution.py:21
  (20 other events, 124.2 us)

commit v4 on v3

--- a/solution.py
+++ b/solution.py
@@ -224,7 +224,7 @@
             ],
         ),
         input_output_aliases=aliases,
-        compiler_params=pltpu.CompilerParams(vmem_limit_bytes=VMEM_LIMIT),
+        compiler_params=pltpu.CompilerParams(vmem_limit_bytes=VMEM_LIMIT * 2 // 3),
         cost_estimate=SMALL,
     )(*operands)
 
@@ -284,7 +284,7 @@
         in_specs=[vmem] * (2 + len(key_parts)),
         out_specs=(vmem, vmem),
         scratch_shapes=[pltpu.VMEM((rows, width), jnp.bfloat16)],
-        compiler_params=pltpu.CompilerParams(vmem_limit_bytes=VMEM_LIMIT),
+        compiler_params=pltpu.CompilerParams(vmem_limit_bytes=VMEM_LIMIT // 2),
         cost_estimate=SMALL,
     )(queries, cotangent, *key_parts)
 
@@ -329,7 +329,7 @@
         ),
         in_specs=[vmem] * (2 + 2 * len(key_parts)),
         out_specs=(vmem, vmem),
-        compiler_params=pltpu.CompilerParams(vmem_limit_bytes=VMEM_LIMIT),
+        compiler_params=pltpu.CompilerParams(vmem_limit_bytes=VMEM_LIMIT // 2),
         cost_estimate=SMALL,
     )(cotangent, chances, *key_parts, *value_parts)
 
@@ -392,7 +392,7 @@
                 result_of(sum(sizes[:n]), size) for n, size in enumerate(sizes)
             ],
         ),
-        compiler_params=pltpu.CompilerParams(vmem_limit_bytes=VMEM_LIMIT),
+        compiler_params=pltpu.CompilerParams(vmem_limit_bytes=VMEM_LIMIT // 2),
         cost_estimate=SMALL,
     )(place, gradient, mine, their_gradient, *their_parts, *arrived)
 
@@ -414,7 +414,7 @@
         grid=(1,),
         in_specs=[pl.BlockSpec((1, width, depth), lambda n: (0, 0, 0))] * len(blocks),
         out_specs=pl.BlockSpec((depth, width), lambda n: (0, 0)),
-        compiler_params=pltpu.CompilerParams(vmem_limit_bytes=VMEM_LIMIT),
+        compiler_params=pltpu.CompilerParams(vmem_limit_bytes=VMEM_LIMIT // 2),
         cost_estimate=SMALL,
     )(*blocks)
 

time: 300 us -> 291 us (0.970)
  Pallas kernels: 98.1 us -> 67 us
  waiting for transfers between devices: 135 us -> 155 us
  starting transfers between devices: 56.6 us -> 60.6 us
    ppermute x17, waiting for transfers between devices: 46 us -> 59.9 us  [ring(): lax.ppermute(values, axis, [(i, (i + shift) % size) for i in range(size)])]
    pallas_call x4, Pallas kernels: 26.5 us -> 12.7 us  [weight_terms(): pl.pallas_call(functools.partial(term_kernel, len(their_parts), sizes, le...]
    pallas_call x4, Pallas kernels: 42.5 us -> 30.4 us  [project(): pl.pallas_call(functools.partial(project_kernel, hops, first, begun is No...]
    ppermute x11, waiting for transfers between devices: 29.2 us -> 35.6 us  [along(): lax.ppermute(values, ('core', 'x'), [(c * 4 + i, c * 4 + (i + steps[c]) %...]
    unnamed x46 -> x28, local copies, waits for them, and re-layouts: 7.65 us -> 5.5 us
  transfers between devices with their start and end apart: 30 -> 30, of which waited for: 17 -> 18; matrix products, arithmetic and copies ran while one was open for 1% -> 1% of each run, Pallas kernels for 26% -> 18%
where the time goes in v4:
time: 291 us; the launch traced here: 290 us
  waiting for transfers between devices  155 us (53%)
  Pallas kernels  67 us (23%)
  starting transfers between devices  60.6 us (21%)
  local copies, waits for them, and re-layouts  6.32 us (2%)
    ppermute x17, waiting for transfers between devices, ring(): lax.ppermute(values, axis, [(i, (i + shift) % size) for i in range(size)])  59.9 us
    all_to_all x1, waiting for transfers between devices, per_device(): arrived = lax.all_to_all(packets, ('z', 'ylo'), 0, 0, tiled=True)  43.1 us
    ppermute x11, waiting for transfers between devices, along(): lax.ppermute(values, ('core', 'x'), [(c * 4 + i, c * 4 + (i + steps[c]) %...  35.6 us
    ppermute x17, starting transfers between devices, ring(): lax.ppermute(values, axis, [(i, (i + shift) % size) for i in range(size)])  32.4 us
    pallas_call x4, Pallas kernels, project(): pl.pallas_call(functools.partial(project_kernel, hops, first, begun is No...  30.4 us
    pallas_call x5, Pallas kernels, copies_call(): pl.pallas_call(kernel, name=name, out_shape=jax.ShapeDtypeStruct(shape, j...  18.7 us
    ppermute x11, starting transfers between devices, along(): lax.ppermute(values, ('core', 'x'), [(c * 4 + i, c * 4 + (i + steps[c]) %...  18.6 us
    all_to_all x1, waiting for transfers between devices, send_planes(): return lax.all_to_all(tie(packets, *after), 'z', 0, 0, tiled=True)  16.2 us
  transfers between devices with their start and end apart: 30, of which 18 were waited for; matrix products, arithmetic and copies ran while one was open for 1% of the time, Pallas kernels for 18%

profile of v4, /device:TPU:6, one launch (start us, length us, event | category | flops | bytes accessed | tf_op | source)
XLA Modules:
  0.0 290.2 jit_solution(1839635534640163560)
XLA Ops:
  8.4 3.6 %collective-permute-start.2 = (s32[2,32]{1,0:T(2,128)S(1)}, s32[2,32]{1,0:T(2,128)S(1)}, u32[]{:S(2)}, u32[]{:S(2)}) collective-permute-start(s32[2,32]{1,0:T(2,128)S(1)} %pad_add_fusion.both), channel_id=1, source_target_pairs={{0,64},{32,96},{64,0},{96,32},{1,65},{33,97},{65,1},{97,33},{2,66}... | collective-permute-start | bytes 776 | tf_op jit(solution)/shard_map/ppermute | solution.py:21
  16.1 5.0 %pack.1 = bf16[32,64,1024]{2,1,0:T(8,128)(2,1)} custom-call(s32[5]{0:T(128)} %stack.23.place, s32[2,32]{1,0:T(2,128)} %copy-done.8, s32[2,32]{1,0:T(2,128)} %copy-done.11, s32[2,32]{1,0:T(2,128)} %copy-done.10, s32[2,32]{1,0:T(2,128)} %copy-done.9, bf16[16,128,1024]{2,1,0:T(8,128)(2,1)} %own.7, bf16[16,128,1024]{2,1,0:T(8,128)(2,1)} %collective-permute-done.4.across), custom_call_target="tpu_custom_call" | custom-call | flops 1 | bytes 1 | tf_op jit(solution)/shard_map/pack/pallas_call | solution.py:114
  21.1 4.6 %all-to-all-start = ((bf16[32,64,1024]{2,1,0:T(8,128)(2,1)}), bf16[32,64,1024]{2,1,0:T(8,128)(2,1)}, u32[]{:S(2)}, u32[]{:S(2)}) async-start(bf16[32,64,1024]{2,1,0:T(8,128)(2,1)} %pack.1), calls=%async_computation | async-start | bytes 8388608 | tf_op jit(solution)/shard_map/all_to_all | solution.py:486
  25.7 4.7 %planes.1 = bf16[32,64,1024]{2,1,0:T(8,128)(2,1)} custom-call(s32[5]{0:T(128)} %stack.23.place, s32[2,32]{1,0:T(2,128)} %copy-done.11, s32[2,32]{1,0:T(2,128)} %copy-done.10, s32[2,32]{1,0:T(2,128)} %copy-done.9, bf16[16,128,1024]{2,1,0:T(8,128)(2,1)} %own.7, bf16[16,128,1024]{2,1,0:T(8,128)(2,1)} %collective-permute-done.4.across), custom_call_target="tpu_custom_call" | custom-call | flops 1 | bytes 1 | tf_op jit(solution)/shard_map/planes/pallas_call | solution.py:114
  30.5 43.1 %all-to-all-done.packets = bf16[32,64,1024]{2,1,0:T(8,128)(2,1)} async-done(((bf16[32,64,1024]{2,1,0:T(8,128)(2,1)}), bf16[32,64,1024]{2,1,0:T(8,128)(2,1)}, u32[]{:S(2)}, u32[]{:S(2)}) %all-to-all-start) | async-done | bytes 4194336 | tf_op jit(solution)/shard_map/all_to_all | solution.py:486
  76.6 5.0 %all-to-all-start.1 = ((bf16[32,64,1024]{2,1,0:T(8,128)(2,1)}), bf16[32,64,1024]{2,1,0:T(8,128)(2,1)}, u32[]{:S(2)}, u32[]{:S(2)}) async-start(bf16[32,64,1024]{2,1,0:T(8,128)(2,1)} %planes.1), calls=%async_computation.1 | async-start | bytes 8388608 | tf_op jit(solution)/shard_map/all_to_all | solution.py:480
  84.9 3.2 %collective-permute-start.5 = (bf16[512,1024]{1,0:T(8,128)(2,1)S(1)}, bf16[512,1024]{1,0:T(8,128)(2,1)}, u32[]{:S(2)}, u32[]{:S(2)}) collective-permute-start(bf16[512,1024]{1,0:T(8,128)(2,1)S(1)} %bitcast.14), channel_id=1, source_target_pairs={{0,1},{1,0},{2,3},{3,2},{4,5},{5,4},{6,7},{7,6},{8,9},{9,8},{10,11... | collective-permute-start | bytes 3145736 | tf_op jit(solution)/shard_map/ppermute | solution.py:21
  88.1 17.1 %collective-permute-done.7.refs_2_ = bf16[512,1024]{1,0:T(8,128)(2,1)S(1)} collective-permute-done((bf16[512,1024]{1,0:T(8,128)(2,1)S(1)}, bf16[512,1024]{1,0:T(8,128)(2,1)S(1)}, u32[]{:S(2)}, u32[]{:S(2)}) %collective-permute-start.7) | collective-permute-done | bytes 1048608 | tf_op jit(solution)/shard_map/ppermute | solution.py:464
  111.8 16.2 %all-to-all-done.1.packets = bf16[32,64,1024]{2,1,0:T(8,128)(2,1)} async-done(((bf16[32,64,1024]{2,1,0:T(8,128)(2,1)}), bf16[32,64,1024]{2,1,0:T(8,128)(2,1)}, u32[]{:S(2)}, u32[]{:S(2)}) %all-to-all-start.1) | async-done | bytes 4194336 | tf_op jit(solution)/shard_map/all_to_all | solution.py:480
  132.5 3.6 %collective-permute-done.9.refs_5_ = bf16[512,1024]{1,0:T(8,128)(2,1)} collective-permute-done((bf16[512,1024]{1,0:T(8,128)(2,1)}, bf16[512,1024]{1,0:T(8,128)(2,1)}, u32[]{:S(2)}, u32[]{:S(2)}) %collective-permute-start.9) | collective-permute-done | bytes 1048608 | tf_op jit(solution)/shard_map/ppermute | solution.py:464
  136.1 3.4 %collective-permute-done.8.refs_4_ = bf16[512,1024]{1,0:T(8,128)(2,1)} collective-permute-done((bf16[512,1024]{1,0:T(8,128)(2,1)}, bf16[512,1024]{1,0:T(8,128)(2,1)}, u32[]{:S(2)}, u32[]{:S(2)}) %collective-permute-start.8) | collective-permute-done | bytes 1048608 | tf_op jit(solution)/shard_map/ppermute | solution.py:464
  140.5 11.9 %collective-permute-done.11.refs_0_ = bf16[8,64,1024]{2,1,0:T(8,128)(2,1)} collective-permute-done((bf16[8,64,1024]{2,1,0:T(8,128)(2,1)}, bf16[8,64,1024]{2,1,0:T(8,128)(2,1)}, u32[]{:S(2)}, u32[]{:S(2)}) %collective-permute-start.11) | collective-permute-done | bytes 1048608 | tf_op jit(solution)/shard_map/ppermute | solution.py:21
  152.5 3.1 %merge.3 = bf16[8,64,1024]{2,1,0:T(8,128)(2,1)} custom-call(s32[5]{0:T(128)} %stack.23.place, s32[2,32]{1,0:T(2,128)} %copy-done.8, bf16[16,128,1024]{2,1,0:T(8,128)(2,1)} %own.7, bf16[16,128,1024]{2,1,0:T(8,128)(2,1)} %collective-permute-done.4.across, bf16[32,64,1024]{2,1,0:T(8,128)(2,1)} %all-to-all-done.1.packets, ...), custom_call_target="tpu_custom_call" | custom-call | flops 1 | bytes 1 | tf_op jit(solution)/shard_map/merge/pallas_call | solution.py:114
  157.6 3.2 %collective-permute-start.13 = (bf16[512,1024]{1,0:T(8,128)(2,1)}, bf16[512,1024]{1,0:T(8,128)(2,1)S(1)}, u32[]{:S(2)}, u32[]{:S(2)}) collective-permute-start(bf16[512,1024]{1,0:T(8,128)(2,1)} %bitcast.10), channel_id=1, source_target_pairs={{0,1},{1,0},{2,3},{3,2},{4,5},{5,4},{6,7},{7,6},{8,9},{9,8},{10,11... | collective-permute-start | bytes 3145736 | tf_op jit(solution)/shard_map/ppermute | solution.py:21
  160.8 12.9 %project.4 = (bf16[512,512]{1,0:T(8,128)(2,1)S(1)}, bf16[8,1024,512]{2,1,0:T(8,128)(2,1)}, bf16[8,512,512]{2,1,0:T(8,128)(2,1)}, bf16[512,512]{1,0:T(8,128)(2,1)S(1)}) custom-call(s32[5]{0:T(128)S(1)} %copy-done.7, bf16[512,1024]{1,0:T(8,128)(2,1)S(1)} %bitcast.15, bf16[512,1024]{1,0:T(8,128)(2,1)S(1)} %collective-permute-done.6.refs_1_, ...), custom_call_target="tpu_custom_call" | custom-call | flops 1 | bytes 1 | tf_op jit(solution)/shard_map/project/pallas_call | solution.py:203
  176.7 3.6 %collective-permute-start.16 = (bf16[512,1024]{1,0:T(8,128)(2,1)S(1)}, bf16[512,1024]{1,0:T(8,128)(2,1)S(1)}, u32[]{:S(2)}, u32[]{:S(2)}) collective-permute-start(bf16[512,1024]{1,0:T(8,128)(2,1)S(1)} %collective-permute-done.14.refs_1_), channel_id=1, source_target_pairs={{0,2},{2,4},{4,6},{6,0},{8,14},{10,8},{12,10},{14,12},{1,3},{3,5},... | collective-permute-start | bytes 3145736 | tf_op jit(solution)/shard_map/ppermute | solution.py:464
  180.3 8.0 %project.5 = (f32[512,512]{1,0:T(8,128)S(1)}, bf16[8,1024,512]{2,1,0:T(8,128)(2,1)}, bf16[8,512,512]{2,1,0:T(8,128)(2,1)S(1)}, f32[512,512]{1,0:T(8,128)S(1)}) custom-call(s32[5]{0:T(128)S(1)} %copy-done.7, bf16[512,1024]{1,0:T(8,128)(2,1)S(1)} %bitcast.11, bf16[512,1024]{1,0:T(8,128)(2,1)S(1)} %collective-permute-done.14.refs_1_, ...), custom_call_target="tpu_custom_call", output_to_operand_aliasing={{1}: (7, {})} | custom-call | flops 1 | bytes 1 | tf_op jit(solution)/shard_map/project/pallas_call | solution.py:203
  188.3 4.3 %collective-permute-done.16.refs_0_ = bf16[512,1024]{1,0:T(8,128)(2,1)S(1)} collective-permute-done((bf16[512,1024]{1,0:T(8,128)(2,1)S(1)}, bf16[512,1024]{1,0:T(8,128)(2,1)S(1)}, u32[]{:S(2)}, u32[]{:S(2)}) %collective-permute-start.16) | collective-permute-done | bytes 1048608 | tf_op jit(solution)/shard_map/ppermute | solution.py:464
  192.6 4.4 %collective-permute-start.19 = (bf16[512,1024]{1,0:T(8,128)(2,1)S(1)}, bf16[512,1024]{1,0:T(8,128)(2,1)S(1)}, u32[]{:S(2)}, u32[]{:S(2)}) collective-permute-start(bf16[512,1024]{1,0:T(8,128)(2,1)S(1)} %collective-permute-done.16.refs_0_), channel_id=1, source_target_pairs={{0,1},{1,0},{2,3},{3,2},{4,5},{5,4},{6,7},{7,6},{8,9},{9,8},{10,11... | collective-permute-start | bytes 3145736 | tf_op jit(solution)/shard_map/ppermute | solution.py:21
  196.9 3.7 %collective-permute-start.17 = (bf16[512,1024]{1,0:T(8,128)(2,1)S(1)}, bf16[512,1024]{1,0:T(8,128)(2,1)S(1)}, u32[]{:S(2)}, u32[]{:S(2)}) collective-permute-start(bf16[512,1024]{1,0:T(8,128)(2,1)S(1)} %collective-permute-done.13.refs_3_), channel_id=1, source_target_pairs={{0,2},{2,4},{4,6},{6,0},{8,14},{10,8},{12,10},{14,12},{1,3},{3,5},... | collective-permute-start | bytes 3145736 | tf_op jit(solution)/shard_map/ppermute | solution.py:464
  200.6 3.6 %project.6 = (f32[512,512]{1,0:T(8,128)S(1)}, bf16[8,1024,512]{2,1,0:T(8,128)(2,1)}, bf16[8,512,512]{2,1,0:T(8,128)(2,1)S(1)}, f32[512,512]{1,0:T(8,128)S(1)}) custom-call(s32[5]{0:T(128)S(1)} %copy-done.7, bf16[512,1024]{1,0:T(8,128)(2,1)S(1)} %collective-permute-done.16.refs_0_, ...), custom_call_target="tpu_custom_call", output_to_operand_aliasing={{1}: (6, {}), {2}: (7, {})} | custom-call | flops 1 | bytes 1 | tf_op jit(solution)/shard_map/project/pallas_call | solution.py:203
  204.2 11.6 %collective-permute-done.19.refs_2_ = bf16[512,1024]{1,0:T(8,128)(2,1)S(1)} collective-permute-done((bf16[512,1024]{1,0:T(8,128)(2,1)S(1)}, bf16[512,1024]{1,0:T(8,128)(2,1)S(1)}, u32[]{:S(2)}, u32[]{:S(2)}) %collective-permute-start.19) | collective-permute-done | bytes 1048608 | tf_op jit(solution)/shard_map/ppermute | solution.py:21
  215.9 4.3 %collective-permute-done.18.refs_1_ = bf16[512,1024]{1,0:T(8,128)(2,1)S(1)} collective-permute-done((bf16[512,1024]{1,0:T(8,128)(2,1)S(1)}, bf16[512,1024]{1,0:T(8,128)(2,1)S(1)}, u32[]{:S(2)}, u32[]{:S(2)}) %collective-permute-start.18) | collective-permute-done | bytes 1048608 | tf_op jit(solution)/shard_map/ppermute | solution.py:464
  220.1 6.0 %project.7 = (bf16[512,512]{1,0:T(8,128)(2,1)S(1)}, bf16[8,1024,512]{2,1,0:T(8,128)(2,1)}, bf16[8,512,512]{2,1,0:T(8,128)(2,1)S(1)}, bf16[512,512]{1,0:T(8,128)(2,1)S(1)}) custom-call(s32[5]{0:T(128)S(1)} %copy-done.7, bf16[512,1024]{1,0:T(8,128)(2,1)S(1)} %collective-permute-done.17.refs_0_, ...), custom_call_target="tpu_custom_call", output_to_operand_aliasing={{1}: (8, {}), {2}: (9, {})} | custom-call | flops 1 | bytes 1 | tf_op jit(solution)/shard_map/project/pallas_call | solution.py:203
  228.9 6.0 %collective-permute-done.20.their_gradient = bf16[512,1024]{1,0:T(8,128)(2,1)S(1)} collective-permute-done((bf16[512,1024]{1,0:T(8,128)(2,1)S(1)}, bf16[512,1024]{1,0:T(8,128)(2,1)S(1)}, u32[]{:S(2)}, u32[]{:S(2)}) %collective-permute-start.20) | collective-permute-done | bytes 1048608 | tf_op jit(solution)/shard_map/ppermute | solution.py:21
  234.9 3.4 %copy-done = bf16[8,1024,512]{2,1,0:T(8,128)(2,1)S(1)} copy-done((bf16[8,1024,512]{2,1,0:T(8,128)(2,1)S(1)}, bf16[8,1024,512]{2,1,0:T(8,128)(2,1)}, u32[]{:S(2)}) %copy-start) | copy-done | bytes 8388632
  238.3 5.8 %terms.4 = (bf16[2,512,512]{2,1,0:T(8,128)(2,1)S(1)}, bf16[2,512,512]{2,1,0:T(8,128)(2,1)S(1)}) custom-call(s32[5]{0:T(128)S(1)} %copy-done.7, bf16[512,1024]{1,0:T(8,128)(2,1)S(1)} %get-tuple-element.70.gradient, bf16[8,1024,512]{2,1,0:T(8,128)(2,1)S(1)} %copy-done, bf16[512,1024]{1,0:T(8,128)(2,1)S(1)} %collective-permute-done.20.their_gradient, ...), custom_call_target="tpu_custom_call" | custom-call | flops 1 | bytes 1 | tf_op jit(solution)/shard_map/terms/pallas_call | solution.py:381
  251.6 3.2 %terms.6 = (bf16[1,512,512]{2,1,0:T(8,128)(2,1)S(1)}, bf16[1,512,512]{2,1,0:T(8,128)(2,1)S(1)}) custom-call(s32[5]{0:T(128)S(1)} %copy-done.7, bf16[512,1024]{1,0:T(8,128)(2,1)S(1)} %get-tuple-element.70.gradient, bf16[8,1024,512]{2,1,0:T(8,128)(2,1)S(1)} %copy-done, bf16[512,1024]{1,0:T(8,128)(2,1)S(1)} %collective-permute-done.20.their_gradient, ...), custom_call_target="tpu_custom_call" | custom-call | flops 1 | bytes 1 | tf_op jit(solution)/shard_map/terms/pallas_call | solution.py:381
  254.8 8.7 %collective-permute-done.25.refs_2_ = bf16[1,512,512]{2,1,0:T(8,128)(2,1)S(1)} collective-permute-done((bf16[1,512,512]{2,1,0:T(8,128)(2,1)S(1)}, bf16[1,512,512]{2,1,0:T(8,128)(2,1)S(1)}, u32[]{:S(2)}, u32[]{:S(2)}) %collective-permute-start.25) | collective-permute-done | bytes 524320 | tf_op jit(solution)/shard_map/ppermute | solution.py:21
  265.4 5.3 %collective-permute-done.23.refs_0_ = bf16[2,512,512]{2,1,0:T(8,128)(2,1)S(1)} collective-permute-done((bf16[2,512,512]{2,1,0:T(8,128)(2,1)S(1)}, bf16[2,512,512]{2,1,0:T(8,128)(2,1)S(1)}, u32[]{:S(2)}, u32[]{:S(2)}) %collective-permute-start.23) | collective-permute-done | bytes 1048608 | tf_op jit(solution)/shard_map/ppermute | solution.py:21
  270.9 3.9 %collective-permute-start.27 = (bf16[1,512,512]{2,1,0:T(8,128)(2,1)S(1)}, bf16[1,512,512]{2,1,0:T(8,128)(2,1)S(1)}, u32[]{:S(2)}, u32[]{:S(2)}) collective-permute-start(bf16[1,512,512]{2,1,0:T(8,128)(2,1)S(1)} %add_convert_fusion), channel_id=1, source_target_pairs={{0,16},{16,0},{1,17},{17,1},{2,18},{18,2},{3,19},{19,3},{4,20},{20... | collective-permute-start | bytes 1572872 | tf_op jit(solution)/shard_map/ppermute | solution.py:21
  278.1 7.8 %collective-permute-done.27.refs_4_ = bf16[1,512,512]{2,1,0:T(8,128)(2,1)S(1)} collective-permute-done((bf16[1,512,512]{2,1,0:T(8,128)(2,1)S(1)}, bf16[1,512,512]{2,1,0:T(8,128)(2,1)S(1)}, u32[]{:S(2)}, u32[]{:S(2)}) %collective-permute-start.27) | collective-permute-done | bytes 524320 | tf_op jit(solution)/shard_map/ppermute | solution.py:21
  (82 shorter events, 55.3 us)
Async XLA Ops:
  0.6 14.9 %collective-permute-start.4 = (bf16[16,128,1024]{2,1,0:T(8,128)(2,1)}, bf16[16,128,1024]{2,1,0:T(8,128)(2,1)}, u32[]{:S(2)}, u32[]{:S(2)}) collective-permute-start(bf16[16,128,1024]{2,1,0:T(8,128)(2,1)} %own.7), channel_id=1, source_target_pairs={{0,8},{8,0},{1,9},{9,1},{2,10},{10,2},{3,11},{11,3},{4,12},{12,4},... | collective-permute-start | bytes 12582920 | tf_op jit(solution)/shard_map/ppermute | solution.py:21
  2.8 3.6 %collective-permute-start = (s32[1,32]{1,0:T(1,128)S(1)}, s32[1,32]{1,0:T(1,128)S(1)}, u32[]{:S(2)}, u32[]{:S(2)}) collective-permute-start(s32[1,32]{1,0:T(1,128)S(1)} %pad_add_fusion.1.wanted), channel_id=1, source_target_pairs={{0,16},{16,0},{1,17},{17,1},{2,18},{18,2},{3,19},{19,3},{4,20},{20... | collective-permute-start | bytes 392 | tf_op jit(solution)/shard_map/ppermute | solution.py:21
  6.5 7.1 %collective-permute-start.3 = (s32[2,32]{1,0:T(2,128)S(1)}, s32[2,32]{1,0:T(2,128)S(1)}, u32[]{:S(2)}, u32[]{:S(2)}) collective-permute-start(s32[2,32]{1,0:T(2,128)S(1)} %pad_add_fusion.both), channel_id=1, source_target_pairs={{0,32},{32,64},{64,96},{96,0},{1,33},{33,65},{65,97},{97,1},{2,34}... | collective-permute-start | bytes 776 | tf_op jit(solution)/shard_map/ppermute | solution.py:21
  8.4 5.2 %collective-permute-start.2 = (s32[2,32]{1,0:T(2,128)S(1)}, s32[2,32]{1,0:T(2,128)S(1)}, u32[]{:S(2)}, u32[]{:S(2)}) collective-permute-start(s32[2,32]{1,0:T(2,128)S(1)} %pad_add_fusion.both), channel_id=1, source_target_pairs={{0,64},{32,96},{64,0},{96,32},{1,65},{33,97},{65,1},{97,33},{2,66}... | collective-permute-start | bytes 776 | tf_op jit(solution)/shard_map/ppermute | solution.py:21
  12.0 3.6 %collective-permute-start.1 = (s32[2,32]{1,0:T(2,128)S(1)}, s32[2,32]{1,0:T(2,128)S(1)}, u32[]{:S(2)}, u32[]{:S(2)}) collective-permute-start(s32[2,32]{1,0:T(2,128)S(1)} %pad_add_fusion.both), channel_id=1, source_target_pairs={{0,96},{32,0},{64,32},{96,64},{1,97},{33,1},{65,33},{97,65},{2,98}... | collective-permute-start | bytes 776 | tf_op jit(solution)/shard_map/ppermute | solution.py:21
  21.1 52.5 %all-to-all-start = ((bf16[32,64,1024]{2,1,0:T(8,128)(2,1)}), bf16[32,64,1024]{2,1,0:T(8,128)(2,1)}, u32[]{:S(2)}, u32[]{:S(2)}) async-start(bf16[32,64,1024]{2,1,0:T(8,128)(2,1)} %pack.1), calls=%async_computation | async-start | bytes 8388608 | tf_op jit(solution)/shard_map/all_to_all | solution.py:486
  76.6 51.3 %all-to-all-start.1 = ((bf16[32,64,1024]{2,1,0:T(8,128)(2,1)}), bf16[32,64,1024]{2,1,0:T(8,128)(2,1)}, u32[]{:S(2)}, u32[]{:S(2)}) async-start(bf16[32,64,1024]{2,1,0:T(8,128)(2,1)} %planes.1), calls=%async_computation.1 | async-start | bytes 8388608 | tf_op jit(solution)/shard_map/all_to_all | solution.py:480
  81.6 23.6 %collective-permute-start.7 = (bf16[512,1024]{1,0:T(8,128)(2,1)S(1)}, bf16[512,1024]{1,0:T(8,128)(2,1)S(1)}, u32[]{:S(2)}, u32[]{:S(2)}) collective-permute-start(bf16[512,1024]{1,0:T(8,128)(2,1)S(1)} %bitcast.12), channel_id=1, source_target_pairs={{0,6},{2,0},{4,2},{6,4},{8,10},{10,12},{12,14},{14,8},{1,7},{3,1},... | collective-permute-start | bytes 3145736 | tf_op jit(solution)/shard_map/ppermute | solution.py:464
  82.5 22.7 %collective-permute-start.6 = (bf16[512,1024]{1,0:T(8,128)(2,1)S(1)}, bf16[512,1024]{1,0:T(8,128)(2,1)S(1)}, u32[]{:S(2)}, u32[]{:S(2)}) collective-permute-start(bf16[512,1024]{1,0:T(8,128)(2,1)S(1)} %bitcast.13), channel_id=1, source_target_pairs={{0,2},{2,4},{4,6},{6,0},{8,14},{10,8},{12,10},{14,12},{1,3},{3,5},... | collective-permute-start | bytes 3145736 | tf_op jit(solution)/shard_map/ppermute | solution.py:464
  84.9 21.9 %collective-permute-start.5 = (bf16[512,1024]{1,0:T(8,128)(2,1)S(1)}, bf16[512,1024]{1,0:T(8,128)(2,1)}, u32[]{:S(2)}, u32[]{:S(2)}) collective-permute-start(bf16[512,1024]{1,0:T(8,128)(2,1)S(1)} %bitcast.14), channel_id=1, source_target_pairs={{0,1},{1,0},{2,3},{3,2},{4,5},{5,4},{6,7},{7,6},{8,9},{9,8},{10,11... | collective-permute-start | bytes 3145736 | tf_op jit(solution)/shard_map/ppermute | solution.py:21
  106.8 25.7 %collective-permute-start.10 = (bf16[512,1024]{1,0:T(8,128)(2,1)S(1)}, bf16[512,1024]{1,0:T(8,128)(2,1)}, u32[]{:S(2)}, u32[]{:S(2)}) collective-permute-start(bf16[512,1024]{1,0:T(8,128)(2,1)S(1)} %collective-permute-done.6.refs_1_), channel_id=1, source_target_pairs={{0,2},{2,4},{4,6},{6,0},{8,14},{10,8},{12,10},{14,12},{1,3},{3,5},... | collective-permute-start | bytes 3145736 | tf_op jit(solution)/shard_map/ppermute | solution.py:464
  108.5 27.6 %collective-permute-start.9 = (bf16[512,1024]{1,0:T(8,128)(2,1)}, bf16[512,1024]{1,0:T(8,128)(2,1)}, u32[]{:S(2)}, u32[]{:S(2)}) collective-permute-start(bf16[512,1024]{1,0:T(8,128)(2,1)} %collective-permute-done.5.refs_3_), channel_id=1, source_target_pairs={{0,6},{2,0},{4,2},{6,4},{8,10},{10,12},{12,14},{14,8},{1,7},{3,1},... | collective-permute-start | bytes 3145736 | tf_op jit(solution)/shard_map/ppermute | solution.py:464
  108.9 30.7 %collective-permute-start.8 = (bf16[512,1024]{1,0:T(8,128)(2,1)}, bf16[512,1024]{1,0:T(8,128)(2,1)}, u32[]{:S(2)}, u32[]{:S(2)}) collective-permute-start(bf16[512,1024]{1,0:T(8,128)(2,1)} %collective-permute-done.5.refs_3_), channel_id=1, source_target_pairs={{0,2},{2,4},{4,6},{6,0},{8,14},{10,8},{12,10},{14,12},{1,3},{3,5},... | collective-permute-start | bytes 3145736 | tf_op jit(solution)/shard_map/ppermute | solution.py:464
  130.8 30.0 %copy-start.7 = (s32[5]{0:T(128)S(1)}, s32[5]{0:T(128)}, u32[]{:S(2)}) copy-start(s32[5]{0:T(128)} %stack.23.place) | copy-start | bytes 64
  130.9 21.6 %collective-permute-start.11 = (bf16[8,64,1024]{2,1,0:T(8,128)(2,1)}, bf16[8,64,1024]{2,1,0:T(8,128)(2,1)}, u32[]{:S(2)}, u32[]{:S(2)}) collective-permute-start(bf16[8,64,1024]{2,1,0:T(8,128)(2,1)} %hand.1), channel_id=1, source_target_pairs={{0,16},{16,0},{1,17},{17,1},{2,18},{18,2},{3,19},{19,3},{4,20},{20... | collective-permute-start | bytes 3145736 | tf_op jit(solution)/shard_map/ppermute | solution.py:21
  139.5 21.3 %collective-permute-start.12 = (bf16[512,1024]{1,0:T(8,128)(2,1)}, bf16[512,1024]{1,0:T(8,128)(2,1)}, u32[]{:S(2)}, u32[]{:S(2)}) collective-permute-start(bf16[512,1024]{1,0:T(8,128)(2,1)} %collective-permute-done.9.refs_5_), channel_id=1, source_target_pairs={{0,6},{2,0},{4,2},{6,4},{8,10},{10,12},{12,14},{14,8},{1,7},{3,1},... | collective-permute-start | bytes 3145736 | tf_op jit(solution)/shard_map/ppermute | solution.py:464
  155.5 24.8 %copy-start.1 = (bf16[8,64,1024]{2,1,0:T(8,128)(2,1)S(1)}, bf16[8,64,1024]{2,1,0:T(8,128)(2,1)}, u32[]{:S(2)}) copy-start(bf16[8,64,1024]{2,1,0:T(8,128)(2,1)} %merge.3) | copy-start | bytes 3145732
  155.5 21.2 %collective-permute-start.14 = (bf16[512,1024]{1,0:T(8,128)(2,1)}, bf16[512,1024]{1,0:T(8,128)(2,1)S(1)}, u32[]{:S(2)}, u32[]{:S(2)}) collective-permute-start(bf16[512,1024]{1,0:T(8,128)(2,1)} %bitcast.8), channel_id=1, source_target_pairs={{0,2},{2,4},{4,6},{6,0},{8,14},{10,8},{12,10},{14,12},{1,3},{3,5},... | collective-permute-start | bytes 3145736 | tf_op jit(solution)/shard_map/ppermute | solution.py:464
  156.1 24.2 %collective-permute-start.15 = (bf16[512,1024]{1,0:T(8,128)(2,1)}, bf16[512,1024]{1,0:T(8,128)(2,1)S(1)}, u32[]{:S(2)}, u32[]{:S(2)}) collective-permute-start(bf16[512,1024]{1,0:T(8,128)(2,1)} %bitcast.9), channel_id=1, source_target_pairs={{0,6},{2,0},{4,2},{6,4},{8,10},{10,12},{12,14},{14,8},{1,7},{3,1},... | collective-permute-start | bytes 3145736 | tf_op jit(solution)/shard_map/ppermute | solution.py:464
  157.6 22.7 %collective-permute-start.13 = (bf16[512,1024]{1,0:T(8,128)(2,1)}, bf16[512,1024]{1,0:T(8,128)(2,1)S(1)}, u32[]{:S(2)}, u32[]{:S(2)}) collective-permute-start(bf16[512,1024]{1,0:T(8,128)(2,1)} %bitcast.10), channel_id=1, source_target_pairs={{0,1},{1,0},{2,3},{3,2},{4,5},{5,4},{6,7},{7,6},{8,9},{9,8},{10,11... | collective-permute-start | bytes 3145736 | tf_op jit(solution)/shard_map/ppermute | solution.py:21
  176.7 15.9 %collective-permute-start.16 = (bf16[512,1024]{1,0:T(8,128)(2,1)S(1)}, bf16[512,1024]{1,0:T(8,128)(2,1)S(1)}, u32[]{:S(2)}, u32[]{:S(2)}) collective-permute-start(bf16[512,1024]{1,0:T(8,128)(2,1)S(1)} %collective-permute-done.14.refs_1_), channel_id=1, source_target_pairs={{0,2},{2,4},{4,6},{6,0},{8,14},{10,8},{12,10},{14,12},{1,3},{3,5},... | collective-permute-start | bytes 3145736 | tf_op jit(solution)/shard_map/ppermute | solution.py:464
  192.6 23.3 %collective-permute-start.19 = (bf16[512,1024]{1,0:T(8,128)(2,1)S(1)}, bf16[512,1024]{1,0:T(8,128)(2,1)S(1)}, u32[]{:S(2)}, u32[]{:S(2)}) collective-permute-start(bf16[512,1024]{1,0:T(8,128)(2,1)S(1)} %collective-permute-done.16.refs_0_), channel_id=1, source_target_pairs={{0,1},{1,0},{2,3},{3,2},{4,5},{5,4},{6,7},{7,6},{8,9},{9,8},{10,11... | collective-permute-start | bytes 3145736 | tf_op jit(solution)/shard_map/ppermute | solution.py:21
  196.9 23.2 %collective-permute-start.18 = (bf16[512,1024]{1,0:T(8,128)(2,1)S(1)}, bf16[512,1024]{1,0:T(8,128)(2,1)S(1)}, u32[]{:S(2)}, u32[]{:S(2)}) collective-permute-start(bf16[512,1024]{1,0:T(8,128)(2,1)S(1)} %collective-permute-done.13.refs_3_), channel_id=1, source_target_pairs={{0,6},{2,0},{4,2},{6,4},{8,10},{10,12},{12,14},{14,8},{1,7},{3,1},... | collective-permute-start | bytes 3145736 | tf_op jit(solution)/shard_map/ppermute | solution.py:464
  196.9 23.2 %collective-permute-start.17 = (bf16[512,1024]{1,0:T(8,128)(2,1)S(1)}, bf16[512,1024]{1,0:T(8,128)(2,1)S(1)}, u32[]{:S(2)}, u32[]{:S(2)}) collective-permute-start(bf16[512,1024]{1,0:T(8,128)(2,1)S(1)} %collective-permute-done.13.refs_3_), channel_id=1, source_target_pairs={{0,2},{2,4},{4,6},{6,0},{8,14},{10,8},{12,10},{14,12},{1,3},{3,5},... | collective-permute-start | bytes 3145736 | tf_op jit(solution)/shard_map/ppermute | solution.py:464
  200.6 28.2 %collective-permute-start.21 = (bf16[8,512,512]{2,1,0:T(8,128)(2,1)}, bf16[8,512,512]{2,1,0:T(8,128)(2,1)S(1)}, u32[]{:S(2)}, u32[]{:S(2)}) collective-permute-start(bf16[8,512,512]{2,1,0:T(8,128)(2,1)} %get-tuple-element.72), channel_id=1, source_target_pairs={{0,8},{8,0},{1,9},{9,1},{2,10},{10,2},{3,11},{11,3},{4,12},{12,4},... | collective-permute-start | bytes 12582920 | tf_op jit(solution)/shard_map/ppermute | solution.py:21
  226.1 8.7 %collective-permute-start.22 = (bf16[8,512,512]{2,1,0:T(8,128)(2,1)S(1)}, bf16[8,512,512]{2,1,0:T(8,128)(2,1)S(1)}, u32[]{:S(2)}, u32[]{:S(2)}) collective-permute-start(bf16[8,512,512]{2,1,0:T(8,128)(2,1)S(1)} %get-tuple-element.73), channel_id=1, source_target_pairs={{0,8},{8,0},{1,9},{9,1},{2,10},{10,2},{3,11},{11,3},{4,12},{12,4},... | collective-permute-start | bytes 12582920 | tf_op jit(solution)/shard_map/ppermute | solution.py:21
  228.3 6.6 %collective-permute-start.20 = (bf16[512,1024]{1,0:T(8,128)(2,1)S(1)}, bf16[512,1024]{1,0:T(8,128)(2,1)S(1)}, u32[]{:S(2)}, u32[]{:S(2)}) collective-permute-start(bf16[512,1024]{1,0:T(8,128)(2,1)S(1)} %get-tuple-element.70.gradient), channel_id=1, source_target_pairs={{0,8},{8,0},{1,9},{9,1},{2,10},{10,2},{3,11},{11,3},{4,12},{12,4},... | collective-permute-start | bytes 3145736 | tf_op jit(solution)/shard_map/ppermute | solution.py:21
  244.1 26.6 %collective-permute-start.23 = (bf16[2,512,512]{2,1,0:T(8,128)(2,1)S(1)}, bf16[2,512,512]{2,1,0:T(8,128)(2,1)S(1)}, u32[]{:S(2)}, u32[]{:S(2)}) collective-permute-start(bf16[2,512,512]{2,1,0:T(8,128)(2,1)S(1)} %get-tuple-element.74), channel_id=1, source_target_pairs={{0,32},{32,64},{64,96},{96,0},{1,33},{33,65},{65,97},{97,1},{2,34}... | collective-permute-start | bytes 3145736 | tf_op jit(solution)/shard_map/ppermute | solution.py:21
  245.5 25.2 %collective-permute-start.24 = (bf16[2,512,512]{2,1,0:T(8,128)(2,1)S(1)}, bf16[2,512,512]{2,1,0:T(8,128)(2,1)S(1)}, u32[]{:S(2)}, u32[]{:S(2)}) collective-permute-start(bf16[2,512,512]{2,1,0:T(8,128)(2,1)S(1)} %get-tuple-element.75), channel_id=1, source_target_pairs={{0,96},{32,0},{64,32},{96,64},{1,97},{33,1},{65,33},{97,65},{2,98}... | collective-permute-start | bytes 3145736 | tf_op jit(solution)/shard_map/ppermute | solution.py:21
  249.2 14.4 %collective-permute-start.25 = (bf16[1,512,512]{2,1,0:T(8,128)(2,1)S(1)}, bf16[1,512,512]{2,1,0:T(8,128)(2,1)S(1)}, u32[]{:S(2)}, u32[]{:S(2)}) collective-permute-start(bf16[1,512,512]{2,1,0:T(8,128)(2,1)S(1)} %terms.5), channel_id=1, source_target_pairs={{0,16},{16,0},{1,17},{17,1},{2,18},{18,2},{3,19},{19,3},{4,20},{20... | collective-permute-start | bytes 1572872 | tf_op jit(solution)/shard_map/ppermute | solution.py:21
  270.9 14.9 %collective-permute-start.27 = (bf16[1,512,512]{2,1,0:T(8,128)(2,1)S(1)}, bf16[1,512,512]{2,1,0:T(8,128)(2,1)S(1)}, u32[]{:S(2)}, u32[]{:S(2)}) collective-permute-start(bf16[1,512,512]{2,1,0:T(8,128)(2,1)S(1)} %add_convert_fusion), channel_id=1, source_target_pairs={{0,16},{16,0},{1,17},{17,1},{2,18},{18,2},{3,19},{19,3},{4,20},{20... | collective-permute-start | bytes 1572872 | tf_op jit(solution)/shard_map/ppermute | solution.py:21
  274.8 14.0 %collective-permute-start.26 = (bf16[1,512,512]{2,1,0:T(8,128)(2,1)S(1)}, bf16[1,512,512]{2,1,0:T(8,128)(2,1)S(1)}, u32[]{:S(2)}, u32[]{:S(2)}) collective-permute-start(bf16[1,512,512]{2,1,0:T(8,128)(2,1)S(1)} %terms.7), channel_id=1, source_target_pairs={{0,64},{32,96},{64,0},{96,32},{1,65},{33,97},{65,1},{97,33},{2,66}... | collective-permute-start | bytes 1572872 | tf_op jit(solution)/shard_map/ppermute | solution.py:21
  (11 other events, 88.6 us)

commit v5 on v4

--- a/solution.py
+++ b/solution.py
@@ -334,10 +334,50 @@
     )(cotangent, chances, *key_parts, *value_parts)
 
 
-def term_kernel(chunks, sizes, adds, place, gradient, mine, their_gradient, *refs):
+def own_kernel(place, gradient, mine, output):
+    output[0] = jnp.dot(gradient[...], mine[0], preferred_element_type=jnp.float32).astype(
+        jnp.bfloat16
+    )
+
+
+def own_terms(place, targets, gradient, mine):
+    count = len(targets)
+    width, rows = gradient.shape
+    half = mine.shape[2]
+    return pl.pallas_call(
+        own_kernel,
+        name="own",
+        out_shape=jax.ShapeDtypeStruct((count, width, half), jnp.bfloat16),
+        grid_spec=pltpu.PrefetchScalarGridSpec(
+            num_scalar_prefetch=1,
+            grid=(count,),
+            in_specs=[
+                pl.BlockSpec((width, rows), lambda n, place: (0, 0)),
+                pl.BlockSpec((1, rows, half), functools.partial(block_of, targets)),
+            ],
+            out_specs=pl.BlockSpec((1, width, half), lambda n, place: (n, 0, 0)),
+        ),
+        compiler_params=pltpu.CompilerParams(vmem_limit_bytes=VMEM_LIMIT // 2),
+        cost_estimate=SMALL,
+    )(place, gradient, mine)
+
+
+def block_of(targets, n, place):
+    dz, dy = jnp.int32(targets[0][0]), jnp.int32(targets[0][1])
+    for m in range(1, len(targets)):
+        dz = jnp.where(n == m, targets[m][0], dz)
+        dy = jnp.where(n == m, targets[m][1], dy)
+    return (place[0] + dz) % 4 * 2 + (place[1] + dy) % 2, 0, 0
+
+
+def term_kernel(chunks, sizes, adds, shared, place, *refs):
     step = pl.program_id(0)
+    if shared:
+        total, their_gradient, refs = refs[0][0], refs[1], refs[2:]
+    else:
+        gradient, mine, their_gradient, refs = *refs[:3], refs[3:]
+        total = jnp.dot(gradient[...], mine[0], preferred_element_type=jnp.float32)
     their_parts, outputs = refs[:chunks], refs[chunks + adds:]
-    total = jnp.dot(gradient[...], mine[0], preferred_element_type=jnp.float32)
     theirs, start = None, 0
     for part in their_parts:
         rows = part.shape[1]
@@ -360,33 +400,37 @@
         low += size
 
 
-def weight_terms(place, targets, sizes, gradient, mine, their_gradient, their_parts, arrived=()):
+def weight_terms(
+    place, targets, sizes, gradient, mine, their_gradient, their_parts, arrived=(), shared=None
+):
     count = len(targets)
     width, rows = gradient.shape
     half = mine.shape[2]
 
-    def block_of(n, place):
-        dz, dy = jnp.int32(targets[0][0]), jnp.int32(targets[0][1])
-        for m in range(1, count):
-            dz = jnp.where(n == m, targets[m][0], dz)
-            dy = jnp.where(n == m, targets[m][1], dy)
-        return (place[0] + dz) % 4 * 2 + (place[1] + dy) % 2, 0, 0
-
     def result_of(low, size):
         return pl.BlockSpec(
             (1, width, half), lambda n, place: (jnp.clip(n - low, 0, size - 1), 0, 0)
         )
 
     whole = pl.BlockSpec((width, rows), lambda n, place: (0, 0))
+    place_of = functools.partial(block_of, targets)
+    if shared is None:
+        operands = [gradient, mine]
+        in_specs = [whole, pl.BlockSpec((1, rows, half), place_of)]
+    else:
+        operands = [shared]
+        in_specs = [pl.BlockSpec((1, width, half), lambda n, place: (n, 0, 0))]
     return pl.pallas_call(
-        functools.partial(term_kernel, len(their_parts), sizes, len(arrived)),
+        functools.partial(
+            term_kernel, len(their_parts), sizes, len(arrived), shared is not None
+        ),
         name="terms",
         out_shape=[jax.ShapeDtypeStruct((size, width, half), jnp.bfloat16) for size in sizes],
         grid_spec=pltpu.PrefetchScalarGridSpec(
             num_scalar_prefetch=1,
             grid=(count,),
-            in_specs=[whole, pl.BlockSpec((1, rows, half), block_of), whole]
-            + [pl.BlockSpec((1, part.shape[1], half), block_of) for part in their_parts]
+            in_specs=[*in_specs, whole]
+            + [pl.BlockSpec((1, part.shape[1], half), place_of) for part in their_parts]
             + [pl.BlockSpec((1, width, half), lambda n, place: (0, 0, 0))] * len(arrived),
             out_specs=[
                 result_of(sum(sizes[:n]), size) for n, size in enumerate(sizes)
@@ -394,7 +438,7 @@
         ),
         compiler_params=pltpu.CompilerParams(vmem_limit_bytes=VMEM_LIMIT // 2),
         cost_estimate=SMALL,
-    )(place, gradient, mine, their_gradient, *their_parts, *arrived)
+    )(place, *operands, their_gradient, *their_parts, *arrived)
 
 
 def total_kernel(*refs):
@@ -525,13 +569,15 @@
 
     chances, gradient = weigh(queries, cotangent, key_parts)
     their_gradient = ring(gradient, "core", 1, 2)
-    def terms(targets, sizes, arrived=(), after=()):
+    def terms(targets, sizes, arrived=(), after=(), shared=None):
         return weight_terms(
             tie(place, *after), targets, sizes, gradient, mine, their_gradient, their_parts,
-            arrived,
-        )
-
-    ahead, behind = terms(((1, 0), (1, 1), (3, 0), (3, 1)), (2, 2))
+            arrived, shared,
+        )
+
+    planes_of = (1, 0), (1, 1), (3, 0), (3, 1)
+    shared = own_terms(place, planes_of, gradient, mine)
+    ahead, behind = terms(planes_of, (2, 2), shared=shared)
     corner, = terms(((2, 1),), (1,), (), (behind,))
     beside, here = terms(((0, 1), (0, 0)), (1, 1), (), (corner,))
     far, = terms(((2, 0),), (1,), (ring(corner, "ylo", 1, 2),), (here,))

time: 291 us -> 286 us (0.983)
  waiting for transfers between devices: 155 us -> 148 us
    ppermute x17, waiting for transfers between devices: 59.9 us -> 54.2 us  [ring(): lax.ppermute(values, axis, [(i, (i + shift) % size) for i in range(size)])]
    pallas_call x0 -> x1, Pallas kernels: none -> 3.46 us  [own_terms(): pl.pallas_call(own_kernel, name='own', out_shape=jax.ShapeDtypeStruct((co...]
    unnamed x28 -> x32, local copies, waits for them, and re-layouts: 5.5 us -> 6.29 us
  transfers between devices with their start and end apart: 30 -> 30, of which waited for: 18 -> 18; matrix products, arithmetic and copies ran while one was open for 1% -> 1% of each run, Pallas kernels for 18% -> 19%
where the time goes in v5:
time: 286 us; the launch traced here: 285 us
  waiting for transfers between devices  148 us (52%)
  Pallas kernels  67.9 us (24%)
  starting transfers between devices  60.5 us (21%)
  local copies, waits for them, and re-layouts  7.15 us (2%)
    ppermute x17, waiting for transfers between devices, ring(): lax.ppermute(values, axis, [(i, (i + shift) % size) for i in range(size)])  54.2 us
    all_to_all x1, waiting for transfers between devices, per_device(): arrived = lax.all_to_all(packets, ('z', 'ylo'), 0, 0, tiled=True)  43.4 us
    ppermute x11, waiting for transfers between devices, along(): lax.ppermute(values, ('core', 'x'), [(c * 4 + i, c * 4 + (i + steps[c]) %...  34.7 us
    ppermute x17, starting transfers between devices, ring(): lax.ppermute(values, axis, [(i, (i + shift) % size) for i in range(size)])  32.3 us
    pallas_call x4, Pallas kernels, project(): pl.pallas_call(functools.partial(project_kernel, hops, first, begun is No...  30.9 us
    ppermute x11, starting transfers between devices, along(): lax.ppermute(values, ('core', 'x'), [(c * 4 + i, c * 4 + (i + steps[c]) %...  18.6 us
    pallas_call x5, Pallas kernels, copies_call(): pl.pallas_call(kernel, name=name, out_shape=jax.ShapeDtypeStruct(shape, j...  17.9 us
    all_to_all x1, waiting for transfers between devices, send_planes(): return lax.all_to_all(tie(packets, *after), 'z', 0, 0, tiled=True)  16.2 us
  transfers between devices with their start and end apart: 30, of which 18 were waited for; matrix products, arithmetic and copies ran while one was open for 1% of the time, Pallas kernels for 19%

profile of v5, /device:TPU:6, one launch (start us, length us, event | category | flops | bytes accessed | tf_op | source)
XLA Modules:
  0.0 285.4 jit_solution(12080842872517333925)
XLA Ops:
  8.4 3.6 %collective-permute-start.2 = (s32[2,32]{1,0:T(2,128)S(1)}, s32[2,32]{1,0:T(2,128)S(1)}, u32[]{:S(2)}, u32[]{:S(2)}) collective-permute-start(s32[2,32]{1,0:T(2,128)S(1)} %pad_add_fusion.both), channel_id=1, source_target_pairs={{0,64},{32,96},{64,0},{96,32},{1,65},{33,97},{65,1},{97,33},{2,66}... | collective-permute-start | bytes 776 | tf_op jit(solution)/shard_map/ppermute | solution.py:21
  16.1 4.7 %pack.1 = bf16[32,64,1024]{2,1,0:T(8,128)(2,1)} custom-call(s32[5]{0:T(128)} %stack.23.place, s32[2,32]{1,0:T(2,128)} %copy-done.8, s32[2,32]{1,0:T(2,128)} %copy-done.11, s32[2,32]{1,0:T(2,128)} %copy-done.10, s32[2,32]{1,0:T(2,128)} %copy-done.9, bf16[16,128,1024]{2,1,0:T(8,128)(2,1)} %own.8, bf16[16,128,1024]{2,1,0:T(8,128)(2,1)} %collective-permute-done.4.across), custom_call_target="tpu_custom_call" | custom-call | flops 1 | bytes 1 | tf_op jit(solution)/shard_map/pack/pallas_call | solution.py:114
  20.8 4.6 %all-to-all-start = ((bf16[32,64,1024]{2,1,0:T(8,128)(2,1)}), bf16[32,64,1024]{2,1,0:T(8,128)(2,1)}, u32[]{:S(2)}, u32[]{:S(2)}) async-start(bf16[32,64,1024]{2,1,0:T(8,128)(2,1)} %pack.1), calls=%async_computation | async-start | bytes 8388608 | tf_op jit(solution)/shard_map/all_to_all | solution.py:530
  25.3 4.4 %planes.1 = bf16[32,64,1024]{2,1,0:T(8,128)(2,1)} custom-call(s32[5]{0:T(128)} %stack.23.place, s32[2,32]{1,0:T(2,128)} %copy-done.11, s32[2,32]{1,0:T(2,128)} %copy-done.10, s32[2,32]{1,0:T(2,128)} %copy-done.9, bf16[16,128,1024]{2,1,0:T(8,128)(2,1)} %own.8, bf16[16,128,1024]{2,1,0:T(8,128)(2,1)} %collective-permute-done.4.across), custom_call_target="tpu_custom_call" | custom-call | flops 1 | bytes 1 | tf_op jit(solution)/shard_map/planes/pallas_call | solution.py:114
  29.8 43.4 %all-to-all-done.packets = bf16[32,64,1024]{2,1,0:T(8,128)(2,1)} async-done(((bf16[32,64,1024]{2,1,0:T(8,128)(2,1)}), bf16[32,64,1024]{2,1,0:T(8,128)(2,1)}, u32[]{:S(2)}, u32[]{:S(2)}) %all-to-all-start) | async-done | bytes 4194336 | tf_op jit(solution)/shard_map/all_to_all | solution.py:530
  76.2 5.0 %all-to-all-start.1 = ((bf16[32,64,1024]{2,1,0:T(8,128)(2,1)}), bf16[32,64,1024]{2,1,0:T(8,128)(2,1)}, u32[]{:S(2)}, u32[]{:S(2)}) async-start(bf16[32,64,1024]{2,1,0:T(8,128)(2,1)} %planes.1), calls=%async_computation.1 | async-start | bytes 8388608 | tf_op jit(solution)/shard_map/all_to_all | solution.py:524
  84.5 3.2 %collective-permute-start.5 = (bf16[512,1024]{1,0:T(8,128)(2,1)S(1)}, bf16[512,1024]{1,0:T(8,128)(2,1)}, u32[]{:S(2)}, u32[]{:S(2)}) collective-permute-start(bf16[512,1024]{1,0:T(8,128)(2,1)S(1)} %bitcast.16), channel_id=1, source_target_pairs={{0,1},{1,0},{2,3},{3,2},{4,5},{5,4},{6,7},{7,6},{8,9},{9,8},{10,11... | collective-permute-start | bytes 3145736 | tf_op jit(solution)/shard_map/ppermute | solution.py:21
  87.7 17.0 %collective-permute-done.7.refs_2_ = bf16[512,1024]{1,0:T(8,128)(2,1)S(1)} collective-permute-done((bf16[512,1024]{1,0:T(8,128)(2,1)S(1)}, bf16[512,1024]{1,0:T(8,128)(2,1)S(1)}, u32[]{:S(2)}, u32[]{:S(2)}) %collective-permute-start.7) | collective-permute-done | bytes 1048608 | tf_op jit(solution)/shard_map/ppermute | solution.py:508
  111.2 16.2 %all-to-all-done.1.packets = bf16[32,64,1024]{2,1,0:T(8,128)(2,1)} async-done(((bf16[32,64,1024]{2,1,0:T(8,128)(2,1)}), bf16[32,64,1024]{2,1,0:T(8,128)(2,1)}, u32[]{:S(2)}, u32[]{:S(2)}) %all-to-all-start.1) | async-done | bytes 4194336 | tf_op jit(solution)/shard_map/all_to_all | solution.py:524
  132.2 3.4 %collective-permute-done.9.refs_5_ = bf16[512,1024]{1,0:T(8,128)(2,1)} collective-permute-done((bf16[512,1024]{1,0:T(8,128)(2,1)}, bf16[512,1024]{1,0:T(8,128)(2,1)}, u32[]{:S(2)}, u32[]{:S(2)}) %collective-permute-start.9) | collective-permute-done | bytes 1048608 | tf_op jit(solution)/shard_map/ppermute | solution.py:508
  135.6 3.3 %collective-permute-done.8.refs_4_ = bf16[512,1024]{1,0:T(8,128)(2,1)} collective-permute-done((bf16[512,1024]{1,0:T(8,128)(2,1)}, bf16[512,1024]{1,0:T(8,128)(2,1)}, u32[]{:S(2)}, u32[]{:S(2)}) %collective-permute-start.8) | collective-permute-done | bytes 1048608 | tf_op jit(solution)/shard_map/ppermute | solution.py:508
  140.0 11.7 %collective-permute-done.11.refs_0_ = bf16[8,64,1024]{2,1,0:T(8,128)(2,1)} collective-permute-done((bf16[8,64,1024]{2,1,0:T(8,128)(2,1)}, bf16[8,64,1024]{2,1,0:T(8,128)(2,1)}, u32[]{:S(2)}, u32[]{:S(2)}) %collective-permute-start.11) | collective-permute-done | bytes 1048608 | tf_op jit(solution)/shard_map/ppermute | solution.py:21
  151.6 3.1 %merge.3 = bf16[8,64,1024]{2,1,0:T(8,128)(2,1)} custom-call(s32[5]{0:T(128)} %stack.23.place, s32[2,32]{1,0:T(2,128)} %copy-done.8, bf16[16,128,1024]{2,1,0:T(8,128)(2,1)} %own.8, bf16[16,128,1024]{2,1,0:T(8,128)(2,1)} %collective-permute-done.4.across, bf16[32,64,1024]{2,1,0:T(8,128)(2,1)} %all-to-all-done.1.packets, ...), custom_call_target="tpu_custom_call" | custom-call | flops 1 | bytes 1 | tf_op jit(solution)/shard_map/merge/pallas_call | solution.py:114
  156.8 3.3 %collective-permute-start.13 = (bf16[512,1024]{1,0:T(8,128)(2,1)}, bf16[512,1024]{1,0:T(8,128)(2,1)S(1)}, u32[]{:S(2)}, u32[]{:S(2)}) collective-permute-start(bf16[512,1024]{1,0:T(8,128)(2,1)} %bitcast.12), channel_id=1, source_target_pairs={{0,1},{1,0},{2,3},{3,2},{4,5},{5,4},{6,7},{7,6},{8,9},{9,8},{10,11... | collective-permute-start | bytes 3145736 | tf_op jit(solution)/shard_map/ppermute | solution.py:21
  160.1 13.2 %project.4 = (bf16[512,512]{1,0:T(8,128)(2,1)S(1)}, bf16[8,1024,512]{2,1,0:T(8,128)(2,1)}, bf16[8,512,512]{2,1,0:T(8,128)(2,1)}, bf16[512,512]{1,0:T(8,128)(2,1)S(1)}) custom-call(s32[5]{0:T(128)S(1)} %copy-done.7, bf16[512,1024]{1,0:T(8,128)(2,1)S(1)} %bitcast.17, bf16[512,1024]{1,0:T(8,128)(2,1)} %collective-permute-done.6.refs_1_, ...), custom_call_target="tpu_custom_call" | custom-call | flops 1 | bytes 1 | tf_op jit(solution)/shard_map/project/pallas_call | solution.py:203
  175.8 3.6 %collective-permute-start.16 = (bf16[512,1024]{1,0:T(8,128)(2,1)S(1)}, bf16[512,1024]{1,0:T(8,128)(2,1)S(1)}, u32[]{:S(2)}, u32[]{:S(2)}) collective-permute-start(bf16[512,1024]{1,0:T(8,128)(2,1)S(1)} %collective-permute-done.14.refs_1_), channel_id=1, source_target_pairs={{0,2},{2,4},{4,6},{6,0},{8,14},{10,8},{12,10},{14,12},{1,3},{3,5},... | collective-permute-start | bytes 3145736 | tf_op jit(solution)/shard_map/ppermute | solution.py:508
  179.5 8.0 %project.5 = (f32[512,512]{1,0:T(8,128)S(1)}, bf16[8,1024,512]{2,1,0:T(8,128)(2,1)}, bf16[8,512,512]{2,1,0:T(8,128)(2,1)}, f32[512,512]{1,0:T(8,128)S(1)}) custom-call(s32[5]{0:T(128)S(1)} %copy-done.7, bf16[512,1024]{1,0:T(8,128)(2,1)S(1)} %bitcast.13, bf16[512,1024]{1,0:T(8,128)(2,1)S(1)} %collective-permute-done.14.refs_1_, ...), custom_call_target="tpu_custom_call", output_to_operand_aliasing={{1}: (7, {})} | custom-call | flops 1 | bytes 1 | tf_op jit(solution)/shard_map/project/pallas_call | solution.py:203
  187.5 4.2 %collective-permute-done.16.refs_0_ = bf16[512,1024]{1,0:T(8,128)(2,1)S(1)} collective-permute-done((bf16[512,1024]{1,0:T(8,128)(2,1)S(1)}, bf16[512,1024]{1,0:T(8,128)(2,1)S(1)}, u32[]{:S(2)}, u32[]{:S(2)}) %collective-permute-start.16) | collective-permute-done | bytes 1048608 | tf_op jit(solution)/shard_map/ppermute | solution.py:508
  191.7 4.2 %collective-permute-start.19 = (bf16[512,1024]{1,0:T(8,128)(2,1)S(1)}, bf16[512,1024]{1,0:T(8,128)(2,1)S(1)}, u32[]{:S(2)}, u32[]{:S(2)}) collective-permute-start(bf16[512,1024]{1,0:T(8,128)(2,1)S(1)} %collective-permute-done.16.refs_0_), channel_id=1, source_target_pairs={{0,1},{1,0},{2,3},{3,2},{4,5},{5,4},{6,7},{7,6},{8,9},{9,8},{10,11... | collective-permute-start | bytes 3145736 | tf_op jit(solution)/shard_map/ppermute | solution.py:21
  195.9 3.7 %collective-permute-start.17 = (bf16[512,1024]{1,0:T(8,128)(2,1)S(1)}, bf16[512,1024]{1,0:T(8,128)(2,1)S(1)}, u32[]{:S(2)}, u32[]{:S(2)}) collective-permute-start(bf16[512,1024]{1,0:T(8,128)(2,1)S(1)} %collective-permute-done.13.refs_3_), channel_id=1, source_target_pairs={{0,2},{2,4},{4,6},{6,0},{8,14},{10,8},{12,10},{14,12},{1,3},{3,5},... | collective-permute-start | bytes 3145736 | tf_op jit(solution)/shard_map/ppermute | solution.py:508
  199.5 3.8 %project.6 = (f32[512,512]{1,0:T(8,128)S(1)}, bf16[8,1024,512]{2,1,0:T(8,128)(2,1)}, bf16[8,512,512]{2,1,0:T(8,128)(2,1)}, f32[512,512]{1,0:T(8,128)S(1)}) custom-call(s32[5]{0:T(128)S(1)} %copy-done.7, bf16[512,1024]{1,0:T(8,128)(2,1)S(1)} %collective-permute-done.16.refs_0_, ...), custom_call_target="tpu_custom_call", output_to_operand_aliasing={{1}: (6, {}), {2}: (7, {})} | custom-call | flops 1 | bytes 1 | tf_op jit(solution)/shard_map/project/pallas_call | solution.py:203
  203.3 12.0 %collective-permute-done.19.refs_2_ = bf16[512,1024]{1,0:T(8,128)(2,1)S(1)} collective-permute-done((bf16[512,1024]{1,0:T(8,128)(2,1)S(1)}, bf16[512,1024]{1,0:T(8,128)(2,1)S(1)}, u32[]{:S(2)}, u32[]{:S(2)}) %collective-permute-start.19) | collective-permute-done | bytes 1048608 | tf_op jit(solution)/shard_map/ppermute | solution.py:21
  215.3 4.3 %collective-permute-done.18.refs_1_ = bf16[512,1024]{1,0:T(8,128)(2,1)S(1)} collective-permute-done((bf16[512,1024]{1,0:T(8,128)(2,1)S(1)}, bf16[512,1024]{1,0:T(8,128)(2,1)S(1)}, u32[]{:S(2)}, u32[]{:S(2)}) %collective-permute-start.18) | collective-permute-done | bytes 1048608 | tf_op jit(solution)/shard_map/ppermute | solution.py:508
  219.6 5.9 %project.7 = (bf16[512,512]{1,0:T(8,128)(2,1)S(1)}, bf16[8,1024,512]{2,1,0:T(8,128)(2,1)}, bf16[8,512,512]{2,1,0:T(8,128)(2,1)}, bf16[512,512]{1,0:T(8,128)(2,1)S(1)}) custom-call(s32[5]{0:T(128)S(1)} %copy-done.7, bf16[512,1024]{1,0:T(8,128)(2,1)S(1)} %collective-permute-done.17.refs_0_, ...), custom_call_target="tpu_custom_call", output_to_operand_aliasing={{1}: (8, {}), {2}: (9, {})} | custom-call | flops 1 | bytes 1 | tf_op jit(solution)/shard_map/project/pallas_call | solution.py:203
  229.0 3.4 %copy-done = bf16[8,1024,512]{2,1,0:T(8,128)(2,1)S(1)} copy-done((bf16[8,1024,512]{2,1,0:T(8,128)(2,1)S(1)}, bf16[8,1024,512]{2,1,0:T(8,128)(2,1)}, u32[]{:S(2)}) %copy-start) | copy-done | bytes 8388632
  232.4 3.5 %own.9.refs_0_ = bf16[4,512,512]{2,1,0:T(8,128)(2,1)S(1)} custom-call(s32[5]{0:T(128)S(1)} %copy-done.7, bf16[512,1024]{1,0:T(8,128)(2,1)S(1)} %get-tuple-element.70.gradient.refs_0_, bf16[8,1024,512]{2,1,0:T(8,128)(2,1)S(1)} %copy-done), custom_call_target="tpu_custom_call" | custom-call | flops 1 | bytes 1 | tf_op jit(solution)/shard_map/own/pallas_call | solution.py:347
  235.9 3.7 %terms.4 = (bf16[2,512,512]{2,1,0:T(8,128)(2,1)S(1)}, bf16[2,512,512]{2,1,0:T(8,128)(2,1)S(1)}) custom-call(s32[5]{0:T(128)S(1)} %copy-done.7, bf16[4,512,512]{2,1,0:T(8,128)(2,1)S(1)} %own.9.refs_0_, bf16[512,1024]{1,0:T(8,128)(2,1)S(1)} %collective-permute-done.20.refs_1_.refs_2_, bf16[8,512,512]{2,1,0:T(8,128)(2,1)S(1)} %collective-permute-done.21.refs_2_.refs_3_, ...), custom_call_target="tpu_custom_call" | custom-call | flops 1 | bytes 1 | tf_op jit(solution)/shard_map/terms/pallas_call | solution.py:423
  247.2 3.2 %terms.6 = (bf16[1,512,512]{2,1,0:T(8,128)(2,1)S(1)}, bf16[1,512,512]{2,1,0:T(8,128)(2,1)S(1)}) custom-call(s32[5]{0:T(128)S(1)} %copy-done.7, bf16[512,1024]{1,0:T(8,128)(2,1)S(1)} %get-tuple-element.70.gradient.refs_0_, bf16[8,1024,512]{2,1,0:T(8,128)(2,1)S(1)} %bitcast.9, bf16[512,1024]{1,0:T(8,128)(2,1)S(1)} %collective-permute-done.20.refs_1_.refs_2_, ...), custom_call_target="tpu_custom_call" | custom-call | flops 1 | bytes 1 | tf_op jit(solution)/shard_map/terms/pallas_call | solution.py:423
  250.4 8.6 %collective-permute-done.25.refs_5_ = bf16[1,512,512]{2,1,0:T(8,128)(2,1)S(1)} collective-permute-done((bf16[1,512,512]{2,1,0:T(8,128)(2,1)S(1)}, bf16[1,512,512]{2,1,0:T(8,128)(2,1)S(1)}, u32[]{:S(2)}, u32[]{:S(2)}) %collective-permute-start.25) | collective-permute-done | bytes 524320 | tf_op jit(solution)/shard_map/ppermute | solution.py:21
  260.9 5.6 %collective-permute-done.23.refs_0_ = bf16[2,512,512]{2,1,0:T(8,128)(2,1)S(1)} collective-permute-done((bf16[2,512,512]{2,1,0:T(8,128)(2,1)S(1)}, bf16[2,512,512]{2,1,0:T(8,128)(2,1)S(1)}, u32[]{:S(2)}, u32[]{:S(2)}) %collective-permute-start.23) | collective-permute-done | bytes 1048608 | tf_op jit(solution)/shard_map/ppermute | solution.py:21
  266.7 3.5 %collective-permute-start.27 = (bf16[1,512,512]{2,1,0:T(8,128)(2,1)S(1)}, bf16[1,512,512]{2,1,0:T(8,128)(2,1)S(1)}, u32[]{:S(2)}, u32[]{:S(2)}) collective-permute-start(bf16[1,512,512]{2,1,0:T(8,128)(2,1)S(1)} %add_convert_fusion), channel_id=1, source_target_pairs={{0,16},{16,0},{1,17},{17,1},{2,18},{18,2},{3,19},{19,3},{4,20},{20... | collective-permute-start | bytes 1572872 | tf_op jit(solution)/shard_map/ppermute | solution.py:21
  273.5 7.6 %collective-permute-done.27.refs_4_ = bf16[1,512,512]{2,1,0:T(8,128)(2,1)S(1)} collective-permute-done((bf16[1,512,512]{2,1,0:T(8,128)(2,1)S(1)}, bf16[1,512,512]{2,1,0:T(8,128)(2,1)S(1)}, u32[]{:S(2)}, u32[]{:S(2)}) %collective-permute-start.27) | collective-permute-done | bytes 524320 | tf_op jit(solution)/shard_map/ppermute | solution.py:21
  (88 shorter events, 55.9 us)
Async XLA Ops:
  0.6 14.9 %collective-permute-start.4 = (bf16[16,128,1024]{2,1,0:T(8,128)(2,1)}, bf16[16,128,1024]{2,1,0:T(8,128)(2,1)}, u32[]{:S(2)}, u32[]{:S(2)}) collective-permute-start(bf16[16,128,1024]{2,1,0:T(8,128)(2,1)} %own.8), channel_id=1, source_target_pairs={{0,8},{8,0},{1,9},{9,1},{2,10},{10,2},{3,11},{11,3},{4,12},{12,4},... | collective-permute-start | bytes 12582920 | tf_op jit(solution)/shard_map/ppermute | solution.py:21
  2.8 3.6 %collective-permute-start = (s32[1,32]{1,0:T(1,128)S(1)}, s32[1,32]{1,0:T(1,128)S(1)}, u32[]{:S(2)}, u32[]{:S(2)}) collective-permute-start(s32[1,32]{1,0:T(1,128)S(1)} %pad_add_fusion.1.wanted), channel_id=1, source_target_pairs={{0,16},{16,0},{1,17},{17,1},{2,18},{18,2},{3,19},{19,3},{4,20},{20... | collective-permute-start | bytes 392 | tf_op jit(solution)/shard_map/ppermute | solution.py:21
  6.5 7.1 %collective-permute-start.3 = (s32[2,32]{1,0:T(2,128)S(1)}, s32[2,32]{1,0:T(2,128)S(1)}, u32[]{:S(2)}, u32[]{:S(2)}) collective-permute-start(s32[2,32]{1,0:T(2,128)S(1)} %pad_add_fusion.both), channel_id=1, source_target_pairs={{0,32},{32,64},{64,96},{96,0},{1,33},{33,65},{65,97},{97,1},{2,34}... | collective-permute-start | bytes 776 | tf_op jit(solution)/shard_map/ppermute | solution.py:21
  8.4 5.2 %collective-permute-start.2 = (s32[2,32]{1,0:T(2,128)S(1)}, s32[2,32]{1,0:T(2,128)S(1)}, u32[]{:S(2)}, u32[]{:S(2)}) collective-permute-start(s32[2,32]{1,0:T(2,128)S(1)} %pad_add_fusion.both), channel_id=1, source_target_pairs={{0,64},{32,96},{64,0},{96,32},{1,65},{33,97},{65,1},{97,33},{2,66}... | collective-permute-start | bytes 776 | tf_op jit(solution)/shard_map/ppermute | solution.py:21
  12.0 3.6 %collective-permute-start.1 = (s32[2,32]{1,0:T(2,128)S(1)}, s32[2,32]{1,0:T(2,128)S(1)}, u32[]{:S(2)}, u32[]{:S(2)}) collective-permute-start(s32[2,32]{1,0:T(2,128)S(1)} %pad_add_fusion.both), channel_id=1, source_target_pairs={{0,96},{32,0},{64,32},{96,64},{1,97},{33,1},{65,33},{97,65},{2,98}... | collective-permute-start | bytes 776 | tf_op jit(solution)/shard_map/ppermute | solution.py:21
  20.8 52.4 %all-to-all-start = ((bf16[32,64,1024]{2,1,0:T(8,128)(2,1)}), bf16[32,64,1024]{2,1,0:T(8,128)(2,1)}, u32[]{:S(2)}, u32[]{:S(2)}) async-start(bf16[32,64,1024]{2,1,0:T(8,128)(2,1)} %pack.1), calls=%async_computation | async-start | bytes 8388608 | tf_op jit(solution)/shard_map/all_to_all | solution.py:530
  76.2 51.2 %all-to-all-start.1 = ((bf16[32,64,1024]{2,1,0:T(8,128)(2,1)}), bf16[32,64,1024]{2,1,0:T(8,128)(2,1)}, u32[]{:S(2)}, u32[]{:S(2)}) async-start(bf16[32,64,1024]{2,1,0:T(8,128)(2,1)} %planes.1), calls=%async_computation.1 | async-start | bytes 8388608 | tf_op jit(solution)/shard_map/all_to_all | solution.py:524
  81.2 23.5 %collective-permute-start.7 = (bf16[512,1024]{1,0:T(8,128)(2,1)S(1)}, bf16[512,1024]{1,0:T(8,128)(2,1)S(1)}, u32[]{:S(2)}, u32[]{:S(2)}) collective-permute-start(bf16[512,1024]{1,0:T(8,128)(2,1)S(1)} %bitcast.14), channel_id=1, source_target_pairs={{0,6},{2,0},{4,2},{6,4},{8,10},{10,12},{12,14},{14,8},{1,7},{3,1},... | collective-permute-start | bytes 3145736 | tf_op jit(solution)/shard_map/ppermute | solution.py:508
  82.1 22.6 %collective-permute-start.6 = (bf16[512,1024]{1,0:T(8,128)(2,1)S(1)}, bf16[512,1024]{1,0:T(8,128)(2,1)}, u32[]{:S(2)}, u32[]{:S(2)}) collective-permute-start(bf16[512,1024]{1,0:T(8,128)(2,1)S(1)} %bitcast.15), channel_id=1, source_target_pairs={{0,2},{2,4},{4,6},{6,0},{8,14},{10,8},{12,10},{14,12},{1,3},{3,5},... | collective-permute-start | bytes 3145736 | tf_op jit(solution)/shard_map/ppermute | solution.py:508
  84.5 21.8 %collective-permute-start.5 = (bf16[512,1024]{1,0:T(8,128)(2,1)S(1)}, bf16[512,1024]{1,0:T(8,128)(2,1)}, u32[]{:S(2)}, u32[]{:S(2)}) collective-permute-start(bf16[512,1024]{1,0:T(8,128)(2,1)S(1)} %bitcast.16), channel_id=1, source_target_pairs={{0,1},{1,0},{2,3},{3,2},{4,5},{5,4},{6,7},{7,6},{8,9},{9,8},{10,11... | collective-permute-start | bytes 3145736 | tf_op jit(solution)/shard_map/ppermute | solution.py:21
  106.3 25.9 %collective-permute-start.10 = (bf16[512,1024]{1,0:T(8,128)(2,1)}, bf16[512,1024]{1,0:T(8,128)(2,1)}, u32[]{:S(2)}, u32[]{:S(2)}) collective-permute-start(bf16[512,1024]{1,0:T(8,128)(2,1)} %collective-permute-done.6.refs_1_), channel_id=1, source_target_pairs={{0,2},{2,4},{4,6},{6,0},{8,14},{10,8},{12,10},{14,12},{1,3},{3,5},... | collective-permute-start | bytes 3145736 | tf_op jit(solution)/shard_map/ppermute | solution.py:508
  108.0 27.6 %collective-permute-start.9 = (bf16[512,1024]{1,0:T(8,128)(2,1)}, bf16[512,1024]{1,0:T(8,128)(2,1)}, u32[]{:S(2)}, u32[]{:S(2)}) collective-permute-start(bf16[512,1024]{1,0:T(8,128)(2,1)} %collective-permute-done.5.refs_3_), channel_id=1, source_target_pairs={{0,6},{2,0},{4,2},{6,4},{8,10},{10,12},{12,14},{14,8},{1,7},{3,1},... | collective-permute-start | bytes 3145736 | tf_op jit(solution)/shard_map/ppermute | solution.py:508
  108.3 30.6 %collective-permute-start.8 = (bf16[512,1024]{1,0:T(8,128)(2,1)}, bf16[512,1024]{1,0:T(8,128)(2,1)}, u32[]{:S(2)}, u32[]{:S(2)}) collective-permute-start(bf16[512,1024]{1,0:T(8,128)(2,1)} %collective-permute-done.5.refs_3_), channel_id=1, source_target_pairs={{0,2},{2,4},{4,6},{6,0},{8,14},{10,8},{12,10},{14,12},{1,3},{3,5},... | collective-permute-start | bytes 3145736 | tf_op jit(solution)/shard_map/ppermute | solution.py:508
  130.1 30.0 %copy-start.7 = (s32[5]{0:T(128)S(1)}, s32[5]{0:T(128)}, u32[]{:S(2)}) copy-start(s32[5]{0:T(128)} %stack.23.place) | copy-start | bytes 64
  130.1 21.5 %collective-permute-start.11 = (bf16[8,64,1024]{2,1,0:T(8,128)(2,1)}, bf16[8,64,1024]{2,1,0:T(8,128)(2,1)}, u32[]{:S(2)}, u32[]{:S(2)}) collective-permute-start(bf16[8,64,1024]{2,1,0:T(8,128)(2,1)} %hand.1), channel_id=1, source_target_pairs={{0,16},{16,0},{1,17},{17,1},{2,18},{18,2},{3,19},{19,3},{4,20},{20... | collective-permute-start | bytes 3145736 | tf_op jit(solution)/shard_map/ppermute | solution.py:21
  138.9 21.1 %collective-permute-start.12 = (bf16[512,1024]{1,0:T(8,128)(2,1)}, bf16[512,1024]{1,0:T(8,128)(2,1)}, u32[]{:S(2)}, u32[]{:S(2)}) collective-permute-start(bf16[512,1024]{1,0:T(8,128)(2,1)} %collective-permute-done.9.refs_5_), channel_id=1, source_target_pairs={{0,6},{2,0},{4,2},{6,4},{8,10},{10,12},{12,14},{14,8},{1,7},{3,1},... | collective-permute-start | bytes 3145736 | tf_op jit(solution)/shard_map/ppermute | solution.py:508
  154.7 24.8 %copy-start.1 = (bf16[8,64,1024]{2,1,0:T(8,128)(2,1)S(1)}, bf16[8,64,1024]{2,1,0:T(8,128)(2,1)}, u32[]{:S(2)}) copy-start(bf16[8,64,1024]{2,1,0:T(8,128)(2,1)} %merge.3) | copy-start | bytes 3145732
  154.7 21.0 %collective-permute-start.14 = (bf16[512,1024]{1,0:T(8,128)(2,1)}, bf16[512,1024]{1,0:T(8,128)(2,1)S(1)}, u32[]{:S(2)}, u32[]{:S(2)}) collective-permute-start(bf16[512,1024]{1,0:T(8,128)(2,1)} %bitcast.10), channel_id=1, source_target_pairs={{0,2},{2,4},{4,6},{6,0},{8,14},{10,8},{12,10},{14,12},{1,3},{3,5},... | collective-permute-start | bytes 3145736 | tf_op jit(solution)/shard_map/ppermute | solution.py:508
  155.3 24.1 %collective-permute-start.15 = (bf16[512,1024]{1,0:T(8,128)(2,1)}, bf16[512,1024]{1,0:T(8,128)(2,1)S(1)}, u32[]{:S(2)}, u32[]{:S(2)}) collective-permute-start(bf16[512,1024]{1,0:T(8,128)(2,1)} %bitcast.11), channel_id=1, source_target_pairs={{0,6},{2,0},{4,2},{6,4},{8,10},{10,12},{12,14},{14,8},{1,7},{3,1},... | collective-permute-start | bytes 3145736 | tf_op jit(solution)/shard_map/ppermute | solution.py:508
  156.8 22.6 %collective-permute-start.13 = (bf16[512,1024]{1,0:T(8,128)(2,1)}, bf16[512,1024]{1,0:T(8,128)(2,1)S(1)}, u32[]{:S(2)}, u32[]{:S(2)}) collective-permute-start(bf16[512,1024]{1,0:T(8,128)(2,1)} %bitcast.12), channel_id=1, source_target_pairs={{0,1},{1,0},{2,3},{3,2},{4,5},{5,4},{6,7},{7,6},{8,9},{9,8},{10,11... | collective-permute-start | bytes 3145736 | tf_op jit(solution)/shard_map/ppermute | solution.py:21
  175.8 15.9 %collective-permute-start.16 = (bf16[512,1024]{1,0:T(8,128)(2,1)S(1)}, bf16[512,1024]{1,0:T(8,128)(2,1)S(1)}, u32[]{:S(2)}, u32[]{:S(2)}) collective-permute-start(bf16[512,1024]{1,0:T(8,128)(2,1)S(1)} %collective-permute-done.14.refs_1_), channel_id=1, source_target_pairs={{0,2},{2,4},{4,6},{6,0},{8,14},{10,8},{12,10},{14,12},{1,3},{3,5},... | collective-permute-start | bytes 3145736 | tf_op jit(solution)/shard_map/ppermute | solution.py:508
  191.7 23.7 %collective-permute-start.19 = (bf16[512,1024]{1,0:T(8,128)(2,1)S(1)}, bf16[512,1024]{1,0:T(8,128)(2,1)S(1)}, u32[]{:S(2)}, u32[]{:S(2)}) collective-permute-start(bf16[512,1024]{1,0:T(8,128)(2,1)S(1)} %collective-permute-done.16.refs_0_), channel_id=1, source_target_pairs={{0,1},{1,0},{2,3},{3,2},{4,5},{5,4},{6,7},{7,6},{8,9},{9,8},{10,11... | collective-permute-start | bytes 3145736 | tf_op jit(solution)/shard_map/ppermute | solution.py:21
  195.8 23.8 %collective-permute-start.18 = (bf16[512,1024]{1,0:T(8,128)(2,1)S(1)}, bf16[512,1024]{1,0:T(8,128)(2,1)S(1)}, u32[]{:S(2)}, u32[]{:S(2)}) collective-permute-start(bf16[512,1024]{1,0:T(8,128)(2,1)S(1)} %collective-permute-done.13.refs_3_), channel_id=1, source_target_pairs={{0,6},{2,0},{4,2},{6,4},{8,10},{10,12},{12,14},{14,8},{1,7},{3,1},... | collective-permute-start | bytes 3145736 | tf_op jit(solution)/shard_map/ppermute | solution.py:508
  195.9 23.8 %collective-permute-start.17 = (bf16[512,1024]{1,0:T(8,128)(2,1)S(1)}, bf16[512,1024]{1,0:T(8,128)(2,1)S(1)}, u32[]{:S(2)}, u32[]{:S(2)}) collective-permute-start(bf16[512,1024]{1,0:T(8,128)(2,1)S(1)} %collective-permute-done.13.refs_3_), channel_id=1, source_target_pairs={{0,2},{2,4},{4,6},{6,0},{8,14},{10,8},{12,10},{14,12},{1,3},{3,5},... | collective-permute-start | bytes 3145736 | tf_op jit(solution)/shard_map/ppermute | solution.py:508
  199.5 36.3 %collective-permute-start.21 = (bf16[8,512,512]{2,1,0:T(8,128)(2,1)}, bf16[8,512,512]{2,1,0:T(8,128)(2,1)S(1)}, u32[]{:S(2)}, u32[]{:S(2)}) collective-permute-start(bf16[8,512,512]{2,1,0:T(8,128)(2,1)} %get-tuple-element.72), channel_id=1, source_target_pairs={{0,8},{8,0},{1,9},{9,1},{2,10},{10,2},{3,11},{11,3},{4,12},{12,4},... | collective-permute-start | bytes 12582920 | tf_op jit(solution)/shard_map/ppermute | solution.py:21
  226.4 9.5 %collective-permute-start.22 = (bf16[8,512,512]{2,1,0:T(8,128)(2,1)}, bf16[8,512,512]{2,1,0:T(8,128)(2,1)S(1)}, u32[]{:S(2)}, u32[]{:S(2)}) collective-permute-start(bf16[8,512,512]{2,1,0:T(8,128)(2,1)} %get-tuple-element.73), channel_id=1, source_target_pairs={{0,8},{8,0},{1,9},{9,1},{2,10},{10,2},{3,11},{11,3},{4,12},{12,4},... | collective-permute-start | bytes 12582920 | tf_op jit(solution)/shard_map/ppermute | solution.py:21
  228.4 7.5 %collective-permute-start.20 = (bf16[512,1024]{1,0:T(8,128)(2,1)S(1)}, bf16[512,1024]{1,0:T(8,128)(2,1)S(1)}, u32[]{:S(2)}, u32[]{:S(2)}) collective-permute-start(bf16[512,1024]{1,0:T(8,128)(2,1)S(1)} %get-tuple-element.70.gradient.refs_0_), channel_id=1, source_target_pairs={{0,8},{8,0},{1,9},{9,1},{2,10},{10,2},{3,11},{11,3},{4,12},{12,4},... | collective-permute-start | bytes 3145736 | tf_op jit(solution)/shard_map/ppermute | solution.py:21
  239.6 26.9 %collective-permute-start.23 = (bf16[2,512,512]{2,1,0:T(8,128)(2,1)S(1)}, bf16[2,512,512]{2,1,0:T(8,128)(2,1)S(1)}, u32[]{:S(2)}, u32[]{:S(2)}) collective-permute-start(bf16[2,512,512]{2,1,0:T(8,128)(2,1)S(1)} %get-tuple-element.74), channel_id=1, source_target_pairs={{0,32},{32,64},{64,96},{96,0},{1,33},{33,65},{65,97},{97,1},{2,34}... | collective-permute-start | bytes 3145736 | tf_op jit(solution)/shard_map/ppermute | solution.py:21
  241.0 25.5 %collective-permute-start.24 = (bf16[2,512,512]{2,1,0:T(8,128)(2,1)S(1)}, bf16[2,512,512]{2,1,0:T(8,128)(2,1)S(1)}, u32[]{:S(2)}, u32[]{:S(2)}) collective-permute-start(bf16[2,512,512]{2,1,0:T(8,128)(2,1)S(1)} %get-tuple-element.75), channel_id=1, source_target_pairs={{0,96},{32,0},{64,32},{96,64},{1,97},{33,1},{65,33},{97,65},{2,98}... | collective-permute-start | bytes 3145736 | tf_op jit(solution)/shard_map/ppermute | solution.py:21
  245.1 13.9 %collective-permute-start.25 = (bf16[1,512,512]{2,1,0:T(8,128)(2,1)S(1)}, bf16[1,512,512]{2,1,0:T(8,128)(2,1)S(1)}, u32[]{:S(2)}, u32[]{:S(2)}) collective-permute-start(bf16[1,512,512]{2,1,0:T(8,128)(2,1)S(1)} %terms.5), channel_id=1, source_target_pairs={{0,16},{16,0},{1,17},{17,1},{2,18},{18,2},{3,19},{19,3},{4,20},{20... | collective-permute-start | bytes 1572872 | tf_op jit(solution)/shard_map/ppermute | solution.py:21
  266.7 14.4 %collective-permute-start.27 = (bf16[1,512,512]{2,1,0:T(8,128)(2,1)S(1)}, bf16[1,512,512]{2,1,0:T(8,128)(2,1)S(1)}, u32[]{:S(2)}, u32[]{:S(2)}) collective-permute-start(bf16[1,512,512]{2,1,0:T(8,128)(2,1)S(1)} %add_convert_fusion), channel_id=1, source_target_pairs={{0,16},{16,0},{1,17},{17,1},{2,18},{18,2},{3,19},{19,3},{4,20},{20... | collective-permute-start | bytes 1572872 | tf_op jit(solution)/shard_map/ppermute | solution.py:21
  270.2 13.9 %collective-permute-start.26 = (bf16[1,512,512]{2,1,0:T(8,128)(2,1)S(1)}, bf16[1,512,512]{2,1,0:T(8,128)(2,1)S(1)}, u32[]{:S(2)}, u32[]{:S(2)}) collective-permute-start(bf16[1,512,512]{2,1,0:T(8,128)(2,1)S(1)} %terms.7), channel_id=1, source_target_pairs={{0,64},{32,96},{64,0},{96,32},{1,65},{33,97},{65,1},{97,33},{2,66}... | collective-permute-start | bytes 1572872 | tf_op jit(solution)/shard_map/ppermute | solution.py:21
  (13 other events, 93.9 us)
